TPU v7x, 32 devices: a whole 2x2x4 slice. The times are simulated.
32 devices in a mesh: groups: 2 (over x), track: 16 (over z, y, core).
Axes of the slice: x: 2, y: 2, z: 4, core: 2. Of those that a mesh axis runs over, the one named last changes fastest.
Arguments:
- volume: bfloat16 [96, 96, 8, 128], P(None, ('groups', 'track')), parts along dimension 1, may hold values from -400 to 400
- labels: int32 [96, 8, 128], P(('groups', 'track')), parts along dimension 0, may hold values from 0 to 3
- conv_taps: float32 [2, 3, 7, 96], replicated, may hold values from -2 to 2
- norm_gain: float32 [2, 96], replicated, may hold values from 0.1 to 1.9
- weight_in: bfloat16 [2, 384, 96], replicated, may hold values from -0.625 to 0.625
- bias_in: float32 [2, 384], replicated, may hold values from -3 to 3
- weight_out: bfloat16 [2, 96, 384], replicated, may hold values from -0.3125 to 0.3125
- layer_scale: float32 [2, 96], replicated, may hold values from 0.3 to 1
- head_weight: bfloat16 [4, 96], replicated, may hold values from -0.625 to 0.625
- head_bias: float32 [4], replicated, may hold values from -4 to 4
Outputs:
- input_grad: float32 [96, 96, 8, 128], P(None, ('groups', 'track')), parts along dimension 1
- grad_taps: float32 [4, 3, 7, 96], P('groups'), parts along dimension 0
- grad_gain: float32 [4, 96], P('groups'), parts along dimension 0
- grad_weight_in: float32 [4, 384, 96], P('groups'), parts along dimension 0
- grad_bias_in: float32 [4, 384], P('groups'), parts along dimension 0
- grad_weight_out: float32 [4, 96, 384], P('groups'), parts along dimension 0
- grad_scale: float32 [4, 96], P('groups'), parts along dimension 0
- grad_head_weight: float32 [8, 96], P('groups'), parts along dimension 0
- grad_head_bias: float32 [8], P('groups'), parts along dimension 0
There are 2 independent parts, one for each index of `groups`. A program takes and returns all parts, laid end to end along the dimension named above; an argument that names none is the same for every part. Nothing has to cross between parts.
All inputs are finite; a program needn't handle non-finite values.
Results may differ from a plain program's by a relative error of at most 0.0046.
Values may be sent and summed in bfloat16 or wider, within the bound.
No kernel may reach another device: no remote copies, remote signals or barrier semaphores. Data moves between devices by JAX's collectives and lax.ppermute only.
A program may use at most 192 MiB of HBM per device.

v0:
```python
import jax
import jax.numpy as jnp
from jax import lax
from jax.sharding import PartitionSpec as P


def padded(block, sides, width):
    for axis, dim in sides:
        count = lax.axis_size(axis)
        forward = [(i, i + 1) for i in range(count - 1)]
        backward = [(target, source) for source, target in forward]
        low = lax.ppermute(
            lax.slice_in_dim(block, block.shape[dim] - width, None, axis=dim), axis, forward
        )
        high = lax.ppermute(lax.slice_in_dim(block, 0, width, axis=dim), axis, backward)
        block = jnp.concatenate([low, block, high], axis=dim)
    return block


def shifted(value, axis, steps):
    count = lax.axis_size(axis)
    first, last = (max(0, -steps), min(count, count - steps))
    return lax.ppermute(value, axis, [(source, source + steps) for source in range(first, last)])


def sweep(field, coeffs, axis):
    radius = coeffs.shape[0] // 2
    channels = field.shape[0]
    shape = [channels, 1, 1, 1, 1]
    shape[axis + 1] = coeffs.shape[0]
    kernel = jnp.transpose(coeffs).reshape(shape)
    padding = [(0, 0), (0, 0), (0, 0)]
    if axis != 1:
        padding[axis - 1] = (radius, radius)
    result = lax.conv_general_dilated(
        field[None],
        kernel,
        (1, 1, 1),
        padding,
        dimension_numbers=("NCDHW", "OIDHW", "NCDHW"),
        feature_group_count=channels,
        precision=lax.Precision.HIGHEST,
    )
    return result[0]


def spread(extended, conv_taps, norm_gain):
    mixed = sweep(extended, conv_taps[0], 1)
    mixed = sweep(mixed, conv_taps[1], 2)
    mixed = sweep(mixed, conv_taps[2], 3)
    centred = mixed - jnp.mean(mixed, axis=0, keepdims=True)
    variance = jnp.mean(centred * centred, axis=0, keepdims=True)
    return centred * lax.rsqrt(variance + 1e-06) * norm_gain[:, None, None, None]


def expand(flattened, weight_in, bias_in):
    hidden = jnp.dot(weight_in, flattened, preferred_element_type=jnp.float32) + bias_in[:, None]
    return (hidden, jax.nn.gelu(hidden).astype(jnp.bfloat16))


def pointwise_back(flattened, hidden, activated, grad_out, weight_in, weight_out, layer_scale):
    lifted = jnp.dot(weight_out, activated, preferred_element_type=jnp.float32)
    grad_scale = jnp.sum(grad_out * lifted, axis=1)
    grad_lift = (grad_out * layer_scale[:, None]).astype(jnp.bfloat16)
    grad_weight_out = lax.dot_general(
        grad_lift, activated, (((1,), (1,)), ((), ())), preferred_element_type=jnp.float32
    )
    grad_act = lax.dot_general(
        weight_out, grad_lift, (((0,), (0,)), ((), ())), preferred_element_type=jnp.float32
    )
    unused, gelu_back = jax.vjp(jax.nn.gelu, hidden)
    grad_hidden = gelu_back(grad_act)[0]
    grad_bias = jnp.sum(grad_hidden, axis=1)
    grad_hid = grad_hidden.astype(jnp.bfloat16)
    grad_weight_in = lax.dot_general(
        grad_hid, flattened, (((1,), (1,)), ((), ())), preferred_element_type=jnp.float32
    )
    grad_normed = lax.dot_general(
        weight_in, grad_hid, (((0,), (0,)), ((), ())), preferred_element_type=jnp.float32
    )
    return (grad_normed, (grad_weight_in, grad_bias, grad_weight_out, grad_scale))


def head_back(final, labels, head_weight, head_bias):
    logits = jnp.dot(head_weight, final, preferred_element_type=jnp.float32) + head_bias[:, None]
    probability = jax.nn.softmax(logits, axis=0)
    classes = jnp.arange(head_weight.shape[0], dtype=jnp.int32)
    onehot = (labels[None, :] == classes[:, None]).astype(jnp.float32)
    grad_logits = probability - onehot
    grad_bias = jnp.sum(grad_logits, axis=1)
    grad_low = grad_logits.astype(jnp.bfloat16)
    grad_weight = lax.dot_general(
        grad_low, final, (((1,), (1,)), ((), ())), preferred_element_type=jnp.float32
    )
    grad_final = lax.dot_general(
        head_weight, grad_low, (((0,), (0,)), ((), ())), preferred_element_type=jnp.float32
    )
    return (grad_final, grad_weight, grad_bias)


def section_forward(extended, conv_taps, norm_gain, weight_in, bias_in, weight_out, layer_scale):
    radius = conv_taps.shape[1] // 2
    normed, pullback = jax.vjp(spread, extended, conv_taps, norm_gain)
    extent = normed.shape
    flattened = normed.reshape(extent[0], -1).astype(jnp.bfloat16)
    center = extended[:, radius : radius + extent[1]].reshape(extent[0], -1)
    hidden, activated = expand(flattened, weight_in, bias_in)
    lifted = center + layer_scale[:, None] * jnp.dot(
        weight_out, activated, preferred_element_type=jnp.float32
    )
    saved = None
    return (lifted.reshape(extent), saved)


def section_back(
    extended, grad_out, conv_taps, norm_gain, weight_in, bias_in, weight_out, layer_scale
):
    radius = conv_taps.shape[1] // 2
    normed, pullback = jax.vjp(spread, extended, conv_taps, norm_gain)
    flattened = normed.reshape(normed.shape[0], -1).astype(jnp.bfloat16)
    hidden, activated = expand(flattened, weight_in, bias_in)
    extent = grad_out.shape
    grad_normed, grads = pointwise_back(
        flattened,
        hidden,
        activated,
        grad_out.reshape(extent[0], -1),
        weight_in,
        weight_out,
        layer_scale,
    )
    grad_ext, grad_taps, grad_gain = pullback(grad_normed.reshape(extent))
    grad_ext = grad_ext.at[:, radius : radius + extent[1]].add(grad_out)
    return (grad_ext, (grad_taps, grad_gain) + grads)


def border(field, radius):
    return padded(field, (("track", 1),), radius)


def fold_rims(grad_ext, radius):
    planes = grad_ext.shape[1] - 2 * radius
    inner = grad_ext[:, radius : radius + planes]
    from_lower = shifted(grad_ext[:, radius + planes :].astype(jnp.bfloat16), "track", 1).astype(
        jnp.float32
    )
    from_upper = shifted(grad_ext[:, :radius].astype(jnp.bfloat16), "track", -1).astype(jnp.float32)
    inner = inner.at[:, :radius].add(from_lower)
    inner = inner.at[:, planes - radius :].add(from_upper)
    return inner


def on_device(
    volume,
    labels,
    conv_taps,
    norm_gain,
    weight_in,
    bias_in,
    weight_out,
    layer_scale,
    head_weight,
    head_bias,
):
    radius = conv_taps.shape[2] // 2
    planes = volume.shape[1]
    devices = lax.axis_size("track")
    first_ext = border(volume, radius).astype(jnp.float32)
    middle, first_saved = section_forward(
        first_ext,
        conv_taps[0],
        norm_gain[0],
        weight_in[0],
        bias_in[0],
        weight_out[0],
        layer_scale[0],
    )
    second_ext = border(middle.astype(jnp.bfloat16), radius).astype(jnp.float32)
    final, second_saved = section_forward(
        second_ext,
        conv_taps[1],
        norm_gain[1],
        weight_in[1],
        bias_in[1],
        weight_out[1],
        layer_scale[1],
    )
    final = final.astype(jnp.bfloat16)
    grad_final, grad_hw, grad_hb = head_back(
        final.reshape(final.shape[0], -1), labels.reshape(-1), head_weight, head_bias
    )
    grad_out = grad_final.reshape(final.shape)
    exts = (first_ext, second_ext)
    collected = [None, None]
    for section in (1, 0):
        grad_ext, grads = section_back(
            exts[section],
            grad_out,
            conv_taps[section],
            norm_gain[section],
            weight_in[section],
            bias_in[section],
            weight_out[section],
            layer_scale[section],
        )
        collected[section] = grads
        grad_out = fold_rims(grad_ext, radius)
    stacked = tuple((jnp.stack([collected[0][index], collected[1][index]]) for index in range(6)))
    summed = lax.psum(
        (stacked[0], stacked[1], stacked[2], stacked[3], stacked[4], stacked[5], grad_hw, grad_hb),
        "track",
    )
    stacked = summed[:6]
    head_w = summed[6]
    head_b = summed[7]
    total = float(devices * planes * volume.shape[2] * volume.shape[3])
    return (
        grad_out,
        stacked[0] / total,
        stacked[1] / total,
        stacked[2] / total,
        stacked[3] / total,
        stacked[4] / total,
        stacked[5] / total,
        head_w / total,
        head_b / total,
    )


def solution(mesh):
    placed = (
        P(None, ("groups", "track"), None, None),
        P(("groups", "track"), None, None),
        P(),
        P(),
        P(),
        P(),
        P(),
        P(),
        P(),
        P(),
    )
    return jax.shard_map(
        on_device,
        mesh=mesh,
        in_specs=placed,
        out_specs=(
            P(None, ("groups", "track"), None, None),
            P("groups", None, None, None),
            P("groups", None),
            P("groups", None, None),
            P("groups", None),
            P("groups", None, None),
            P("groups", None),
            P("groups", None),
            P("groups"),
        ),
        check_vma=False,
    )
```

profile of v0, /device:TPU:0, one launch (start us, length us, event | category | flops | bytes accessed | tf_op | source)
XLA Modules:
  0.0 647.6 jit_solution(6352100220278742689)
XLA Ops:
  23.3 104.8 %fusion.28 = f32[3,8,8,16,96]{4,2,3,1,0:T(8,128)S(1)} fusion(f32[96,1,7,1,1]{0,1,4,3,2:T(1,128)S(1)} %copy-done.92, bf16[96,9,8,8,16]{0,4,3,2,1:T(8,128)(2,1)S(1)} %bitcast.539), kind=kOutput, calls=%fused_computation.51 | convolution fusion | flops 24772608 | bytes 2951808 | tf_op jit(solution)/shard_map/jvp()/conv_general_dilated | solution.py:35
  128.1 15.0 %fusion.220 = f32[3,8,8,16,96]{4,2,3,1,0:T(8,128)S(1)} fusion(f32[3,8,8,16,96]{4,2,3,1,0:T(8,128)S(1)} %fusion.28, f32[96,1,1,7,1]{0,1,4,3,2:T(1,128)S(1)} %copy-done.79), kind=kOutput, calls=%fused_computation.347 | convolution fusion | flops 19464192 | bytes 2361984 | tf_op jit(solution)/shard_map/jvp()/conv_general_dilated | solution.py:35
  148.2 3.9 fusion.19
  155.8 8.2 %collective-permute-start.2 = (bf16[96,3,8,128]{3,2,1,0:T(8,128)(2,1)}, bf16[96,3,8,128]{3,2,1,0:T(8,128)(2,1)}, u32[]{:S(2)}, u32[]{:S(2)}) collective-permute-start(bf16[96,3,8,128]{3,2,1,0:T(8,128)(2,1)} %bitcast.197), channel_id=1, source_target_pairs={{0,1},{1,2},{2,3},{3,4},{4,5},{5,6},{6,7},{7,8},{8,9},{9,10},{10,1... | collective-permute-start | bytes 1769480 | tf_op jit(solution)/shard_map/ppermute | solution.py:12
  196.3 3.0 fusion.205
  199.4 105.1 %fusion.26 = f32[3,8,8,16,96]{4,2,3,1,0:T(8,128)S(1)} fusion(f32[96,1,7,1,1]{0,1,4,3,2:T(1,128)S(1)} %copy-done.90, bf16[96,9,8,8,16]{0,4,3,2,1:T(8,128)(2,1)S(1)} %bitcast.540), kind=kOutput, calls=%fused_computation.49 | convolution fusion | flops 24772608 | bytes 2951808 | tf_op jit(solution)/shard_map/jvp()/conv_general_dilated | solution.py:35
  304.5 15.0 %fusion.221 = f32[3,8,8,16,96]{4,2,3,1,0:T(8,128)S(1)} fusion(f32[3,8,8,16,96]{4,2,3,1,0:T(8,128)S(1)} %fusion.26, f32[96,1,1,7,1]{0,1,4,3,2:T(1,128)S(1)} %reshape.571), kind=kOutput, calls=%fused_computation.348 | convolution fusion | flops 19464192 | bytes 2361984 | tf_op jit(solution)/shard_map/jvp()/conv_general_dilated | solution.py:35
  329.2 4.4 fusion.218
  337.0 2.9 copy.170
  339.9 2.8 multiply_reduce_fusion.1
  342.7 2.9 copy.172
  345.6 2.8 multiply_reduce_fusion.5
  348.5 3.7 fusion.64
  371.3 4.9 collective-permute-start.4
  401.7 2.9 copy.126
  409.2 2.9 copy.144
  412.1 3.1 convolution_bitcast_fusion.4
  425.0 4.3 multiply_reduce_fusion.4
  430.3 6.1 fusion.219
  448.6 5.8 fusion.118
  464.3 62.5 %all-reduce.6 = (f32[2,3,7,96]{3,2,1,0:T(8,128)S(1)}, f32[2,96]{1,0:T(2,128)S(1)}, f32[2,384]{1,0:T(2,128)S(1)}, f32[2,96]{1,0:T(2,128)S(1)}, f32[4,96]{1,0:T(4,128)S(1)}, /*index=5*/f32[4]{0:T(128)}) all-reduce(f32[2,3,7,96]{3,2,1,0:T(8,128)S(1)} %pad_maximum_fusion.4, ...), channel_id=1, replica_groups=mesh['groups'=2,'track'=16] {'track'}, use_global_device_ids=true, to_apply=%region_10.0 | all-reduce | flops 5572 | bytes 44576 | tf_op jit(solution)/shard_map/psum | solution.py:209
  545.9 78.9 %all-reduce.10.cloned.1.call-done = (f32[2,384,96]{1,2,0:T(8,128)}, f32[2,96,384]{2,1,0:T(8,128)}) async-done(((f32[2,384,96]{1,2,0:T(8,128)}, f32[2,96,384]{2,1,0:T(8,128)}), (f32[2,384,96]{1,2,0:T(8,128)}, f32[2,96,384]{2,1,0:T(8,128)})) %all-reduce.10.cloned.1.call-update) | async-done | bytes 589840 | tf_op jit(solution)/shard_map/psum | solution.py:209
  633.4 4.2 fusion.76
  637.6 2.9 copy.168
  (399 shorter events, 178.8 us)
Async XLA Ops:
  7.2 320.5 %copy-start = (bf16[4,96]{1,0:T(4,128)(2,1)S(1)}, bf16[4,96]{1,0:T(4,128)(2,1)}, u32[]{:S(2)}) copy-start(bf16[4,96]{1,0:T(4,128)(2,1)} %param.38) | copy-start | bytes 2308
  7.2 9.8 %copy-start.46 = (bf16[96,3,8,128]{3,2,1,0:T(8,128)(2,1)S(1)}, bf16[96,3,8,128]{3,2,1,0:T(8,128)(2,1)}, u32[]{:S(2)}) copy-start(bf16[96,3,8,128]{3,2,1,0:T(8,128)(2,1)} %param.30) | copy-start | bytes 1769476
  7.2 617.6 %all-reduce.10.cloned.1.call-start = ((), (), s32[]{:S(2)}) async-start(), calls=%async_computation | async-start | bytes 1179648 | tf_op jit(solution)/shard_map/psum | solution.py:209
  7.2 13.1 %collective-permute-start = (bf16[96,3,8,128]{3,2,1,0:T(8,128)(2,1)}, bf16[96,3,8,128]{3,2,1,0:T(8,128)(2,1)S(1)}, u32[]{:S(2)}, u32[]{:S(2)}) collective-permute-start(bf16[96,3,8,128]{3,2,1,0:T(8,128)(2,1)} %param.30), channel_id=1, source_target_pairs={{0,1},{1,2},{2,3},{3,4},{4,5},{5,6},{6,7},{7,8},{8,9},{9,10},{10,1... | collective-permute-start | bytes 1769480 | tf_op jit(solution)/shard_map/ppermute | solution.py:12
  9.8 11.1 %collective-permute-start.1 = (bf16[96,3,8,128]{3,2,1,0:T(8,128)(2,1)}, bf16[96,3,8,128]{3,2,1,0:T(8,128)(2,1)S(1)}, u32[]{:S(2)}, u32[]{:S(2)}) collective-permute-start(bf16[96,3,8,128]{3,2,1,0:T(8,128)(2,1)} %param.30), channel_id=1, source_target_pairs={{1,0},{2,1},{3,2},{4,3},{5,4},{6,5},{7,6},{8,7},{9,8},{10,9},{11,1... | collective-permute-start | bytes 1769480 | tf_op jit(solution)/shard_map/ppermute | solution.py:15
  13.7 6.2 copy-start.102
  23.3 104.8 %copy-start.79 = (f32[96,1,1,7,1]{0,1,4,3,2:T(1,128)S(1)}, f32[96,1,1,7,1]{0,1,4,3,2:T(1,128)}, u32[]{:S(2)}) copy-start(f32[96,1,1,7,1]{0,1,4,3,2:T(1,128)} %reshape.567) | copy-start | bytes 8068
  128.1 15.0 %copy-start.2 = (f32[3,8,8,16,96]{4,2,3,1,0:T(8,128)}, f32[3,8,8,16,96]{4,2,3,1,0:T(8,128)S(1)}, u32[]{:S(2)}) copy-start(f32[3,8,8,16,96]{4,2,3,1,0:T(8,128)S(1)} %fusion.28) | copy-start | bytes 3538948
  128.1 15.0 %copy-start.91 = (f32[96,1,1,1,7]{0,1,4,3,2:T(1,128)S(1)}, f32[96,1,1,1,7]{0,1,4,3,2:T(1,128)}, u32[]{:S(2)}) copy-start(f32[96,1,1,1,7]{0,1,4,3,2:T(1,128)} %reshape.568) | copy-start | bytes 8068
  155.8 36.7 %collective-permute-start.2 = (bf16[96,3,8,128]{3,2,1,0:T(8,128)(2,1)}, bf16[96,3,8,128]{3,2,1,0:T(8,128)(2,1)}, u32[]{:S(2)}, u32[]{:S(2)}) collective-permute-start(bf16[96,3,8,128]{3,2,1,0:T(8,128)(2,1)} %bitcast.197), channel_id=1, source_target_pairs={{0,1},{1,2},{2,3},{3,4},{4,5},{5,6},{6,7},{7,8},{8,9},{9,10},{10,1... | collective-permute-start | bytes 1769480 | tf_op jit(solution)/shard_map/ppermute | solution.py:12
  163.9 30.1 %collective-permute-start.3 = (bf16[96,3,8,128]{3,2,1,0:T(8,128)(2,1)}, bf16[96,3,8,128]{3,2,1,0:T(8,128)(2,1)}, u32[]{:S(2)}, u32[]{:S(2)}) collective-permute-start(bf16[96,3,8,128]{3,2,1,0:T(8,128)(2,1)} %bitcast.197), channel_id=1, source_target_pairs={{1,0},{2,1},{3,2},{4,3},{5,4},{6,5},{7,6},{8,7},{9,8},{10,9},{11,1... | collective-permute-start | bytes 1769480 | tf_op jit(solution)/shard_map/ppermute | solution.py:15
  304.4 15.0 %copy-start.89 = (f32[96,1,1,1,7]{0,1,4,3,2:T(1,128)S(1)}, f32[96,1,1,1,7]{0,1,4,3,2:T(1,128)}, u32[]{:S(2)}) copy-start(f32[96,1,1,1,7]{0,1,4,3,2:T(1,128)} %reshape.572) | copy-start | bytes 8068
  321.8 23.9 %copy-start.69 = (f32[3072]{0:T(1024)}, f32[3072]{0:T(1024)S(1)}, u32[]{:S(2)}) copy-start(f32[3072]{0:T(1024)S(1)} %get-tuple-element.199) | copy-start | bytes 36868
  371.3 45.2 %collective-permute-start.4 = (bf16[96,3,8,128]{3,2,1,0:T(8,128)(2,1)}, bf16[96,3,8,128]{3,2,1,0:T(8,128)(2,1)}, u32[]{:S(2)}, u32[]{:S(2)}) collective-permute-start(bf16[96,3,8,128]{3,2,1,0:T(8,128)(2,1)} %copy.128), channel_id=1, source_target_pairs={{0,1},{1,2},{2,3},{3,4},{4,5},{5,6},{6,7},{7,8},{8,9},{9,10},{10,1... | collective-permute-start | bytes 1769480 | tf_op jit(solution)/shard_map/ppermute | solution.py:23
  378.7 41.0 %collective-permute-start.5 = (bf16[96,3,8,128]{3,2,1,0:T(8,128)(2,1)}, bf16[96,3,8,128]{3,2,1,0:T(8,128)(2,1)}, u32[]{:S(2)}, u32[]{:S(2)}) collective-permute-start(bf16[96,3,8,128]{3,2,1,0:T(8,128)(2,1)} %copy.131), channel_id=1, source_target_pairs={{1,0},{2,1},{3,2},{4,3},{5,4},{6,5},{7,6},{8,7},{9,8},{10,9},{11,1... | collective-permute-start | bytes 1769480 | tf_op jit(solution)/shard_map/ppermute | solution.py:23
  430.3 7.5 %copy-start.65 = (bf16[2,384,96]{1,2,0:T(8,128)(2,1)S(1)}, bf16[2,384,96]{1,2,0:T(8,128)(2,1)}, u32[]{:S(2)}) copy-start(bf16[2,384,96]{1,2,0:T(8,128)(2,1)} %param.34) | copy-start | bytes 442372
  462.3 66.8 %copy-start.77 = (f32[1,96,7,1,1]{1,2,4,3,0:T(8,128)S(1)}, f32[1,96,7,1,1]{1,2,4,3,0:T(8,128)}, u32[]{:S(2)}) copy-start(f32[1,96,7,1,1]{1,2,4,3,0:T(8,128)} %get-tuple-element.236) | copy-start | bytes 8068
  535.6 6.8 %copy-start.104 = (f32[4]{0:T(128)S(1)}, f32[4]{0:T(128)}, u32[]{:S(2)}) copy-start(f32[4]{0:T(128)} %get-tuple-element.151) | copy-start | bytes 52
  537.6 90.8 %collective-permute-start.6 = (bf16[96,3,8,128]{3,2,1,0:T(8,128)(2,1)}, bf16[96,3,8,128]{3,2,1,0:T(8,128)(2,1)}, u32[]{:S(2)}, u32[]{:S(2)}) collective-permute-start(bf16[96,3,8,128]{3,2,1,0:T(8,128)(2,1)} %copy.146), channel_id=1, source_target_pairs={{0,1},{1,2},{2,3},{3,4},{4,5},{5,6},{6,7},{7,8},{8,9},{9,10},{10,1... | collective-permute-start | bytes 1769480 | tf_op jit(solution)/shard_map/ppermute | solution.py:23
  541.1 89.8 %collective-permute-start.7 = (bf16[96,3,8,128]{3,2,1,0:T(8,128)(2,1)}, bf16[96,3,8,128]{3,2,1,0:T(8,128)(2,1)}, u32[]{:S(2)}, u32[]{:S(2)}) collective-permute-start(bf16[96,3,8,128]{3,2,1,0:T(8,128)(2,1)} %copy.148), channel_id=1, source_target_pairs={{1,0},{2,1},{3,2},{4,3},{5,4},{6,5},{7,6},{8,7},{9,8},{10,9},{11,1... | collective-permute-start | bytes 1769480 | tf_op jit(solution)/shard_map/ppermute | solution.py:23
  626.5 6.9 %copy-start.24 = (f32[3,8,8,17,96]{4,1,3,2,0:T(8,128)S(1)}, f32[3,8,8,17,96]{4,1,3,2,0:T(8,128)}, u32[]{:S(2)}) copy-start(f32[3,8,8,17,96]{4,1,3,2,0:T(8,128)} %copy-done.23) | copy-start | bytes 3760132
  626.5 6.9 %copy-start.38 = (bf16[96,3,8,128]{0,2,3,1:T(8,128)(2,1)S(1)}, bf16[96,3,8,128]{0,2,3,1:T(8,128)(2,1)}, u32[]{:S(2)}) copy-start(bf16[96,3,8,128]{0,2,3,1:T(8,128)(2,1)} %copy-done.37) | copy-start | bytes 1769476
  626.5 6.9 %copy-start.39 = (bf16[96,3,8,128]{0,2,3,1:T(8,128)(2,1)S(1)}, bf16[96,3,8,128]{0,2,3,1:T(8,128)(2,1)}, u32[]{:S(2)}) copy-start(bf16[96,3,8,128]{0,2,3,1:T(8,128)(2,1)} %copy.132) | copy-start | bytes 1769476
  633.4 7.1 %copy-start.1 = (bf16[4,96]{1,0:T(4,128)(2,1)S(1)}, bf16[4,96]{1,0:T(4,128)(2,1)}, u32[]{:S(2)}) copy-start(bf16[4,96]{1,0:T(4,128)(2,1)} %param.38) | copy-start | bytes 2308
  (92 other events, 192.6 us)
Sparse Core Ops, SparseCore 0:
  535.7 89.0 all-reduce.9
where the time goes:
time: 655 us; the launch traced here: 648 us
  matrix products  295 us (45%)
  local copies, waits for them, and re-layouts  115 us (18%)
  waiting for transfers between devices  79 us (12%)
  blocking collectives  62.5 us (10%)
  other arithmetic  56.6 us (9%)
  starting transfers between devices  23.8 us (4%)
  between operations  15.9 us (2%)
    conv_general_dilated x18, matrix products, sweep(): lax.conv_general_dilated(field[None], kernel, (1, 1, 1), padding, dimensi...  264 us
    psum x1, waiting for transfers between devices, on_device(): lax.psum((stacked[0], stacked[1], stacked[2], stacked[3], stacked[4], sta...  78.9 us
    psum x1, blocking collectives, on_device(): lax.psum((stacked[0], stacked[1], stacked[2], stacked[3], stacked[4], sta...  62.5 us
    unnamed x227, local copies, waits for them, and re-layouts  39.6 us
    conv_general_dilated x32, local copies, waits for them, and re-layouts, sweep(): lax.conv_general_dilated(field[None], kernel, (1, 1, 1), padding, dimensi...  16.6 us
  transfers between devices with their start and end apart: 9, of which 1 were waited for; matrix products, arithmetic and copies ran while one was open for 12% of the time, Pallas kernels for 0%

commit v1 on v0

v1 whole, which is shorter than its diff:
```python
import functools

import jax
import jax.numpy as jnp
from jax import lax
from jax.experimental import pallas as pl
from jax.experimental.pallas import tpu as pltpu
from jax.sharding import PartitionSpec as P

F32 = jnp.float32
BF16 = jnp.bfloat16
LANES = 128
ROWS = 8
RADIUS = 3
TAPS = 7
PLANES = 3
Y = 8
OWN = PLANES * Y
EXT = (PLANES + 2 * RADIUS) * Y
CHUNK = 4
GELU_A = 0.7978845608028654
GELU_B = 0.044715 * GELU_A
VMEM_LIMIT = 44 * 1024 * 1024


def group_rows(index):
    return pl.ds(pl.multiple_of(index * ROWS, ROWS), ROWS)


def tap_tables(taps):
    lane = jnp.arange(LANES)
    reach = jnp.arange(TAPS) - RADIUS
    inside = (lane[None] + reach[:, None] >= 0) & (lane[None] + reach[:, None] < LANES)
    inside = inside.astype(F32)[:, None, :]
    wide = jnp.broadcast_to(taps[:, :, :, None], taps.shape + (LANES,))
    return jnp.concatenate([wide[0], wide[1], wide[2] * inside, wide[2] * inside[::-1]], axis=0)


def unpack(source, wide, ext, first):
    wide[...] = source[...].astype(F32)
    channels = ext.shape[1]

    def one(group, carry):
        rows = group_rows(group)
        for tile in range(OWN):
            ext[first + tile, rows, :] = wide[pl.ds(group * ROWS * OWN + tile, ROWS, stride=OWN), :]
        return carry

    lax.fori_loop(0, channels // ROWS, one, 0)


def widen(source, ext, first, count):
    def one(tile, carry):
        ext[first + tile] = source[tile].astype(F32)
        return carry

    lax.fori_loop(0, count, one, 0, unroll=4)


def weighted(terms):
    total = None
    for coeff, value in terms:
        product = coeff * value
        total = product if total is None else total + product
    return total


def forward_x(ext, taps, rows):
    tx = [taps[k, rows, :] for k in range(TAPS)]
    out = [[None] * Y for _ in range(PLANES)]
    for y in range(Y):
        column = [ext[j * Y + y, rows, :] for j in range(PLANES + 2 * RADIUS)]
        for p in range(PLANES):
            out[p][y] = weighted([(tx[k], column[p + k]) for k in range(TAPS)])
    return out


def forward_y(field, taps, rows):
    ty = [taps[TAPS + k, rows, :] for k in range(TAPS)]
    out = [[None] * Y for _ in range(PLANES)]
    for p in range(PLANES):
        for y in range(Y):
            out[p][y] = weighted(
                [(ty[k], field[p][y + k - RADIUS]) for k in range(TAPS) if 0 <= y + k - RADIUS < Y]
            )
    return out


def turned(value, shift):
    return value if shift % LANES == 0 else pltpu.roll(value, shift % LANES, 1)


def convolve(ext, taps, mixed):
    def one(group, carry):
        rows = group_rows(group)
        field = forward_y(forward_x(ext, taps, rows), taps, rows)
        tz = [taps[2 * TAPS + k, rows, :] for k in range(TAPS)]
        for p in range(PLANES):
            for y in range(Y):
                mixed[p * Y + y, rows, :] = weighted(
                    [(tz[k], turned(field[p][y], RADIUS - k)) for k in range(TAPS)]
                )
        return carry

    lax.fori_loop(0, mixed.shape[1] // ROWS, one, 0)


def convolve_back(dmixed, taps, gext):
    def one(group, carry):
        rows = group_rows(group)
        tx = [taps[k, rows, :] for k in range(TAPS)]
        ty = [taps[TAPS + k, rows, :] for k in range(TAPS)]
        tz = [taps[3 * TAPS + k, rows, :] for k in range(TAPS)]
        along = [[None] * Y for _ in range(PLANES)]
        for p in range(PLANES):
            cross = []
            for y in range(Y):
                value = dmixed[p * Y + y, rows, :]
                cross.append(weighted([(tz[k], turned(value, k - RADIUS)) for k in range(TAPS)]))
            for y in range(Y):
                along[p][y] = weighted(
                    [(ty[k], cross[y - k + RADIUS]) for k in range(TAPS) if 0 <= y - k + RADIUS < Y]
                )
        for y in range(Y):
            for j in range(PLANES + 2 * RADIUS):
                gext[j * Y + y, rows, :] = weighted(
                    [(tx[k], along[j - k][y]) for k in range(TAPS) if 0 <= j - k < PLANES]
                )
        return carry

    lax.fori_loop(0, dmixed.shape[1] // ROWS, one, 0)


def tap_sums(ext, dmixed, taps, out):
    lane = lax.broadcasted_iota(jnp.int32, (ROWS, LANES), 1)

    def one(group, carry):
        rows = group_rows(group)
        mx = forward_x(ext, taps, rows)
        mxy = forward_y(mx, taps, rows)
        ty = [taps[TAPS + k, rows, :] for k in range(TAPS)]
        tz = [taps[3 * TAPS + k, rows, :] for k in range(TAPS)]
        sum_x, sum_y, sum_z = ([None] * TAPS for _ in range(3))

        def add(sums, k, value):
            sums[k] = value if sums[k] is None else sums[k] + value

        for p in range(PLANES):
            cross = []
            for y in range(Y):
                value = dmixed[p * Y + y, rows, :]
                spun = [turned(value, k - RADIUS) for k in range(TAPS)]
                for k in range(TAPS):
                    add(sum_z, k, spun[k] * mxy[p][y])
                cross.append(weighted([(tz[k], spun[k]) for k in range(TAPS)]))
            for y in range(Y):
                for k in range(TAPS):
                    if 0 <= y + k - RADIUS < Y:
                        add(sum_y, k, cross[y] * mx[p][y + k - RADIUS])
            for y in range(Y):
                along = weighted(
                    [(ty[k], cross[y - k + RADIUS]) for k in range(TAPS) if 0 <= y - k + RADIUS < Y]
                )
                for k in range(TAPS):
                    add(sum_x, k, along * ext[(p + k) * Y + y, rows, :])
        for k in range(TAPS):
            reach = k - RADIUS
            kept = (lane - reach >= 0) & (lane - reach < LANES)
            sum_z[k] = jnp.where(kept, sum_z[k], 0.0)
        total = jnp.zeros((ROWS, LANES), F32)
        for index, value in enumerate(sum_x + sum_y + sum_z):
            total = jnp.where(lane == index, jnp.sum(value, axis=1, keepdims=True), total)
        out[rows, :] = total
        return carry

    lax.fori_loop(0, dmixed.shape[1] // ROWS, one, 0)


def tiles(ref, first):
    return jnp.concatenate([ref[first + i] for i in range(CHUNK)], axis=1)


def put(ref, first, value):
    for i in range(CHUNK):
        ref[first + i] = value[:, i * LANES : (i + 1) * LANES].astype(ref.dtype)


def folded(value):
    total = value[:, :LANES]
    for i in range(1, CHUNK):
        total = total + value[:, i * LANES : (i + 1) * LANES]
    return total


def normalise(mixed):
    scale = 1.0 / mixed.shape[0]
    centred = mixed - jnp.sum(mixed, axis=0, keepdims=True) * scale
    variance = jnp.sum(centred * centred, axis=0, keepdims=True) * scale
    inverse = lax.rsqrt(variance + 1e-06)
    return centred * inverse, inverse


def dot(a, b):
    return jnp.dot(a, b, preferred_element_type=F32)


def dot_t(a, b):
    return lax.dot_general(a, b, (((1,), (1,)), ((), ())), preferred_element_type=F32)


def forward_kernel(
    par, vol, ha, hb, taps, gain, w_in, b_in, w_out, scale, out, wide, ext, mixed
):
    unpack(vol, wide, ext, RADIUS * Y)
    unpack(ha, wide, ext, (1 - par[0]) * 2 * RADIUS * Y)
    unpack(hb, wide, ext, par[0] * 2 * RADIUS * Y)
    convolve(ext, taps, mixed)

    def one(step, carry):
        first = step * CHUNK
        normal, inverse = normalise(tiles(mixed, first))
        normed = (normal * gain[...]).astype(BF16)
        hidden = dot(w_in[...], normed) + b_in[...]
        half = jnp.tanh(hidden * (GELU_A + GELU_B * (hidden * hidden)))
        act = (0.5 * hidden * (1.0 + half)).astype(BF16)
        put(out, first, tiles(ext, RADIUS * Y + first) + scale[...] * dot(w_out[...], act))
        return carry

    lax.fori_loop(0, OWN // CHUNK, one, 0)


def again_kernel(par, vol, ha, hb, taps, mixed, ext_low, wide, ext):
    unpack(vol, wide, ext, RADIUS * Y)
    unpack(ha, wide, ext, (1 - par[0]) * 2 * RADIUS * Y)
    unpack(hb, wide, ext, par[0] * 2 * RADIUS * Y)
    convolve(ext, taps, mixed)

    def one(tile, carry):
        ext_low[tile] = ext[tile].astype(BF16)
        return carry

    lax.fori_loop(0, EXT, one, 0, unroll=4)


def section_back(
    make_grad, par, mixed, taps, gain, w_in, w_in_t, b_in, w_out, w_out_t, scale,
    rim_a, rim_b, inner, dmixed, sums, small, gext, acc_bias, acc_gain, acc_scale,
):
    channels = gain.shape[0]
    acc_bias[...] = jnp.zeros_like(acc_bias)
    acc_gain[...] = jnp.zeros_like(acc_gain)
    acc_scale[...] = jnp.zeros_like(acc_scale)
    sums[...] = jnp.zeros_like(sums)

    def one(step, carry):
        first = step * CHUNK
        normal, inverse = normalise(tiles(mixed, first))
        normed = (normal * gain[...]).astype(BF16)
        hidden = dot(w_in[...], normed) + b_in[...]
        square = hidden * hidden
        half = jnp.tanh(hidden * (GELU_A + GELU_B * square))
        rise = 0.5 + 0.5 * half
        act = (hidden * rise).astype(BF16)
        slope = rise + (hidden * (0.5 - 0.5 * (half * half))) * (GELU_A + 3.0 * GELU_B * square)
        lifted = dot(w_out[...], act)
        grad = make_grad(step, first, lifted)
        acc_scale[...] += folded(grad * lifted)
        put(inner, first, grad)
        g_lift = (grad * scale[...]).astype(BF16)
        sums[:channels, :] += dot_t(g_lift, act)
        g_hidden = dot(w_out_t[...], g_lift) * slope
        acc_bias[...] += folded(g_hidden)
        g_hid = g_hidden.astype(BF16)
        sums[channels : 2 * channels, :] += dot_t(normed, g_hid)
        g_norm = dot(w_in_t[...], g_hid)
        acc_gain[...] += folded(g_norm * normal)
        g_normal = g_norm * gain[...]
        share = 1.0 / channels
        mean_a = jnp.sum(g_normal, axis=0, keepdims=True) * share
        mean_b = jnp.sum(g_normal * normal, axis=0, keepdims=True) * share
        put(dmixed, first, inverse * (g_normal - mean_a - normal * mean_b))
        return carry

    lax.fori_loop(0, OWN // CHUNK, one, 0)
    sums[2 * channels : 2 * channels + 1, :] = jnp.sum(acc_bias[...].T, axis=0, keepdims=True)
    lane = lax.broadcasted_iota(jnp.int32, (channels, LANES), 1)
    small[...] = jnp.where(
        lane == 3 * TAPS,
        jnp.sum(acc_gain[...], axis=1, keepdims=True),
        jnp.where(lane == 3 * TAPS + 1, jnp.sum(acc_scale[...], axis=1, keepdims=True), 0.0),
    )
    convolve_back(dmixed, taps, gext)
    first_a = (1 - par[0]) * 2 * RADIUS * Y
    first_b = par[0] * 2 * RADIUS * Y

    def finish(tile, carry):
        rim_a[tile] = gext[first_a + tile].astype(BF16)
        rim_b[tile] = gext[first_b + tile].astype(BF16)
        inner[tile] += gext[RADIUS * Y + tile]
        return carry

    lax.fori_loop(0, OWN, finish, 0, unroll=2)


def turn_kernel(
    par, mid, ma, mb, labels, taps, gain, w_in, w_in_t, b_in, w_out, w_out_t, scale,
    head, head_t, head_b,
    rim_a, rim_b, inner, dmixed, sums, small, head_sum, head_bias,
    ext, mixed, gext, acc_bias, acc_gain, acc_scale,
):
    widen(mid, ext, RADIUS * Y, OWN)
    widen(ma, ext, (1 - par[0]) * 2 * RADIUS * Y, OWN)
    widen(mb, ext, par[0] * 2 * RADIUS * Y, OWN)
    convolve(ext, taps, mixed)
    head_sum[...] = jnp.zeros_like(head_sum)
    head_bias[...] = jnp.zeros_like(head_bias)

    def make_grad(step, first, lifted):
        final = (tiles(ext, RADIUS * Y + first) + scale[...] * lifted).astype(BF16)
        logits = dot(head[...], final) + head_b[...]
        raised = jnp.exp(logits - jnp.max(logits, axis=0, keepdims=True))
        probability = raised / jnp.sum(raised, axis=0, keepdims=True)
        classes = lax.broadcasted_iota(jnp.int32, logits.shape, 0)
        g_logits = probability - (labels[step] == classes).astype(F32)
        head_bias[...] += folded(g_logits)
        g_low = g_logits.astype(BF16)
        head_sum[...] += dot_t(g_low, final)
        return dot(head_t[...], g_low)

    section_back(
        make_grad, par, mixed, taps, gain, w_in, w_in_t, b_in, w_out, w_out_t, scale,
        rim_a, rim_b, inner, dmixed, sums, small, gext, acc_bias, acc_gain, acc_scale,
    )


def back_kernel(
    par, before, ra, rb, mixed, taps, gain, w_in, w_in_t, b_in, w_out, w_out_t, scale,
    rim_a, rim_b, inner, dmixed, sums, small,
    gext, acc_bias, acc_gain, acc_scale,
):
    def make_grad(step, first, lifted):
        return tiles(before, first) + tiles(ra, first).astype(F32) + tiles(rb, first).astype(F32)

    section_back(
        make_grad, par, mixed, taps, gain, w_in, w_in_t, b_in, w_out, w_out_t, scale,
        rim_a, rim_b, inner, dmixed, sums, small, gext, acc_bias, acc_gain, acc_scale,
    )


def taps_two_kernel(par, mid, ma, mb, dmixed, taps, out, ext):
    widen(mid, ext, RADIUS * Y, OWN)
    widen(ma, ext, (1 - par[0]) * 2 * RADIUS * Y, OWN)
    widen(mb, ext, par[0] * 2 * RADIUS * Y, OWN)
    tap_sums(ext, dmixed, taps, out)


def taps_one_kernel(ext_low, dmixed, taps, out, ext):
    widen(ext_low, ext, 0, EXT)
    tap_sums(ext, dmixed, taps, out)


def last_kernel(before, ra, rb, out, total):
    def add(tile, carry):
        total[tile] = before[tile] + ra[tile].astype(F32) + rb[tile].astype(F32)
        return carry

    lax.fori_loop(0, OWN, add, 0, unroll=2)
    channels = before.shape[1]

    def one(group, carry):
        rows = group_rows(group)
        for tile in range(OWN):
            out[pl.ds(group * ROWS * OWN + tile, ROWS, stride=OWN), :] = total[tile, rows, :]
        return carry

    lax.fori_loop(0, channels // ROWS, one, 0)


def call(kernel, name, operands, outs, scratch, flops=0):
    smem = pl.BlockSpec(memory_space=pltpu.SMEM)
    vmem = pl.BlockSpec(memory_space=pltpu.VMEM)
    moved = sum(x.size * x.dtype.itemsize for x in operands) + sum(
        x.size * x.dtype.itemsize for x in outs
    )
    return pl.pallas_call(
        kernel,
        name=name,
        out_shape=tuple(outs),
        in_specs=[smem if x.dtype == jnp.int32 and x.shape == (1,) else vmem for x in operands],
        out_specs=tuple([vmem] * len(outs)),
        scratch_shapes=scratch,
        compiler_params=pltpu.CompilerParams(vmem_limit_bytes=VMEM_LIMIT),
        cost_estimate=pl.CostEstimate(flops=flops, bytes_accessed=moved, transcendentals=0),
    )(*operands)


def shape(dims, dtype):
    return jax.ShapeDtypeStruct(dims, dtype)


def swap(value_a, value_b):
    count = lax.axis_size("track")
    near = [(i, i ^ 1) for i in range(count)]
    far = []
    for i in range(1, count - 1, 2):
        far += [(i, i + 1), (i + 1, i)]
    return lax.ppermute(value_b, "track", far), lax.ppermute(value_a, "track", near)


def summed(value):
    count = lax.axis_size("track")
    if count & (count - 1):
        return lax.psum(value, "track")
    step = 1
    while step < count:
        value = value + lax.ppermute(value, "track", [(i, i ^ step) for i in range(count)])
        step *= 2
    return value


def on_device(
    volume, labels, conv_taps, norm_gain, weight_in, bias_in, weight_out, layer_scale, head_weight, head_bias
):
    channels, planes, rows, depth = volume.shape
    hidden = weight_in.shape[1]
    classes = head_weight.shape[0]
    devices = lax.axis_size("track")
    par = (lax.axis_index("track") % 2).astype(jnp.int32).reshape(1)

    flat = volume.reshape(channels * OWN, depth)
    hb, ha = swap(flat, flat)
    tables = [tap_tables(conv_taps[s]) for s in range(2)]
    params = []
    for s in range(2):
        params.append(
            dict(
                gain=norm_gain[s][:, None],
                w_in=weight_in[s],
                w_in_t=weight_in[s].T,
                b_in=bias_in[s][:, None],
                w_out=weight_out[s],
                w_out_t=weight_out[s].T,
                scale=layer_scale[s][:, None],
            )
        )
    padded = jnp.zeros((ROWS, channels), BF16).at[:classes].set(head_weight)
    padded_b = jnp.full((ROWS,), -1e30, F32).at[:classes].set(head_bias)[:, None]
    flat_labels = labels.reshape(OWN // CHUNK, 1, CHUNK * depth)

    own_low = shape((OWN, channels, depth), BF16)
    own_wide = shape((OWN, channels, depth), F32)
    s_ext = pltpu.VMEM((EXT, channels, depth), F32)
    s_own = pltpu.VMEM((OWN, channels, depth), F32)
    s_wide = pltpu.VMEM((channels * OWN, depth), F32)
    s_bias = pltpu.VMEM((hidden, LANES), F32)
    s_chan = pltpu.VMEM((channels, LANES), F32)
    voxels = OWN * depth
    point = 2 * channels * hidden * voxels

    p = params[0]
    (mid,) = call(
        forward_kernel, "forward_one",
        (par, flat, ha, hb, tables[0], p["gain"], p["w_in"], p["b_in"], p["w_out"], p["scale"]),
        [own_low], [s_wide, s_ext, s_own], 2 * point,
    )
    mb, ma = swap(mid, mid)
    mid_tied, flat_tied = lax.optimization_barrier((mid, flat))
    mixed_one, ext_one = call(
        again_kernel, "again_one", (par, flat_tied, ha, hb, tables[0]),
        [own_wide, shape((EXT, channels, depth), BF16)], [s_wide, s_ext], 2 * point,
    )
    back_outs = [
        own_low, own_low, own_wide, own_wide,
        shape((2 * channels + ROWS, hidden), F32), shape((channels, LANES), F32),
    ]
    p = params[1]
    rim_a, rim_b, inner, dmixed, sums_two, small_two, head_sum, head_lanes = call(
        turn_kernel, "turn_two",
        (par, mid, ma, mb, flat_labels, tables[1], p["gain"], p["w_in"], p["w_in_t"], p["b_in"],
         p["w_out"], p["w_out_t"], p["scale"], padded, padded.T, padded_b),
        back_outs + [shape((ROWS, channels), F32), shape((ROWS, LANES), F32)],
        [s_ext, s_own, s_ext, s_bias, s_chan, s_chan], 6 * point,
    )
    rb, ra = swap(rim_a, rim_b)
    (taps_two,) = call(
        taps_two_kernel, "taps_two", (par, mid, ma, mb, dmixed, tables[1]),
        [shape((channels, LANES), F32)], [s_ext], 2 * point,
    )
    p = params[0]
    rim_a, rim_b, inner, dmixed, sums_one, small_one = call(
        back_kernel, "back_one",
        (par, inner, ra, rb, mixed_one, tables[0], p["gain"], p["w_in"], p["w_in_t"], p["b_in"],
         p["w_out"], p["w_out_t"], p["scale"]),
        back_outs, [s_ext, s_bias, s_chan, s_chan], 6 * point,
    )
    rb, ra = swap(rim_a, rim_b)
    (taps_one,) = call(
        taps_one_kernel, "taps_one", (ext_one, dmixed, tables[0]),
        [shape((channels, LANES), F32)], [s_ext], 2 * point,
    )
    (grad,) = call(
        last_kernel, "last", (inner, ra, rb),
        [shape((channels * OWN, depth), F32)], [s_own],
    )

    total = 1.0 / float(devices * planes * rows * depth)
    sums_two = summed(sums_two) * total
    sums_one = summed(sums_one) * total
    tail = jnp.concatenate(
        [small_one + taps_one, small_two + taps_two,
         jnp.pad(head_sum, ((0, 0), (0, LANES - channels))), head_lanes], axis=0
    )
    tail = summed(tail) * total
    stats = tail[: 2 * channels].reshape(2, channels, LANES)
    grad_taps = jnp.moveaxis(stats[:, :, : 3 * TAPS], 1, 2).reshape(2, 3, TAPS, channels)
    head_rows = tail[2 * channels : 2 * channels + classes, :channels]
    head_cols = jnp.sum(tail[2 * channels + ROWS : 2 * channels + ROWS + classes], axis=1)
    both = jnp.stack([sums_one, sums_two])
    return (
        grad.reshape(volume.shape),
        grad_taps,
        stats[:, :, 3 * TAPS],
        jnp.swapaxes(both[:, channels : 2 * channels], 1, 2),
        both[:, 2 * channels],
        both[:, :channels],
        stats[:, :, 3 * TAPS + 1],
        head_rows,
        head_cols,
    )


def solution(mesh):
    placed = (
        P(None, ("groups", "track"), None, None),
        P(("groups", "track"), None, None),
        P(), P(), P(), P(), P(), P(), P(), P(),
    )
    return jax.shard_map(
        on_device,
        mesh=mesh,
        in_specs=placed,
        out_specs=(
            P(None, ("groups", "track"), None, None),
            P("groups", None, None, None),
            P("groups", None),
            P("groups", None, None),
            P("groups", None),
            P("groups", None, None),
            P("groups", None),
            P("groups", None),
            P("groups"),
        ),
        check_vma=False,
    )
```

time: 655 us -> 168 us (0.26); the launches traced: 648 us -> 167 us
  matrix products: 295 us -> 0 us
  local copies, waits for them, and re-layouts: 115 us -> 28 us
  blocking collectives: 62.5 us -> 0 us
  Pallas kernels: 0 us -> 56.7 us
  other arithmetic: 56.6 us -> 7.87 us
  waiting for transfers between devices: 79 us -> 31.2 us
  starting transfers between devices: 23.8 us -> 42.3 us
  between operations: 15.9 us -> 1.33 us
    conv_general_dilated x18 -> x0, matrix products: 264 us -> none  [sweep(): lax.conv_general_dilated(field[None], kernel, (1, 1, 1), padding, dimensi...]
    psum x1 -> x0, waiting for transfers between devices: 78.9 us -> none  [on_device(): lax.psum((stacked[0], stacked[1], stacked[2], stacked[3], stacked[4], sta...]
    psum x1 -> x0, blocking collectives: 62.5 us -> none  [on_device(): lax.psum((stacked[0], stacked[1], stacked[2], stacked[3], stacked[4], sta...]
    pallas_call x0 -> x7, Pallas kernels: none -> 56.7 us  [call(): pl.pallas_call(kernel, name=name, out_shape=tuple(outs), in_specs=[smem i...]
    ppermute x8 -> x20, waiting for transfers between devices: 0.02 us -> 31.2 us  [the longest x12 31.1 us: summed(): lax.ppermute(value, 'track', [(i, i ^ step) for i in range(count)])]
    dot_general x15 -> x0, matrix products: 31.1 us -> none  [the longest x2 10.5 us: pointwise_back(): lax.dot_general(weight_out, grad_lift, (((0,), (0,)), ((), ())), preferre...]
    unnamed x227 -> x81, local copies, waits for them, and re-layouts: 39.6 us -> 13.7 us
    ppermute x8 -> x20, starting transfers between devices: 23.8 us -> 42.3 us  [the longest x12 24.9 us: summed(): lax.ppermute(value, 'track', [(i, i ^ step) for i in range(count)])]
  transfers between devices with their start and end apart: 9 -> 20, of which waited for: 1 -> 6; matrix products, arithmetic and copies ran while one was open for 12% -> 16% of each run, Pallas kernels for 0% -> 18%
where the time goes in v1:
time: 168 us; the launch traced here: 167 us
  Pallas kernels  56.7 us (34%)
  starting transfers between devices  42.3 us (25%)
  waiting for transfers between devices  31.2 us (19%)
  local copies, waits for them, and re-layouts  28 us (17%)
  other arithmetic  7.87 us (5%)
    pallas_call x7, Pallas kernels, call(): pl.pallas_call(kernel, name=name, out_shape=tuple(outs), in_specs=[smem i...  56.7 us
    ppermute x12, waiting for transfers between devices, summed(): lax.ppermute(value, 'track', [(i, i ^ step) for i in range(count)])  31.1 us
    ppermute x12, starting transfers between devices, summed(): lax.ppermute(value, 'track', [(i, i ^ step) for i in range(count)])  24.9 us
    unnamed x81, local copies, waits for them, and re-layouts  13.7 us
    ppermute x4, starting transfers between devices, swap(): lax.ppermute(value_a, 'track', near)  13.1 us
    ppermute x4, starting transfers between devices, swap(): lax.ppermute(value_b, 'track', far)  4.35 us
  transfers between devices with their start and end apart: 20, of which 6 were waited for; matrix products, arithmetic and copies ran while one was open for 16% of the time, Pallas kernels for 18%

profile of v1, /device:TPU:0, one launch (start us, length us, event | category | flops | bytes accessed | tf_op | source)
XLA Modules:
  0.0 167.3 jit_solution(18255764337774956584)
XLA Ops:
  1.3 4.4 %collective-permute-start = (bf16[2304,128]{1,0:T(8,128)(2,1)}, bf16[2304,128]{1,0:T(8,128)(2,1)S(1)}, u32[]{:S(2)}, u32[]{:S(2)}) collective-permute-start(bf16[2304,128]{1,0:T(8,128)(2,1)} %bitcast.67), channel_id=1, source_target_pairs={{0,1},{1,0},{2,3},{3,2},{4,5},{5,4},{6,7},{7,6},{8,9},{9,8},{10,11... | collective-permute-start | bytes 1769480 | tf_op jit(solution)/shard_map/ppermute | solution.py:407
  11.0 1.6 slice_bitcast_fusion.3
  16.0 7.9 %forward_one.1.mid = bf16[24,96,128]{2,1,0:T(8,128)(2,1)S(1)} custom-call(s32[1]{0:T(128)} %bitcast.par, bf16[2304,128]{1,0:T(8,128)(2,1)S(1)} %bitcast.68, bf16[2304,128]{1,0:T(8,128)(2,1)S(1)} %collective-permute-done.ha, bf16[2304,128]{1,0:T(8,128)(2,1)S(1)} %collective-permute-done.1.hb, f32[28,96,128]{2,1,0:T(8,128)S(1)} %pad_maximum_fusion.taps, ...), custom_call_target="tpu_custom_call" | custom-call | flops 452984832 | bytes 3885316 | tf_op jit(solution)/shard_map/forward_one/pallas_call | solution.py:385
  25.3 6.1 %collective-permute-start.2 = (bf16[24,96,128]{2,1,0:T(8,128)(2,1)S(1)}, bf16[24,96,128]{2,1,0:T(8,128)(2,1)}, u32[]{:S(2)}, u32[]{:S(2)}) collective-permute-start(bf16[24,96,128]{2,1,0:T(8,128)(2,1)S(1)} %forward_one.1.mid), channel_id=1, source_target_pairs={{0,1},{1,0},{2,3},{3,2},{4,5},{5,4},{6,7},{7,6},{8,9},{9,8},{10,11... | collective-permute-start | bytes 1769480 | tf_op jit(solution)/shard_map/ppermute | solution.py:407
  34.0 1.6 copy.55.w_in
  35.6 1.6 copy.76
  39.1 18.4 %turn_two.1 = (bf16[24,96,128]{2,1,0:T(8,128)(2,1)}, bf16[24,96,128]{2,1,0:T(8,128)(2,1)}, f32[24,96,128]{2,1,0:T(8,128)S(1)}, f32[24,96,128]{2,1,0:T(8,128)S(1)...) custom-call(s32[1]{0:T(128)} %bitcast.par, ...), custom_call_target="tpu_custom_call" | custom-call | flops 1358954496 | bytes 7360804 | tf_op jit(solution)/shard_map/turn_two/pallas_call | solution.py:385
  60.9 2.6 %collective-permute-start.4 = (bf16[24,96,128]{2,1,0:T(8,128)(2,1)}, bf16[24,96,128]{2,1,0:T(8,128)(2,1)}, u32[]{:S(2)}, u32[]{:S(2)}) collective-permute-start(bf16[24,96,128]{2,1,0:T(8,128)(2,1)} %get-tuple-element.51), channel_id=1, source_target_pairs={{0,1},{1,0},{2,3},{3,2},{4,5},{5,4},{6,7},{7,6},{8,9},{9,8},{10,11... | collective-permute-start | bytes 1769480 | tf_op jit(solution)/shard_map/ppermute | solution.py:407
  65.0 1.6 copy.72
  69.8 4.3 %again_one.1 = (f32[24,96,128]{2,1,0:T(8,128)S(1)}, bf16[72,96,128]{2,1,0:T(8,128)(2,1)S(1)}) custom-call(s32[1]{0:T(128)} %bitcast.par, bf16[2304,128]{1,0:T(8,128)(2,1)S(1)} %bitcast.69, bf16[2304,128]{1,0:T(8,128)(2,1)S(1)} %copy-done.5, bf16[2304,128]{1,0:T(8,128)(2,1)S(1)} %copy-done.3, f32[28,96,128]{2,1,0:T(8,128)S(1)} %pad_maximum_fusion.taps), custom_call_target="tpu_custom_call" | custom-call | flops 452984832 | bytes 6094852 | tf_op jit(solution)/shard_map/again_one/pallas_call | solution.py:385
  74.1 3.1 %collective-permute-start.16 = (f32[200,384]{1,0:T(8,128)S(1)}, f32[200,384]{1,0:T(8,128)S(1)}, u32[]{:S(2)}, u32[]{:S(2)}) collective-permute-start(f32[200,384]{1,0:T(8,128)S(1)} %copy-done.20), channel_id=1, source_target_pairs={{0,1},{1,0},{2,3},{3,2},{4,5},{5,4},{6,7},{7,6},{8,9},{9,8},{10,11... | collective-permute-start | bytes 921608 | tf_op jit(solution)/shard_map/ppermute | solution.py:416
  77.3 6.6 %taps_two.1 = f32[96,128]{1,0:T(8,128)S(1)} custom-call(s32[1]{0:T(128)} %bitcast.par, bf16[24,96,128]{2,1,0:T(8,128)(2,1)S(1)} %forward_one.1.mid, bf16[24,96,128]{2,1,0:T(8,128)(2,1)} %collective-permute-done.2.ma, bf16[24,96,128]{2,1,0:T(8,128)(2,1)} %collective-permute-done.3.mb, f32[24,96,128]{2,1,0:T(8,128)S(1)} %copy-done.7, ...), custom_call_target="tpu_custom_call" | custom-call | flops 452984832 | bytes 4374532 | tf_op jit(solution)/shard_map/taps_two/pallas_call | solution.py:385
  84.0 12.7 %back_one.1 = (bf16[24,96,128]{2,1,0:T(8,128)(2,1)}, bf16[24,96,128]{2,1,0:T(8,128)(2,1)S(1)}, f32[24,96,128]{2,1,0:T(8,128)S(1)}, f32[24,96,128]{2,1,0:T(8,128)...) custom-call(s32[1]{0:T(128)} %bitcast.par, f32[24,96,128]{2,1,0:T(8,128)S(1)} %copy-done.9, ...), custom_call_target="tpu_custom_call" | custom-call | flops 1358954496 | bytes 9107716 | tf_op jit(solution)/shard_map/back_one/pallas_call | solution.py:385
  96.7 5.3 %taps_one.1 = f32[96,128]{1,0:T(8,128)S(1)} custom-call(bf16[72,96,128]{2,1,0:T(8,128)(2,1)S(1)} %get-tuple-element.59.ext_low, f32[24,96,128]{2,1,0:T(8,128)S(1)} %get-tuple-element.60.dmixed, f32[28,96,128]{2,1,0:T(8,128)S(1)} %pad_maximum_fusion.taps), custom_call_target="tpu_custom_call" | custom-call | flops 452984832 | bytes 4374528 | tf_op jit(solution)/shard_map/taps_one/pallas_call | solution.py:385
  104.6 7.7 %collective-permute-done.17 = f32[200,384]{1,0:T(8,128)S(1)} collective-permute-done((f32[200,384]{1,0:T(8,128)S(1)}, f32[200,384]{1,0:T(8,128)S(1)}, u32[]{:S(2)}, u32[]{:S(2)}) %collective-permute-start.17) | collective-permute-done | bytes 307232 | tf_op jit(solution)/shard_map/ppermute | solution.py:416
  112.3 2.1 %collective-permute-start.18 = (f32[200,384]{1,0:T(8,128)S(1)}, f32[200,384]{1,0:T(8,128)S(1)}, u32[]{:S(2)}, u32[]{:S(2)}) collective-permute-start(f32[200,384]{1,0:T(8,128)S(1)} %add.126), channel_id=1, source_target_pairs={{0,4},{1,5},{2,6},{3,7},{4,0},{5,1},{6,2},{7,3},{8,12},{9,13},{10,... | collective-permute-start | bytes 921608 | tf_op jit(solution)/shard_map/ppermute | solution.py:416
  115.8 7.3 %collective-permute-done.10 = f32[208,128]{1,0:T(8,128)S(1)} collective-permute-done((f32[208,128]{1,0:T(8,128)S(1)}, f32[208,128]{1,0:T(8,128)S(1)}, u32[]{:S(2)}, u32[]{:S(2)}) %collective-permute-start.10) | collective-permute-done | bytes 106528 | tf_op jit(solution)/shard_map/ppermute | solution.py:416
  123.1 2.2 %collective-permute-start.11 = (f32[208,128]{1,0:T(8,128)S(1)}, f32[208,128]{1,0:T(8,128)S(1)}, u32[]{:S(2)}, u32[]{:S(2)}) collective-permute-start(f32[208,128]{1,0:T(8,128)S(1)} %add.119), channel_id=1, source_target_pairs={{0,8},{1,9},{2,10},{3,11},{4,12},{5,13},{6,14},{7,15},{8,0},{9,1},... | collective-permute-start | bytes 319496 | tf_op jit(solution)/shard_map/ppermute | solution.py:416
  127.8 4.2 %collective-permute-start.19 = (f32[200,384]{1,0:T(8,128)S(1)}, f32[200,384]{1,0:T(8,128)}, u32[]{:S(2)}, u32[]{:S(2)}) collective-permute-start(f32[200,384]{1,0:T(8,128)S(1)} %add.127), channel_id=1, source_target_pairs={{0,8},{1,9},{2,10},{3,11},{4,12},{5,13},{6,14},{7,15},{8,0},{9,1},... | collective-permute-start | bytes 921608 | tf_op jit(solution)/shard_map/ppermute | solution.py:416
  132.0 3.1 %collective-permute-done.13 = f32[200,384]{1,0:T(8,128)S(1)} collective-permute-done((f32[200,384]{1,0:T(8,128)S(1)}, f32[200,384]{1,0:T(8,128)S(1)}, u32[]{:S(2)}, u32[]{:S(2)}) %collective-permute-start.13) | collective-permute-done | bytes 307232 | tf_op jit(solution)/shard_map/ppermute | solution.py:416
  140.4 8.4 %collective-permute-done.14 = f32[200,384]{1,0:T(8,128)} collective-permute-done((f32[200,384]{1,0:T(8,128)}, f32[200,384]{1,0:T(8,128)}, u32[]{:S(2)}, u32[]{:S(2)}) %collective-permute-start.14) | collective-permute-done | bytes 307232 | tf_op jit(solution)/shard_map/ppermute | solution.py:416
  149.9 7.4 %collective-permute-start.15 = (f32[200,384]{1,0:T(8,128)S(1)}, f32[200,384]{1,0:T(8,128)S(1)}, u32[]{:S(2)}, u32[]{:S(2)}) collective-permute-start(f32[200,384]{1,0:T(8,128)S(1)} %add.123), channel_id=1, source_target_pairs={{0,8},{1,9},{2,10},{3,11},{4,12},{5,13},{6,14},{7,15},{8,0},{9,1},... | collective-permute-start | bytes 921608 | tf_op jit(solution)/shard_map/ppermute | solution.py:416
  160.2 2.4 %collective-permute-done.19 = f32[200,384]{1,0:T(8,128)} collective-permute-done((f32[200,384]{1,0:T(8,128)S(1)}, f32[200,384]{1,0:T(8,128)}, u32[]{:S(2)}, u32[]{:S(2)}) %collective-permute-start.19) | collective-permute-done | bytes 307232 | tf_op jit(solution)/shard_map/ppermute | solution.py:416
  163.5 2.3 %collective-permute-done.15 = f32[200,384]{1,0:T(8,128)S(1)} collective-permute-done((f32[200,384]{1,0:T(8,128)S(1)}, f32[200,384]{1,0:T(8,128)S(1)}, u32[]{:S(2)}, u32[]{:S(2)}) %collective-permute-start.15) | collective-permute-done | bytes 307232 | tf_op jit(solution)/shard_map/ppermute | solution.py:416
  (158 shorter events, 41.1 us)
Async XLA Ops:
  0.6 15.2 %collective-permute-start.1 = (bf16[2304,128]{1,0:T(8,128)(2,1)}, bf16[2304,128]{1,0:T(8,128)(2,1)S(1)}, u32[]{:S(2)}, u32[]{:S(2)}) collective-permute-start(bf16[2304,128]{1,0:T(8,128)(2,1)} %bitcast.66), channel_id=1, source_target_pairs={{1,2},{2,1},{3,4},{4,3},{5,6},{6,5},{7,8},{8,7},{9,10},{10,9},{11,... | collective-permute-start | bytes 1769480 | tf_op jit(solution)/shard_map/ppermute | solution.py:407
  1.3 14.5 %collective-permute-start = (bf16[2304,128]{1,0:T(8,128)(2,1)}, bf16[2304,128]{1,0:T(8,128)(2,1)S(1)}, u32[]{:S(2)}, u32[]{:S(2)}) collective-permute-start(bf16[2304,128]{1,0:T(8,128)(2,1)} %bitcast.67), channel_id=1, source_target_pairs={{0,1},{1,0},{2,3},{3,2},{4,5},{5,4},{6,7},{7,6},{8,9},{9,8},{10,11... | collective-permute-start | bytes 1769480 | tf_op jit(solution)/shard_map/ppermute | solution.py:407
  15.9 8.0 %copy-start.2 = (bf16[2304,128]{1,0:T(8,128)(2,1)}, bf16[2304,128]{1,0:T(8,128)(2,1)S(1)}, u32[]{:S(2)}) copy-start(bf16[2304,128]{1,0:T(8,128)(2,1)S(1)} %collective-permute-done.1.hb) | copy-start | bytes 1769476
  15.9 15.5 %copy-start.36 = (f32[4]{0:T(128)S(1)}, f32[4]{0:T(128)}, u32[]{:S(2)}) copy-start(f32[4]{0:T(128)} %param.23) | copy-start | bytes 52
  15.9 15.6 %copy-start.35 = (bf16[4,96]{1,0:T(4,128)(2,1)S(1)}, bf16[4,96]{1,0:T(4,128)(2,1)}, u32[]{:S(2)}) copy-start(bf16[4,96]{1,0:T(4,128)(2,1)} %param.22) | copy-start | bytes 2308
  15.9 15.8 %copy-start.34 = (f32[96,1]{0,1:T(1,128)S(1)}, f32[96,1]{0,1:T(1,128)}, u32[]{:S(2)}) copy-start(f32[96,1]{0,1:T(1,128)} %get-tuple-element.91) | copy-start | bytes 1156
  23.9 15.1 %collective-permute-start.3 = (bf16[24,96,128]{2,1,0:T(8,128)(2,1)S(1)}, bf16[24,96,128]{2,1,0:T(8,128)(2,1)}, u32[]{:S(2)}, u32[]{:S(2)}) collective-permute-start(bf16[24,96,128]{2,1,0:T(8,128)(2,1)S(1)} %forward_one.1.mid), channel_id=1, source_target_pairs={{1,2},{2,1},{3,4},{4,3},{5,6},{6,5},{7,8},{8,7},{9,10},{10,9},{11,... | collective-permute-start | bytes 1769480 | tf_op jit(solution)/shard_map/ppermute | solution.py:407
  25.3 13.6 %collective-permute-start.2 = (bf16[24,96,128]{2,1,0:T(8,128)(2,1)S(1)}, bf16[24,96,128]{2,1,0:T(8,128)(2,1)}, u32[]{:S(2)}, u32[]{:S(2)}) collective-permute-start(bf16[24,96,128]{2,1,0:T(8,128)(2,1)S(1)} %forward_one.1.mid), channel_id=1, source_target_pairs={{0,1},{1,0},{2,3},{3,2},{4,5},{5,4},{6,7},{7,6},{8,9},{9,8},{10,11... | collective-permute-start | bytes 1769480 | tf_op jit(solution)/shard_map/ppermute | solution.py:407
  60.9 23.0 %collective-permute-start.4 = (bf16[24,96,128]{2,1,0:T(8,128)(2,1)}, bf16[24,96,128]{2,1,0:T(8,128)(2,1)}, u32[]{:S(2)}, u32[]{:S(2)}) collective-permute-start(bf16[24,96,128]{2,1,0:T(8,128)(2,1)} %get-tuple-element.51), channel_id=1, source_target_pairs={{0,1},{1,0},{2,3},{3,2},{4,5},{5,4},{6,7},{7,6},{8,9},{9,8},{10,11... | collective-permute-start | bytes 1769480 | tf_op jit(solution)/shard_map/ppermute | solution.py:407
  63.5 20.4 %collective-permute-start.5 = (bf16[24,96,128]{2,1,0:T(8,128)(2,1)}, bf16[24,96,128]{2,1,0:T(8,128)(2,1)}, u32[]{:S(2)}, u32[]{:S(2)}) collective-permute-start(bf16[24,96,128]{2,1,0:T(8,128)(2,1)} %get-tuple-element.52), channel_id=1, source_target_pairs={{1,2},{2,1},{3,4},{4,3},{5,6},{6,5},{7,8},{8,7},{9,10},{10,9},{11,... | collective-permute-start | bytes 1769480 | tf_op jit(solution)/shard_map/ppermute | solution.py:407
  74.1 28.0 %collective-permute-start.16 = (f32[200,384]{1,0:T(8,128)S(1)}, f32[200,384]{1,0:T(8,128)S(1)}, u32[]{:S(2)}, u32[]{:S(2)}) collective-permute-start(f32[200,384]{1,0:T(8,128)S(1)} %copy-done.20), channel_id=1, source_target_pairs={{0,1},{1,0},{2,3},{3,2},{4,5},{5,4},{6,7},{7,6},{8,9},{9,8},{10,11... | collective-permute-start | bytes 921608 | tf_op jit(solution)/shard_map/ppermute | solution.py:416
  102.0 1.5 collective-permute-start.8
  102.2 10.1 %collective-permute-start.17 = (f32[200,384]{1,0:T(8,128)S(1)}, f32[200,384]{1,0:T(8,128)S(1)}, u32[]{:S(2)}, u32[]{:S(2)}) collective-permute-start(f32[200,384]{1,0:T(8,128)S(1)} %add.125), channel_id=1, source_target_pairs={{0,2},{1,3},{2,0},{3,1},{4,6},{5,7},{6,4},{7,5},{8,10},{9,11},{10,... | collective-permute-start | bytes 921608 | tf_op jit(solution)/shard_map/ppermute | solution.py:416
  103.4 22.0 %collective-permute-start.12 = (f32[200,384]{1,0:T(8,128)S(1)}, f32[200,384]{1,0:T(8,128)S(1)}, u32[]{:S(2)}, u32[]{:S(2)}) collective-permute-start(f32[200,384]{1,0:T(8,128)S(1)} %get-tuple-element.65), channel_id=1, source_target_pairs={{0,1},{1,0},{2,3},{3,2},{4,5},{5,4},{6,7},{7,6},{8,9},{9,8},{10,11... | collective-permute-start | bytes 921608 | tf_op jit(solution)/shard_map/ppermute | solution.py:416
  103.6 10.8 %collective-permute-start.9 = (f32[208,128]{1,0:T(8,128)S(1)}, f32[208,128]{1,0:T(8,128)S(1)}, u32[]{:S(2)}, u32[]{:S(2)}) collective-permute-start(f32[208,128]{1,0:T(8,128)S(1)} %fusion.9), channel_id=1, source_target_pairs={{0,2},{1,3},{2,0},{3,1},{4,6},{5,7},{6,4},{7,5},{8,10},{9,11},{10,... | collective-permute-start | bytes 319496 | tf_op jit(solution)/shard_map/ppermute | solution.py:416
  112.3 15.4 %collective-permute-start.18 = (f32[200,384]{1,0:T(8,128)S(1)}, f32[200,384]{1,0:T(8,128)S(1)}, u32[]{:S(2)}, u32[]{:S(2)}) collective-permute-start(f32[200,384]{1,0:T(8,128)S(1)} %add.126), channel_id=1, source_target_pairs={{0,4},{1,5},{2,6},{3,7},{4,0},{5,1},{6,2},{7,3},{8,12},{9,13},{10,... | collective-permute-start | bytes 921608 | tf_op jit(solution)/shard_map/ppermute | solution.py:416
  114.4 8.7 %collective-permute-start.10 = (f32[208,128]{1,0:T(8,128)S(1)}, f32[208,128]{1,0:T(8,128)S(1)}, u32[]{:S(2)}, u32[]{:S(2)}) collective-permute-start(f32[208,128]{1,0:T(8,128)S(1)} %add.118), channel_id=1, source_target_pairs={{0,4},{1,5},{2,6},{3,7},{4,0},{5,1},{6,2},{7,3},{8,12},{9,13},{10,... | collective-permute-start | bytes 319496 | tf_op jit(solution)/shard_map/ppermute | solution.py:416
  123.1 8.8 %collective-permute-start.11 = (f32[208,128]{1,0:T(8,128)S(1)}, f32[208,128]{1,0:T(8,128)S(1)}, u32[]{:S(2)}, u32[]{:S(2)}) collective-permute-start(f32[208,128]{1,0:T(8,128)S(1)} %add.119), channel_id=1, source_target_pairs={{0,8},{1,9},{2,10},{3,11},{4,12},{5,13},{6,14},{7,15},{8,0},{9,1},... | collective-permute-start | bytes 319496 | tf_op jit(solution)/shard_map/ppermute | solution.py:416
  125.4 9.6 %collective-permute-start.13 = (f32[200,384]{1,0:T(8,128)S(1)}, f32[200,384]{1,0:T(8,128)S(1)}, u32[]{:S(2)}, u32[]{:S(2)}) collective-permute-start(f32[200,384]{1,0:T(8,128)S(1)} %add.121), channel_id=1, source_target_pairs={{0,2},{1,3},{2,0},{3,1},{4,6},{5,7},{6,4},{7,5},{8,10},{9,11},{10,... | collective-permute-start | bytes 921608 | tf_op jit(solution)/shard_map/ppermute | solution.py:416
  127.0 31.6 %collective-permute-start.6 = (bf16[24,96,128]{2,1,0:T(8,128)(2,1)}, bf16[24,96,128]{2,1,0:T(8,128)(2,1)S(1)}, u32[]{:S(2)}, u32[]{:S(2)}) collective-permute-start(bf16[24,96,128]{2,1,0:T(8,128)(2,1)} %get-tuple-element.56), channel_id=1, source_target_pairs={{0,1},{1,0},{2,3},{3,2},{4,5},{5,4},{6,7},{7,6},{8,9},{9,8},{10,11... | collective-permute-start | bytes 1769480 | tf_op jit(solution)/shard_map/ppermute | solution.py:407
  127.0 31.6 %collective-permute-start.7 = (bf16[24,96,128]{2,1,0:T(8,128)(2,1)S(1)}, bf16[24,96,128]{2,1,0:T(8,128)(2,1)S(1)}, u32[]{:S(2)}, u32[]{:S(2)}) collective-permute-start(bf16[24,96,128]{2,1,0:T(8,128)(2,1)S(1)} %get-tuple-element.57), channel_id=1, source_target_pairs={{1,2},{2,1},{3,4},{4,3},{5,6},{6,5},{7,8},{8,7},{9,10},{10,9},{11,... | collective-permute-start | bytes 1769480 | tf_op jit(solution)/shard_map/ppermute | solution.py:407
  127.8 34.7 %collective-permute-start.19 = (f32[200,384]{1,0:T(8,128)S(1)}, f32[200,384]{1,0:T(8,128)}, u32[]{:S(2)}, u32[]{:S(2)}) collective-permute-start(f32[200,384]{1,0:T(8,128)S(1)} %add.127), channel_id=1, source_target_pairs={{0,8},{1,9},{2,10},{3,11},{4,12},{5,13},{6,14},{7,15},{8,0},{9,1},... | collective-permute-start | bytes 921608 | tf_op jit(solution)/shard_map/ppermute | solution.py:416
  135.8 13.0 %collective-permute-start.14 = (f32[200,384]{1,0:T(8,128)}, f32[200,384]{1,0:T(8,128)}, u32[]{:S(2)}, u32[]{:S(2)}) collective-permute-start(f32[200,384]{1,0:T(8,128)} %add.122), channel_id=1, source_target_pairs={{0,4},{1,5},{2,6},{3,7},{4,0},{5,1},{6,2},{7,3},{8,12},{9,13},{10,... | collective-permute-start | bytes 921608 | tf_op jit(solution)/shard_map/ppermute | solution.py:416
  149.9 15.9 %collective-permute-start.15 = (f32[200,384]{1,0:T(8,128)S(1)}, f32[200,384]{1,0:T(8,128)S(1)}, u32[]{:S(2)}, u32[]{:S(2)}) collective-permute-start(f32[200,384]{1,0:T(8,128)S(1)} %add.123), channel_id=1, source_target_pairs={{0,8},{1,9},{2,10},{3,11},{4,12},{5,13},{6,14},{7,15},{8,0},{9,1},... | collective-permute-start | bytes 921608 | tf_op jit(solution)/shard_map/ppermute | solution.py:416
  (33 other events, 112.5 us)

commit v2 on v1

v2 whole, which is shorter than its diff:
```python
import functools

import jax
import jax.numpy as jnp
from jax import lax
from jax.experimental import pallas as pl
from jax.experimental.pallas import tpu as pltpu
from jax.sharding import PartitionSpec as P

F32 = jnp.float32
BF16 = jnp.bfloat16
LANES = 128
ROWS = 8
PAIR = 16
RADIUS = 3
TAPS = 7
PLANES = 3
Y = 8
OWN = PLANES * Y
EXT = (PLANES + 2 * RADIUS) * Y
CHUNK = 12
GELU_A = 0.7978845608028654
GELU_B = 0.044715 * GELU_A
MIB = 1024 * 1024


T_X, T_Y, T_Z, T_Z_BACK = 0, 7, 14, 21
GAIN, SCALE = 21, 22


def group_rows(index, size=ROWS):
    return pl.ds(pl.multiple_of(index * size, size), size)


def coeffs(source, rows, first, count=TAPS):
    if len(source.shape) == 3:
        return [source[k, rows, :] for k in range(first, first + count)]
    found = []
    for k in range(first, first + count):
        column = source[rows, k : k + 1]
        found.append(jnp.broadcast_to(column, (column.shape[0], LANES)))
    return found


def tables_kernel(
    cols, b_in, w_in, w_out, head, head_b, labels,
    tables, cols_out, b_out, w_in_out, w_in_t, w_out_out, w_out_t, head_out, head_t, head_b_out, labels_out,
):
    def one(group, carry):
        rows = group_rows(group)
        lane = lax.broadcasted_iota(jnp.int32, (ROWS, LANES), 1)
        for s in range(2):
            for k, value in enumerate(coeffs(cols.at[s], rows, T_X, 2 * TAPS)):
                tables[s, k, rows, :] = value
            for k, value in enumerate(coeffs(cols.at[s], rows, T_Z)):
                for first, reach in ((T_Z, k - RADIUS), (T_Z_BACK, RADIUS - k)):
                    kept = (lane + reach >= 0) & (lane + reach < LANES)
                    tables[s, first + k, rows, :] = jnp.where(kept, value, 0.0)
        return carry

    lax.fori_loop(0, tables.shape[2] // ROWS, one, 0)
    for s in range(2):
        w_in_t[s] = w_in[s].T
        w_out_t[s] = w_out[s].T
    head_t[...] = head[...].astype(F32).T.astype(BF16)
    for source, out in (
        (cols, cols_out), (b_in, b_out), (w_in, w_in_out), (w_out, w_out_out), (head, head_out),
        (head_b, head_b_out), (labels, labels_out),
    ):
        out[...] = source[...]


def rim_coeffs(par, cols, rows, low_if_even):
    tx = coeffs(cols, rows, T_X)
    zero = jnp.zeros_like(tx[0])
    low = (par[0] == 0) == low_if_even
    found = {}
    for d in range(1 - PLANES, PLANES):
        found[d] = jnp.where(low, tx[d] if d >= 0 else zero, tx[2 * RADIUS + d] if d <= 0 else zero)
    return found


def unpack(source, wide, out, first=0):
    wide[...] = source[...].astype(F32)

    def one(group, carry):
        rows = group_rows(group)
        for tile in range(OWN):
            out[first + tile, rows, :] = wide[pl.ds(group * ROWS * OWN + tile, ROWS, stride=OWN), :]
        return carry

    lax.fori_loop(0, out.shape[1] // ROWS, one, 0)


def widen(source, ext, first, count):
    def one(tile, carry):
        ext[first + tile] = source[tile].astype(F32)
        return carry

    lax.fori_loop(0, count, one, 0, unroll=4)


def weighted(terms, total=None):
    for coeff, value in terms:
        product = coeff * value
        total = product if total is None else total + product
    return total


def along_own(par, own, near, cols, out):
    def one(group, carry):
        rows = group_rows(group, PAIR)
        tx = coeffs(cols, rows, T_X)
        tn = rim_coeffs(par, cols, rows, False)
        for y in range(Y):
            mine = [own[r * Y + y, rows, :].astype(F32) for r in range(PLANES)]
            other = [near[r * Y + y, rows, :].astype(F32) for r in range(PLANES)]
            for p in range(PLANES):
                out[p * Y + y, rows, :] = weighted(
                    [(tx[RADIUS + r - p], mine[r]) for r in range(PLANES)]
                    + [(tn[q - p], other[q]) for q in range(PLANES)]
                )
        return carry

    lax.fori_loop(0, out.shape[1] // PAIR, one, 0)


def along_far(par, part, far, cols, out):
    def one(group, carry):
        rows = group_rows(group, PAIR)
        tf = rim_coeffs(par, cols, rows, True)
        for y in range(Y):
            other = [far[r * Y + y, rows, :].astype(F32) for r in range(PLANES)]
            for p in range(PLANES):
                out[p * Y + y, rows, :] = weighted(
                    [(tf[q - p], other[q]) for q in range(PLANES)], part[p * Y + y, rows, :]
                )
        return carry

    lax.fori_loop(0, out.shape[1] // PAIR, one, 0)


def across(field, ty, y):
    return weighted([(ty[k], field[y + k - RADIUS]) for k in range(TAPS) if 0 <= y + k - RADIUS < Y])


def across_back(field, ty, y):
    return weighted([(ty[k], field[y - k + RADIUS]) for k in range(TAPS) if 0 <= y - k + RADIUS < Y])


def turned(value, shift):
    return value if shift % LANES == 0 else pltpu.roll(value, shift % LANES, 1)


def rest_of_conv(field, cols, mixed):
    def one(group, carry):
        rows = group_rows(group)
        ty = coeffs(cols, rows, T_Y)
        tz = coeffs(cols, rows, T_Z)
        for p in range(PLANES):
            plane = [field[p * Y + y, rows, :] for y in range(Y)]
            for y in range(Y):
                value = across(plane, ty, y)
                mixed[p * Y + y, rows, :] = weighted(
                    [(tz[k], turned(value, RADIUS - k)) for k in range(TAPS)]
                )
        return carry

    lax.fori_loop(0, mixed.shape[1] // ROWS, one, 0)


def convolve_back(dmixed, cols, along):
    def one(group, carry):
        rows = group_rows(group)
        ty = coeffs(cols, rows, T_Y)
        tz = coeffs(cols, rows, T_Z_BACK)
        for p in range(PLANES):
            cross = []
            for y in range(Y):
                value = dmixed[p * Y + y, rows, :]
                cross.append(weighted([(tz[k], turned(value, k - RADIUS)) for k in range(TAPS)]))
            for y in range(Y):
                along[p * Y + y, rows, :] = across_back(cross, ty, y)
        return carry

    lax.fori_loop(0, dmixed.shape[1] // ROWS, one, 0)


def rim(par, along, cols, far, out):
    def one(group, carry):
        rows = group_rows(group, PAIR)
        tt = rim_coeffs(par, cols, rows, far)
        for y in range(Y):
            column = [along[p * Y + y, rows, :] for p in range(PLANES)]
            for q in range(PLANES):
                out[q * Y + y, rows, :] = weighted(
                    [(tt[q - p], column[p]) for p in range(PLANES)]
                ).astype(out.dtype)
        return carry

    lax.fori_loop(0, out.shape[1] // PAIR, one, 0)


def inside(along, cols, base, out):
    def one(group, carry):
        rows = group_rows(group)
        tx = coeffs(cols, rows, T_X)
        for y in range(Y):
            column = [along[p * Y + y, rows, :] for p in range(PLANES)]
            for r in range(PLANES):
                out[r * Y + y, rows, :] = weighted(
                    [(tx[RADIUS + r - p], column[p]) for p in range(PLANES)], base[r * Y + y, rows, :]
                )
        return carry

    lax.fori_loop(0, out.shape[1] // ROWS, one, 0)


def tap_sums(ext, dmixed, along, cols, out):
    lane = lax.broadcasted_iota(jnp.int32, (ROWS, LANES), 1)

    def one(group, carry):
        rows = group_rows(group)
        tx = coeffs(cols, rows, T_X)
        ty = coeffs(cols, rows, T_Y)
        tz = coeffs(cols, rows, T_Z_BACK)
        sum_x, sum_y, sum_z = ([None] * TAPS for _ in range(3))

        def add(sums, k, value):
            sums[k] = value if sums[k] is None else sums[k] + value

        for p in range(PLANES):
            plane = []
            for y in range(Y):
                column = [ext[(p + k) * Y + y, rows, :] for k in range(TAPS)]
                plane.append(weighted([(tx[k], column[k]) for k in range(TAPS)]))
                back = along[p * Y + y, rows, :]
                for k in range(TAPS):
                    add(sum_x, k, back * column[k])
            for y in range(Y):
                value = dmixed[p * Y + y, rows, :]
                spun = [turned(value, k - RADIUS) for k in range(TAPS)]
                field = across(plane, ty, y)
                for k in range(TAPS):
                    add(sum_z, k, spun[k] * field)
                cross = weighted([(tz[k], spun[k]) for k in range(TAPS)])
                for k in range(TAPS):
                    if 0 <= y + k - RADIUS < Y:
                        add(sum_y, k, cross * plane[y + k - RADIUS])
        for k in range(TAPS):
            reach = k - RADIUS
            kept = (lane - reach >= 0) & (lane - reach < LANES)
            sum_z[k] = jnp.where(kept, sum_z[k], 0.0)
        total = jnp.zeros((ROWS, LANES), F32)
        for index, value in enumerate(sum_x + sum_y + sum_z):
            total = jnp.where(lane == index, jnp.sum(value, axis=1, keepdims=True), total)
        out[rows, :] = total
        return carry

    lax.fori_loop(0, dmixed.shape[1] // ROWS, one, 0)


def tiles(ref, first):
    return jnp.concatenate([ref[first + i] for i in range(CHUNK)], axis=1)


def put(ref, first, value):
    for i in range(CHUNK):
        ref[first + i] = value[:, i * LANES : (i + 1) * LANES].astype(ref.dtype)


def folded(value):
    total = value[:, :LANES]
    for i in range(1, CHUNK):
        total = total + value[:, i * LANES : (i + 1) * LANES]
    return total


def normalise(mixed):
    scale = 1.0 / mixed.shape[0]
    centred = mixed - jnp.sum(mixed, axis=0, keepdims=True) * scale
    variance = jnp.sum(centred * centred, axis=0, keepdims=True) * scale
    inverse = lax.rsqrt(variance + 1e-06)
    return centred * inverse, inverse


def normalise_back(g_norm, normal, inverse, gain):
    share = 1.0 / g_norm.shape[0]
    g_normal = g_norm * gain
    mean_a = jnp.sum(g_normal, axis=0, keepdims=True) * share
    mean_b = jnp.sum(g_normal * normal, axis=0, keepdims=True) * share
    return inverse * (g_normal - mean_a - normal * mean_b)


def dot(a, b):
    return jnp.dot(a, b, preferred_element_type=F32)


def dot_t(a, b):
    return lax.dot_general(a, b, (((1,), (1,)), ((), ())), preferred_element_type=F32)


def gelu_parts(hidden):
    square = hidden * hidden
    half = jnp.tanh(hidden * (GELU_A + GELU_B * square))
    rise = 0.5 + 0.5 * half
    act = (hidden * rise).astype(BF16)
    slope = rise + (hidden * (0.5 - 0.5 * (half * half))) * (GELU_A + 3.0 * GELU_B * square)
    return act, slope


def steps():
    return [(step, step * CHUNK) for step in range(OWN // CHUNK)]


def mixed_sums(pairs):
    for have, got, out, low in pairs:
        total = have[...] + got[...].astype(F32)
        out[...] = total
        if low is not None:
            low[...] = total.astype(BF16)


def start_kernel(par, vol, near, tables, part, own, other, wide):
    unpack(vol, wide, own)
    unpack(near, wide, other)
    along_own(par, own, other, tables.at[0], part)


def forward_kernel(
    par, far, part, own_tiles, cols, tables, w_in, b_in, w_out, out, mixed, other, wide, field
):
    unpack(far, wide, other)
    along_far(par, part, other, tables.at[0], field)
    rest_of_conv(field, tables.at[0], mixed)
    gain, scale = cols[0, :, GAIN : GAIN + 1], cols[0, :, SCALE : SCALE + 1]
    for step, first in steps():
        normal, inverse = normalise(tiles(mixed, first))
        normed = (normal * gain).astype(BF16)
        hidden = dot(w_in[0], normed) + b_in[:, 0:1]
        half = jnp.tanh(hidden * (GELU_A + GELU_B * (hidden * hidden)))
        act = (hidden * (0.5 + 0.5 * half)).astype(BF16)
        put(out, first, tiles(own_tiles, first) + scale * dot(w_out[0], act))


def save_kernel(mixed, cols, w_in, b_in, normed, normal, inverse, act, slope):
    for step, first in steps():
        value, inverse[step] = normalise(tiles(mixed, first))
        put(normal, first, value)
        low = (value * cols[0, :, GAIN : GAIN + 1]).astype(BF16)
        put(normed, first, low)
        act[step], slope[step] = gelu_parts(dot(w_in[0], low) + b_in[:, 0:1])


def middle_kernel(par, mid, near, tables, part):
    along_own(par, mid, near, tables.at[1], part)


def turn_kernel(
    par, far, part, mid, labels, cols, tables, w_in, w_in_t, b_in, w_out, w_out_t, head, head_t,
    head_b, rim_far, rim_near, along, dmixed, base, keep, send, acc_gain, acc_scale, head_cols, head_bias,
    field, mixed, sums, acc_bias,
):
    channels = mid.shape[1]
    taps = tables.at[1]
    along_far(par, part, far, taps, field)
    rest_of_conv(field, taps, mixed)
    sums[...] = jnp.zeros_like(sums)
    acc_bias[...] = jnp.zeros_like(acc_bias)
    acc_gain[...] = jnp.zeros_like(acc_gain)
    acc_scale[...] = jnp.zeros_like(acc_scale)
    head_cols[...] = jnp.zeros_like(head_cols)
    head_bias[...] = jnp.zeros_like(head_bias)
    gain, scale = cols[1, :, GAIN : GAIN + 1], cols[1, :, SCALE : SCALE + 1]
    for step, first in steps():
        normal, inverse = normalise(tiles(mixed, first))
        normed = (normal * gain).astype(BF16)
        act, slope = gelu_parts(dot(w_in[1], normed) + b_in[:, 1:2])
        lifted = dot(w_out[1], act)
        final = (tiles(mid, first).astype(F32) + scale * lifted).astype(BF16)
        logits = dot(head[...], final) + head_b[...]
        raised = jnp.exp(logits - jnp.max(logits, axis=0, keepdims=True))
        probability = raised / jnp.sum(raised, axis=0, keepdims=True)
        classes = lax.broadcasted_iota(jnp.int32, logits.shape, 0)
        g_logits = probability - (labels[step] == classes).astype(F32)
        head_bias[...] += folded(g_logits)
        g_low = g_logits.astype(BF16)
        head_cols[...] += dot_t(final, g_low)
        grad = dot(head_t[...], g_low)
        acc_scale[...] += folded(grad * lifted)
        put(base, first, grad)
        g_lift = (grad * scale).astype(BF16)
        sums[0, :channels] += dot_t(g_lift, act)
        g_hidden = dot(w_out_t[1], g_lift) * slope
        acc_bias[...] += folded(g_hidden)
        g_hid = g_hidden.astype(BF16)
        sums[1, :channels] += dot_t(normed, g_hid)
        g_norm = dot(w_in_t[1], g_hid)
        acc_gain[...] += folded(g_norm * normal)
        put(dmixed, first, normalise_back(g_norm, normal, inverse, gain))
    convolve_back(dmixed, taps, along)
    rim(par, along, taps, True, rim_far)
    rim(par, along, taps, False, rim_near)
    sums[1, channels : channels + 1] = jnp.sum(acc_bias[...].T, axis=0, keepdims=True)
    keep[...] = sums[par[0]]
    send[...] = sums[1 - par[0]]


def fill(par, own, near, far, ext):
    widen(own, ext, RADIUS * Y, OWN)
    widen(near, ext, (1 - par[0]) * 2 * RADIUS * Y, OWN)
    widen(far, ext, par[0] * 2 * RADIUS * Y, OWN)


def total_of(ref):
    return jnp.sum(ref[...], axis=1, keepdims=True)


def taps_two_kernel(
    par, own, near, far, dmixed, along, base, tables, acc_gain, acc_scale, head_cols, head_bias,
    have, got, out, inner, new, new_low, ext,
):
    taps = tables.at[1]
    mixed_sums([(have, got, new, new_low)])
    fill(par, own, near, far, ext)
    inside(along, taps, base, inner)
    tap_sums(ext, dmixed, along, taps, out)
    lane = lax.broadcasted_iota(jnp.int32, out.shape, 1)
    value = jnp.where(lane == 3 * TAPS, total_of(acc_gain), out[...])
    value = jnp.where(lane == 3 * TAPS + 1, total_of(acc_scale), value)
    value = pltpu.roll(value, 32, 1)
    for k in range(ROWS):
        value = jnp.where(lane == 64 + k, head_cols[:, k : k + 1], value)
    out[...] = value
    out[:ROWS] = jnp.where(lane[:ROWS] == 72, total_of(head_bias), out[:ROWS])


def taps_one_kernel(
    par, own, near, far, dmixed, along, tables, acc_gain, gs_scale, stats_two, out, ext
):
    fill(par, own, near, far, ext)
    tap_sums(ext, dmixed, along, tables.at[0], out)
    lane = lax.broadcasted_iota(jnp.int32, out.shape, 1)
    value = jnp.where(lane == 3 * TAPS, total_of(acc_gain), out[...])
    value = jnp.where(lane == 3 * TAPS + 1, gs_scale[...], value)
    out[...] = jnp.where(lane < 32, value, stats_two[...])


def inside_kernel(along, base, tables, inner):
    inside(along, tables.at[0], base, inner)


def point_back_kernel(
    par, inner, near, far, act, slope, normed, cols, w_in_t, w_out, w_out_t, have, got,
    base, g_norm, keep, send, gs_scale, new, new_low, sums, acc_bias,
):
    channels = inner.shape[1]
    mixed_sums([(have, got, new, new_low)])
    sums[...] = jnp.zeros_like(sums)
    acc_bias[...] = jnp.zeros_like(acc_bias)
    scale = cols[0, :, SCALE : SCALE + 1]
    for step, first in steps():
        grad = tiles(inner, first) + (tiles(near, first).astype(F32) + tiles(far, first).astype(F32))
        put(base, first, grad)
        g_lift = (grad * scale).astype(BF16)
        sums[0, :channels] += dot_t(g_lift, act[step])
        g_hidden = dot(w_out_t[0], g_lift) * slope[step]
        acc_bias[...] += folded(g_hidden)
        g_hid = g_hidden.astype(BF16)
        sums[1, :channels] += dot_t(tiles(normed, first), g_hid)
        put(g_norm, first, dot(w_in_t[0], g_hid))
    sums[1, channels : channels + 1] = jnp.sum(acc_bias[...].T, axis=0, keepdims=True)
    spread = jnp.sum(sums[0, :channels] * w_out[0].astype(F32), axis=1, keepdims=True)
    gs_scale[...] = spread / scale
    keep[...] = sums[par[0]]
    send[...] = sums[1 - par[0]]


def conv_back_kernel(
    par, g_norm, normal, inverse, cols, tables, rim_far, rim_near, along, dmixed, acc_gain
):
    taps = tables.at[0]
    acc_gain[...] = jnp.zeros_like(acc_gain)
    for step, first in steps():
        value, unit = tiles(g_norm, first), tiles(normal, first)
        acc_gain[...] += folded(value * unit)
        put(dmixed, first, normalise_back(value, unit, inverse[step], cols[0, :, GAIN : GAIN + 1]))
    convolve_back(dmixed, taps, along)
    rim(par, along, taps, True, rim_far)
    rim(par, along, taps, False, rim_near)


def sums_kernel(count, *refs):
    have, got, out, low = (refs[i * count : (i + 1) * count] for i in range(4))
    mixed_sums(zip(have, got, out, low))


def gather_kernel(have, got, value, first, second, third, out, low, total):
    mixed_sums([(have, got, out, low)])
    total[...] = (value[...] + first[...]) + (second[...] + third[...])


def last_kernel(inner, near, far, out, total):
    def add(tile, carry):
        total[tile] = inner[tile] + (near[tile].astype(F32) + far[tile].astype(F32))
        return carry

    lax.fori_loop(0, OWN, add, 0, unroll=2)

    def one(group, carry):
        rows = group_rows(group)
        for tile in range(OWN):
            out[pl.ds(group * ROWS * OWN + tile, ROWS, stride=OWN), :] = total[tile, rows, :]
        return carry

    lax.fori_loop(0, inner.shape[1] // ROWS, one, 0)


def weights_kernel(share, par, one_a, one_b, two_a, two_b, g_in_t, g_bias, g_out):
    channels = g_out.shape[1]
    for s, (mine, other) in enumerate(((one_a, one_b), (two_a, two_b))):
        even = par[0] == 0
        first = jnp.where(even, mine[...], other[...]) * share
        second = jnp.where(even, other[...], mine[...]) * share
        g_out[s] = first[:channels]
        g_in_t[s] = second[:channels]
        g_bias[s : s + 1] = second[channels : channels + 1]


def stats_kernel(share, stats, g_taps, g_gain, g_scale, g_head, g_head_b):
    rows = stats[...].T * share
    for s in range(2):
        for axis in range(3):
            first = 32 * s + axis * TAPS
            g_taps[s, axis] = rows[first : first + TAPS]
        g_gain[s : s + 1] = rows[32 * s + 21 : 32 * s + 22]
        g_scale[s : s + 1] = rows[32 * s + 22 : 32 * s + 23]
    g_head[...] = rows[64 : 64 + g_head.shape[0]]
    g_head_b[...] = rows[72:73]


def call(kernel, name, operands, outs, scratch=(), room=8, after=()):
    smem = pl.BlockSpec(memory_space=pltpu.SMEM)
    vmem = pl.BlockSpec(memory_space=pltpu.VMEM)
    anywhere = pl.BlockSpec(memory_space=pl.ANY)
    count = len(operands)

    def run(*refs):
        kernel(*refs[:count], *refs[count + len(after) :])

    in_specs = [smem if x.dtype == jnp.int32 and x.shape == (1,) else vmem for x in operands]
    return pl.pallas_call(
        run,
        name=name,
        out_shape=tuple(outs),
        in_specs=in_specs + [anywhere] * len(after),
        out_specs=tuple([vmem] * len(outs)),
        scratch_shapes=list(scratch),
        compiler_params=pltpu.CompilerParams(vmem_limit_bytes=room * MIB),
        cost_estimate=pl.CostEstimate(flops=0, bytes_accessed=0, transcendentals=0),
    )(*operands, *after)


def pinned(dims, dtype=F32):
    return pltpu.VMEM(dims, dtype)


def shape(dims, dtype=F32):
    return jax.ShapeDtypeStruct(dims, dtype)


def near_swap(value):
    count = lax.axis_size("track")
    return lax.ppermute(value, "track", [(i, i ^ 1) for i in range(count)])


def far_swap(value):
    count = lax.axis_size("track")
    pairs = []
    for i in range(1, count - 1, 2):
        pairs += [(i, i + 1), (i + 1, i)]
    return lax.ppermute(value, "track", pairs)


def bit_swap(value, step):
    count = lax.axis_size("track")
    return lax.ppermute(value, "track", [(i, i ^ step) for i in range(count)])


def exchanged(value, step):
    return value + bit_swap(value.astype(BF16), step).astype(F32)


def on_device(
    volume, labels, conv_taps, norm_gain, weight_in, bias_in, weight_out, layer_scale, head_weight, head_bias
):
    channels, planes, rows, depth = volume.shape
    hidden = weight_in.shape[1]
    classes = head_weight.shape[0]
    devices = lax.axis_size("track")
    share = 1.0 / float(devices * planes * rows * depth)
    par = (lax.axis_index("track") % 2).astype(jnp.int32).reshape(1)
    parts = OWN // CHUNK

    flat = volume.reshape(channels * OWN, depth)
    near = near_swap(flat)
    far = far_swap(flat)
    cols = jnp.swapaxes(
        jnp.concatenate(
            [conv_taps.reshape(2, 3 * TAPS, channels), norm_gain[:, None], layer_scale[:, None]], axis=1
        ), 1, 2,
    )
    b_in = bias_in.T
    head = jnp.zeros((ROWS, channels), BF16).at[:classes].set(head_weight)
    head_b = jnp.full((ROWS,), -1e30, F32).at[:classes].set(head_bias)[:, None]
    flat_labels = labels.reshape(parts, 1, CHUNK * depth)

    low = shape((OWN, channels, depth), BF16)
    full = shape((OWN, channels, depth))
    half = shape((channels + ROWS, hidden))
    half_low = shape((channels + ROWS, hidden), BF16)
    stat = shape((channels, LANES))
    s_full = pltpu.VMEM((OWN, channels, depth), F32)
    s_wide = pltpu.VMEM((channels * OWN, depth), F32)
    s_ext = pltpu.VMEM((EXT, channels, depth), F32)
    s_sums = pltpu.VMEM((2, channels + ROWS, hidden), F32)
    s_bias = pltpu.VMEM((hidden, LANES), F32)
    k_full = pinned((OWN, channels, depth))
    k_half = pinned((channels + ROWS, hidden))
    k_stat = pinned((channels, LANES))

    small = (cols, b_in, weight_in, weight_out, head, head_b, flat_labels)
    (tables, cols, b_in, w_in, w_in_t, w_out, w_out_t, head, head_t, head_b, flat_labels) = call(
        tables_kernel, "tables", small,
        [pinned((2, 4 * TAPS, channels, LANES)), pinned(cols.shape), pinned(b_in.shape),
         pinned(weight_in.shape, BF16), pinned(weight_out.shape, BF16), pinned(weight_out.shape, BF16),
         pinned(weight_in.shape, BF16), pinned(head.shape, BF16), pinned((channels, ROWS), BF16),
         pinned(head_b.shape), pinned(flat_labels.shape, jnp.int32)],
    )
    part, own_kept, near_kept = call(
        start_kernel, "start_one", (par, flat, near, tables), [k_full, k_full, k_full], [s_wide],
    )
    mid, mixed_one, far_kept = call(
        forward_kernel, "forward_one", (par, far, part, own_kept, cols, tables, w_in, b_in, w_out),
        [low, k_full, k_full], [s_wide, s_full], 16,
    )
    near = near_swap(mid)
    far = far_swap(mid)
    normed, normal, inverse, act, slope = call(
        save_kernel, "save_one", (mixed_one, cols, w_in, b_in),
        [pinned((OWN, channels, depth), BF16), k_full, pinned((parts, 1, CHUNK * depth)),
         pinned((parts, hidden, CHUNK * depth), BF16), pinned((parts, hidden, CHUNK * depth))],
        (), 16,
    )
    (part,) = call(
        middle_kernel, "start_two", (par, mid, near, tables), [k_full], (), 4, after=(inverse,)
    )
    (rim_far, rim_near, along, dmixed, base, keep, send,
     acc_gain, acc_scale, head_cols, head_lanes) = call(
        turn_kernel, "turn_two",
        (par, far, part, mid, flat_labels, cols, tables, w_in, w_in_t, b_in, w_out, w_out_t,
         head, head_t, head_b),
        [low, low, k_full, k_full, k_full, k_half, half, k_stat, k_stat, pinned((channels, ROWS)),
         pinned((ROWS, LANES))],
        [s_full, s_full, s_sums, s_bias], 24,
    )
    rim_near = near_swap(rim_near)
    rim_far = far_swap(rim_far)
    got = near_swap(send)
    stats, inner, two, two_low = call(
        taps_two_kernel, "taps_two",
        (par, mid, near, far, dmixed, along, base, tables, acc_gain, acc_scale, head_cols, head_lanes,
         keep, got),
        [k_stat, k_full, k_half, half_low], [s_ext], 8, after=(rim_near,),
    )
    got = bit_swap(two_low, 2)
    base, g_norm, keep, send, gs_scale, two, two_low = call(
        point_back_kernel, "point_back_one",
        (par, inner, rim_near, rim_far, act, slope, normed, cols, w_in_t, w_out, w_out_t, two, got),
        [k_full, k_full, k_half, half, pinned((channels, 1)), k_half, half_low], [s_sums, s_bias], 16,
    )
    got_two = bit_swap(two_low, 4)
    got_one = near_swap(send)
    rim_far, rim_near, along, dmixed, acc_gain = call(
        conv_back_kernel, "conv_back_one", (par, g_norm, normal, inverse, cols, tables),
        [low, low, k_full, k_full, k_stat], (), 12,
    )
    rim_near = near_swap(rim_near)
    rim_far = far_swap(rim_far)
    one, two, one_low, two_low = call(
        functools.partial(sums_kernel, 2), "sums_a", (keep, two, got_one, got_two),
        [k_half, k_half, half_low, half_low], (), 4, after=(rim_near,),
    )
    got_one = bit_swap(one_low, 2)
    got_two = bit_swap(two_low, 8)
    (stats,) = call(
        taps_one_kernel, "taps_one",
        (par, own_kept, near_kept, far_kept, dmixed, along, tables, acc_gain, gs_scale, stats),
        [stat], [s_ext], 8, after=(one,),
    )
    one, two, one_low, two_low = call(
        functools.partial(sums_kernel, 2), "sums_b", (one, two, got_one, got_two),
        [k_half, half, half_low, half_low], (), 4, after=(stats,),
    )
    got_one = bit_swap(one_low, 4)
    got_stats = [bit_swap(stats, step) for step in (1, 2, 3)]
    (inner,) = call(inside_kernel, "inside_one", (along, base, tables), [k_full], (), 4, after=(one,))
    one, one_low, stats = call(
        gather_kernel, "sums_c", (one, got_one, stats, *got_stats), [k_half, half_low, stat], (), 4,
        after=(inner,),
    )
    got_one = bit_swap(one_low, 8)
    got_stats = [bit_swap(stats, step) for step in (4, 8, 12)]
    (grad,) = call(
        last_kernel, "last", (inner, rim_near, rim_far), [shape((channels * OWN, depth))], [s_full], 4,
        after=(one,),
    )
    one, one_low, stats = call(
        gather_kernel, "sums_d", (one, got_one, stats, *got_stats), [half, half_low, stat], (), 4,
        after=(grad,),
    )
    step = 16
    while step < devices:
        one, two, stats = exchanged(one, step), exchanged(two, step), stats + bit_swap(stats, step)
        step *= 2
    g_taps, g_gain, g_scale, g_head, g_head_b = call(
        functools.partial(stats_kernel, share), "stats", (stats,),
        [shape((2, 3, TAPS, channels)), shape((2, channels)), shape((2, channels)),
         shape((classes, channels)), shape((1, channels))],
    )
    g_in_t, g_bias, g_out = call(
        functools.partial(weights_kernel, share), "weights",
        (par, one, near_swap(one), two, near_swap(two)),
        [shape((2, channels, hidden)), shape((2, hidden)), shape((2, channels, hidden))],
    )
    return (
        grad.reshape(volume.shape), g_taps, g_gain, jnp.swapaxes(g_in_t, 1, 2), g_bias, g_out, g_scale,
        g_head, g_head_b[0, :classes],
    )


def solution(mesh):
    placed = (
        P(None, ("groups", "track"), None, None),
        P(("groups", "track"), None, None),
        P(), P(), P(), P(), P(), P(), P(), P(),
    )
    return jax.shard_map(
        on_device,
        mesh=mesh,
        in_specs=placed,
        out_specs=(
            P(None, ("groups", "track"), None, None),
            P("groups", None, None, None),
            P("groups", None),
            P("groups", None, None),
            P("groups", None),
            P("groups", None, None),
            P("groups", None),
            P("groups", None),
            P("groups"),
        ),
        check_vma=False,
    )
```

time: 168 us -> 127 us (0.76)
  local copies, waits for them, and re-layouts: 28 us -> 7.45 us
  waiting for transfers between devices: 31.2 us -> 19.6 us
  Pallas kernels: 56.7 us -> 47 us
  starting transfers between devices: 42.3 us -> 50.8 us
  other arithmetic: 7.87 us -> 0.78 us
    ppermute x20 -> x24, waiting for transfers between devices: 31.2 us -> 19.6 us  [the longest x12 17.7 us: bit_swap(): return lax.ppermute(value, 'track', [(i, i ^ step) for i in range(count)])]
    pallas_call x7 -> x18, Pallas kernels: 56.7 us -> 47 us  [call(): pl.pallas_call(run, name=name, out_shape=tuple(outs), in_specs=in_specs +...]
    ppermute x20 -> x24, starting transfers between devices: 42.3 us -> 50.8 us  [the longest x8 32.5 us: near_swap(): return lax.ppermute(value, 'track', [(i, i ^ 1) for i in range(count)])]
    unnamed x81 -> x11, local copies, waits for them, and re-layouts: 13.7 us -> 5.4 us
    another operation x10 -> x0, local copies, waits for them, and re-layouts: 6.66 us -> none  [the longest x3 2.72 us: on_device(): layer_scale[s][:, None]]
    slice x5 -> x0, local copies, waits for them, and re-layouts: 2.84 us -> none  [the longest x1 0.8 us: tap_tables(): wide[0]]
    transpose x4 -> x0, local copies, waits for them, and re-layouts: 2.35 us -> none  [the longest x1 1.64 us: on_device(): weight_in[s]]
    add x11 -> x0, other arithmetic: 2.04 us -> none  [the longest x9 2.02 us: summed(): value + lax.ppermute(value, 'track', [(i, i ^ step) for i in range(count)])]
  transfers between devices with their start and end apart: 20 -> 24, of which waited for: 6 -> 7; matrix products, arithmetic and copies ran while one was open for 16% -> 4% of each run, Pallas kernels for 18% -> 17%
where the time goes in v2:
time: 127 us
  starting transfers between devices  50.8 us (40%)
  Pallas kernels  47 us (37%)
  waiting for transfers between devices  19.6 us (15%)
  local copies, waits for them, and re-layouts  7.45 us (6%)
    pallas_call x18, Pallas kernels, call(): pl.pallas_call(run, name=name, out_shape=tuple(outs), in_specs=in_specs +...  47 us
    ppermute x8, starting transfers between devices, near_swap(): return lax.ppermute(value, 'track', [(i, i ^ 1) for i in range(count)])  32.5 us
    ppermute x12, waiting for transfers between devices, bit_swap(): return lax.ppermute(value, 'track', [(i, i ^ step) for i in range(count)])  17.7 us
    ppermute x12, starting transfers between devices, bit_swap(): return lax.ppermute(value, 'track', [(i, i ^ step) for i in range(count)])  15.2 us
    unnamed x11, local copies, waits for them, and re-layouts  5.4 us
    ppermute x4, starting transfers between devices, far_swap(): return lax.ppermute(value, 'track', pairs)  3.15 us
  transfers between devices with their start and end apart: 24, of which 7 were waited for; matrix products, arithmetic and copies ran while one was open for 4% of the time, Pallas kernels for 17%

profile of v2, /device:TPU:0, one launch (start us, length us, event | category | flops | bytes accessed | tf_op | source)
XLA Modules:
  0.0 126.5 jit_solution(3115880886701859741)
XLA Ops:
  7.7 1.8 %tables.1 = (f32[2,28,96,128]{3,2,1,0:T(8,128)S(1)}, f32[2,96,23]{2,1,0:T(8,128)S(1)}, f32[384,2]{1,0:T(8,128)S(1)}, bf16[2,384,96]{2,1,0:T(8,128)(2,1)S(1)}, bf...) custom-call(f32[2,96,23]{2,1,0:T(8,128)S(1)} %bitcast.18, ...), custom_call_target="tpu_custom_call" | custom-call | tf_op jit(solution)/shard_map/tables/pallas_call | solution.py:552
  10.7 5.6 %forward_one.1 = (bf16[24,96,128]{2,1,0:T(8,128)(2,1)S(1)}, f32[24,96,128]{2,1,0:T(8,128)S(1)}, f32[24,96,128]{2,1,0:T(8,128)S(1)}) custom-call(s32[1]{0:T(128)} %bitcast.refs_0_, bf16[2304,128]{1,0:T(8,128)(2,1)S(1)} %collective-permute-done.refs_1_, f32[24,96,128]{2,1,0:T(8,128)S(1)} %get-tuple-element.103.refs_2_, ...), custom_call_target="tpu_custom_call" | custom-call | tf_op jit(solution)/shard_map/forward_one/pallas_call | solution.py:552
  16.4 8.6 %collective-permute-start.2 = (bf16[24,96,128]{2,1,0:T(8,128)(2,1)S(1)}, bf16[24,96,128]{2,1,0:T(8,128)(2,1)S(1)}, u32[]{:S(2)}, u32[]{:S(2)}) collective-permute-start(bf16[24,96,128]{2,1,0:T(8,128)(2,1)S(1)} %get-tuple-element.109.refs_1_.refs_3_), channel_id=1, source_target_pairs={{0,1},{1,0},{2,3},{3,2},{4,5},{5,4},{6,7},{7,6},{8,9},{9,8},{10,11... | collective-permute-start | bytes 1769480 | tf_op jit(solution)/shard_map/ppermute | solution.py:574
  25.9 3.1 %save_one.1 = (bf16[24,96,128]{2,1,0:T(8,128)(2,1)S(1)}, f32[24,96,128]{2,1,0:T(8,128)S(1)}, f32[2,1,1536]{2,1,0:T(1,128)S(1)}, bf16[2,384,1536]{2,1,0:T(8,128)(2,1)S(1)}, f32[2,384,1536]{2,1,0:T(8,128)S(1)}) custom-call(f32[24,96,128]{2,1,0:T(8,128)S(1)} %get-tuple-element.110.refs_0_, f32[2,96,23]{2,1,0:T(8,128)S(1)} %get-tuple-element.105.refs_4_.refs_1_.refs_5_.refs_7_, ...), custom_call_target="tpu_custom_call" | custom-call | tf_op jit(solution)/shard_map/save_one/pallas_call | solution.py:552
  29.6 12.4 %turn_two.1 = (bf16[24,96,128]{2,1,0:T(8,128)(2,1)S(1)}, bf16[24,96,128]{2,1,0:T(8,128)(2,1)S(1)}, f32[24,96,128]{2,1,0:T(8,128)S(1)}, f32[24,96,128]{2,1,0:T(8,...) custom-call(s32[1]{0:T(128)} %bitcast.refs_0_, ...), custom_call_target="tpu_custom_call" | custom-call | tf_op jit(solution)/shard_map/turn_two/pallas_call | solution.py:552
  42.1 12.9 %collective-permute-start.5 = (bf16[24,96,128]{2,1,0:T(8,128)(2,1)S(1)}, bf16[24,96,128]{2,1,0:T(8,128)(2,1)S(1)}, u32[]{:S(2)}, u32[]{:S(2)}) collective-permute-start(bf16[24,96,128]{2,1,0:T(8,128)(2,1)S(1)} %get-tuple-element.127), channel_id=1, source_target_pairs={{0,1},{1,0},{2,3},{3,2},{4,5},{5,4},{6,7},{7,6},{8,9},{9,8},{10,11... | collective-permute-start | bytes 1769480 | tf_op jit(solution)/shard_map/ppermute | solution.py:574
  55.8 3.8 %collective-permute-start.4 = (f32[104,384]{1,0:T(8,128)S(1)}, f32[104,384]{1,0:T(8,128)S(1)}, u32[]{:S(2)}, u32[]{:S(2)}) collective-permute-start(f32[104,384]{1,0:T(8,128)S(1)} %get-tuple-element.126), channel_id=1, source_target_pairs={{0,1},{1,0},{2,3},{3,2},{4,5},{5,4},{6,7},{7,6},{8,9},{9,8},{10,11... | collective-permute-start | bytes 479240 | tf_op jit(solution)/shard_map/ppermute | solution.py:574
  60.6 5.6 %taps_two.1 = (f32[96,128]{1,0:T(8,128)S(1)}, f32[24,96,128]{2,1,0:T(8,128)S(1)}, f32[104,384]{1,0:T(8,128)S(1)}, bf16[104,384]{1,0:T(8,128)(2,1)S(1)}) custom-call(s32[1]{0:T(128)} %bitcast.refs_0_, bf16[24,96,128]{2,1,0:T(8,128)(2,1)S(1)} %get-tuple-element.109.refs_1_.refs_3_, bf16[24,96,128]{2,1,0:T(8,128)(2,1)S(1)} %collective-permute-done.2.refs_2_, ...), custom_call_target="tpu_custom_call" | custom-call | tf_op jit(solution)/shard_map/taps_two/pallas_call | solution.py:552
  66.2 1.9 %collective-permute-start.7 = (bf16[104,384]{1,0:T(8,128)(2,1)S(1)}, bf16[104,384]{1,0:T(8,128)(2,1)S(1)}, u32[]{:S(2)}, u32[]{:S(2)}) collective-permute-start(bf16[104,384]{1,0:T(8,128)(2,1)S(1)} %get-tuple-element.134), channel_id=1, source_target_pairs={{0,2},{1,3},{2,0},{3,1},{4,6},{5,7},{6,4},{7,5},{8,10},{9,11},{10,... | collective-permute-start | bytes 239624 | tf_op jit(solution)/shard_map/ppermute | solution.py:587
  68.2 2.9 %collective-permute-done.7.refs_12_ = bf16[104,384]{1,0:T(8,128)(2,1)S(1)} collective-permute-done((bf16[104,384]{1,0:T(8,128)(2,1)S(1)}, bf16[104,384]{1,0:T(8,128)(2,1)S(1)}, u32[]{:S(2)}, u32[]{:S(2)}) %collective-permute-start.7) | collective-permute-done | bytes 79904 | tf_op jit(solution)/shard_map/ppermute | solution.py:587
  71.1 2.6 %point_back_one.1 = (f32[24,96,128]{2,1,0:T(8,128)S(1)}, f32[24,96,128]{2,1,0:T(8,128)S(1)}, f32[104,384]{1,0:T(8,128)S(1)}, f32[104,384]{1,0:T(8,128)S(1)}, f32...) custom-call(s32[1]{0:T(128)} %bitcast.refs_0_, ...), custom_call_target="tpu_custom_call" | custom-call | tf_op jit(solution)/shard_map/point_back_one/pallas_call | solution.py:552
  73.7 4.2 %conv_back_one.1 = (bf16[24,96,128]{2,1,0:T(8,128)(2,1)S(1)}, bf16[24,96,128]{2,1,0:T(8,128)(2,1)S(1)}, f32[24,96,128]{2,1,0:T(8,128)S(1)}, f32[24,96,128]{2,1,0:T(8,128)S(1)}, f32[96,128]{1,0:T(8,128)S(1)}) custom-call(s32[1]{0:T(128)} %bitcast.refs_0_, f32[24,96,128]{2,1,0:T(8,128)S(1)} %get-tuple-element.135.refs_1_, ...), custom_call_target="tpu_custom_call" | custom-call | tf_op jit(solution)/shard_map/conv_back_one/pallas_call | solution.py:552
  77.9 3.1 %collective-permute-start.10 = (bf16[24,96,128]{2,1,0:T(8,128)(2,1)S(1)}, bf16[24,96,128]{2,1,0:T(8,128)(2,1)S(1)}, u32[]{:S(2)}, u32[]{:S(2)}) collective-permute-start(bf16[24,96,128]{2,1,0:T(8,128)(2,1)S(1)} %get-tuple-element.143), channel_id=1, source_target_pairs={{0,1},{1,0},{2,3},{3,2},{4,5},{5,4},{6,7},{7,6},{8,9},{9,8},{10,11... | collective-permute-start | bytes 1769480 | tf_op jit(solution)/shard_map/ppermute | solution.py:574
  81.7 3.6 %collective-permute-start.8 = (f32[104,384]{1,0:T(8,128)S(1)}, f32[104,384]{1,0:T(8,128)S(1)}, u32[]{:S(2)}, u32[]{:S(2)}) collective-permute-start(f32[104,384]{1,0:T(8,128)S(1)} %get-tuple-element.141), channel_id=1, source_target_pairs={{0,1},{1,0},{2,3},{3,2},{4,5},{5,4},{6,7},{7,6},{8,9},{9,8},{10,11... | collective-permute-start | bytes 479240 | tf_op jit(solution)/shard_map/ppermute | solution.py:574
  85.3 1.6 %collective-permute-start.9 = (bf16[104,384]{1,0:T(8,128)(2,1)S(1)}, bf16[104,384]{1,0:T(8,128)(2,1)S(1)}, u32[]{:S(2)}, u32[]{:S(2)}) collective-permute-start(bf16[104,384]{1,0:T(8,128)(2,1)S(1)} %get-tuple-element.142), channel_id=1, source_target_pairs={{0,4},{1,5},{2,6},{3,7},{4,0},{5,1},{6,2},{7,3},{8,12},{9,13},{10,... | collective-permute-start | bytes 239624 | tf_op jit(solution)/shard_map/ppermute | solution.py:587
  86.9 8.9 %collective-permute-done.9.refs_3_ = bf16[104,384]{1,0:T(8,128)(2,1)S(1)} collective-permute-done((bf16[104,384]{1,0:T(8,128)(2,1)S(1)}, bf16[104,384]{1,0:T(8,128)(2,1)S(1)}, u32[]{:S(2)}, u32[]{:S(2)}) %collective-permute-start.9) | collective-permute-done | bytes 79904 | tf_op jit(solution)/shard_map/ppermute | solution.py:587
  95.9 2.7 %collective-permute-start.12 = (bf16[104,384]{1,0:T(8,128)(2,1)S(1)}, bf16[104,384]{1,0:T(8,128)(2,1)S(1)}, u32[]{:S(2)}, u32[]{:S(2)}) collective-permute-start(bf16[104,384]{1,0:T(8,128)(2,1)S(1)} %get-tuple-element.147), channel_id=1, source_target_pairs={{0,8},{1,9},{2,10},{3,11},{4,12},{5,13},{6,14},{7,15},{8,0},{9,1},... | collective-permute-start | bytes 239624 | tf_op jit(solution)/shard_map/ppermute | solution.py:587
  98.5 5.0 %taps_one.1.refs_4_.refs_2_ = f32[96,128]{1,0:T(8,128)S(1)} custom-call(s32[1]{0:T(128)} %bitcast.refs_0_, f32[24,96,128]{2,1,0:T(8,128)S(1)} %get-tuple-element.104.refs_3_.refs_1_, f32[24,96,128]{2,1,0:T(8,128)S(1)} %get-tuple-element.148.refs_2_, f32[24,96,128]{2,1,0:T(8,128)S(1)} %get-tuple-element.149.refs_3_, ...), custom_call_target="tpu_custom_call" | custom-call | tf_op jit(solution)/shard_map/taps_one/pallas_call | solution.py:552
  105.7 1.7 %collective-permute-start.16 = (f32[96,128]{1,0:T(8,128)S(1)}, f32[96,128]{1,0:T(8,128)S(1)}, u32[]{:S(2)}, u32[]{:S(2)}) collective-permute-start(f32[96,128]{1,0:T(8,128)S(1)} %taps_one.1.refs_4_.refs_2_), channel_id=1, source_target_pairs={{0,2},{1,3},{2,0},{3,1},{4,6},{5,7},{6,4},{7,5},{8,10},{9,11},{10,... | collective-permute-start | bytes 147464 | tf_op jit(solution)/shard_map/ppermute | solution.py:587
  108.1 2.4 %collective-permute-done.16.refs_4_ = f32[96,128]{1,0:T(8,128)S(1)} collective-permute-done((f32[96,128]{1,0:T(8,128)S(1)}, f32[96,128]{1,0:T(8,128)S(1)}, u32[]{:S(2)}, u32[]{:S(2)}) %collective-permute-start.16) | collective-permute-done | bytes 49184 | tf_op jit(solution)/shard_map/ppermute | solution.py:587
  111.8 1.5 %collective-permute-start.21 = (f32[96,128]{1,0:T(8,128)S(1)}, f32[96,128]{1,0:T(8,128)S(1)}, u32[]{:S(2)}, u32[]{:S(2)}) collective-permute-start(f32[96,128]{1,0:T(8,128)S(1)} %get-tuple-element.159.refs_2_), channel_id=1, source_target_pairs={{0,12},{1,13},{2,14},{3,15},{4,8},{5,9},{6,10},{7,11},{8,4},{9,5},... | collective-permute-start | bytes 147464 | tf_op jit(solution)/shard_map/ppermute | solution.py:587
  113.8 2.4 %collective-permute-start.19 = (f32[96,128]{1,0:T(8,128)S(1)}, f32[96,128]{1,0:T(8,128)S(1)}, u32[]{:S(2)}, u32[]{:S(2)}) collective-permute-start(f32[96,128]{1,0:T(8,128)S(1)} %get-tuple-element.159.refs_2_), channel_id=1, source_target_pairs={{0,4},{1,5},{2,6},{3,7},{4,0},{5,1},{6,2},{7,3},{8,12},{9,13},{10,... | collective-permute-start | bytes 147464 | tf_op jit(solution)/shard_map/ppermute | solution.py:587
  116.2 1.5 %last.1.refs_6_ = f32[2304,128]{1,0:T(8,128)} custom-call(f32[24,96,128]{2,1,0:T(8,128)S(1)} %inside_one.1.refs_6_.refs_0_, bf16[24,96,128]{2,1,0:T(8,128)(2,1)S(1)} %collective-permute-done.10.refs_4_.refs_1_, bf16[24,96,128]{2,1,0:T(8,128)(2,1)S(1)} %collective-permute-done.13.refs_2_, f32[104,384]{1,0:T(8,128)S(1)} %get-tuple-element.157.refs_3_.refs_0_), custom_call_target="tpu_custom_call" | custom-call | tf_op jit(solution)/shard_map/last/pallas_call | solution.py:552
  117.7 3.3 %collective-permute-done.20.refs_4_ = f32[96,128]{1,0:T(8,128)S(1)} collective-permute-done((f32[96,128]{1,0:T(8,128)S(1)}, f32[96,128]{1,0:T(8,128)S(1)}, u32[]{:S(2)}, u32[]{:S(2)}) %collective-permute-start.20) | collective-permute-done | bytes 49184 | tf_op jit(solution)/shard_map/ppermute | solution.py:587
  (59 shorter events, 22.6 us)
Async XLA Ops:
  0.7 8.9 %collective-permute-start.1 = (bf16[2304,128]{1,0:T(8,128)(2,1)}, bf16[2304,128]{1,0:T(8,128)(2,1)S(1)}, u32[]{:S(2)}, u32[]{:S(2)}) collective-permute-start(bf16[2304,128]{1,0:T(8,128)(2,1)} %bitcast.15), channel_id=1, source_target_pairs={{0,1},{1,0},{2,3},{3,2},{4,5},{5,4},{6,7},{7,6},{8,9},{9,8},{10,11... | collective-permute-start | bytes 1769480 | tf_op jit(solution)/shard_map/ppermute | solution.py:574
  1.2 9.6 %collective-permute-start = (bf16[2304,128]{1,0:T(8,128)(2,1)}, bf16[2304,128]{1,0:T(8,128)(2,1)S(1)}, u32[]{:S(2)}, u32[]{:S(2)}) collective-permute-start(bf16[2304,128]{1,0:T(8,128)(2,1)} %bitcast.16), channel_id=1, source_target_pairs={{1,2},{2,1},{3,4},{4,3},{5,6},{6,5},{7,8},{8,7},{9,10},{10,9},{11,... | collective-permute-start | bytes 1769480 | tf_op jit(solution)/shard_map/ppermute | solution.py:582
  16.4 12.6 %collective-permute-start.2 = (bf16[24,96,128]{2,1,0:T(8,128)(2,1)S(1)}, bf16[24,96,128]{2,1,0:T(8,128)(2,1)S(1)}, u32[]{:S(2)}, u32[]{:S(2)}) collective-permute-start(bf16[24,96,128]{2,1,0:T(8,128)(2,1)S(1)} %get-tuple-element.109.refs_1_.refs_3_), channel_id=1, source_target_pairs={{0,1},{1,0},{2,3},{3,2},{4,5},{5,4},{6,7},{7,6},{8,9},{9,8},{10,11... | collective-permute-start | bytes 1769480 | tf_op jit(solution)/shard_map/ppermute | solution.py:574
  25.0 4.6 %collective-permute-start.3 = (bf16[24,96,128]{2,1,0:T(8,128)(2,1)S(1)}, bf16[24,96,128]{2,1,0:T(8,128)(2,1)S(1)}, u32[]{:S(2)}, u32[]{:S(2)}) collective-permute-start(bf16[24,96,128]{2,1,0:T(8,128)(2,1)S(1)} %get-tuple-element.109.refs_1_.refs_3_), channel_id=1, source_target_pairs={{1,2},{2,1},{3,4},{4,3},{5,6},{6,5},{7,8},{8,7},{9,10},{10,9},{11,... | collective-permute-start | bytes 1769480 | tf_op jit(solution)/shard_map/ppermute | solution.py:582
  42.1 18.6 %collective-permute-start.5 = (bf16[24,96,128]{2,1,0:T(8,128)(2,1)S(1)}, bf16[24,96,128]{2,1,0:T(8,128)(2,1)S(1)}, u32[]{:S(2)}, u32[]{:S(2)}) collective-permute-start(bf16[24,96,128]{2,1,0:T(8,128)(2,1)S(1)} %get-tuple-element.127), channel_id=1, source_target_pairs={{0,1},{1,0},{2,3},{3,2},{4,5},{5,4},{6,7},{7,6},{8,9},{9,8},{10,11... | collective-permute-start | bytes 1769480 | tf_op jit(solution)/shard_map/ppermute | solution.py:574
  54.9 13.3 %collective-permute-start.6 = (bf16[24,96,128]{2,1,0:T(8,128)(2,1)S(1)}, bf16[24,96,128]{2,1,0:T(8,128)(2,1)S(1)}, u32[]{:S(2)}, u32[]{:S(2)}) collective-permute-start(bf16[24,96,128]{2,1,0:T(8,128)(2,1)S(1)} %get-tuple-element.129), channel_id=1, source_target_pairs={{1,2},{2,1},{3,4},{4,3},{5,6},{6,5},{7,8},{8,7},{9,10},{10,9},{11,... | collective-permute-start | bytes 1769480 | tf_op jit(solution)/shard_map/ppermute | solution.py:582
  55.8 4.8 %collective-permute-start.4 = (f32[104,384]{1,0:T(8,128)S(1)}, f32[104,384]{1,0:T(8,128)S(1)}, u32[]{:S(2)}, u32[]{:S(2)}) collective-permute-start(f32[104,384]{1,0:T(8,128)S(1)} %get-tuple-element.126), channel_id=1, source_target_pairs={{0,1},{1,0},{2,3},{3,2},{4,5},{5,4},{6,7},{7,6},{8,9},{9,8},{10,11... | collective-permute-start | bytes 479240 | tf_op jit(solution)/shard_map/ppermute | solution.py:574
  66.2 4.9 %collective-permute-start.7 = (bf16[104,384]{1,0:T(8,128)(2,1)S(1)}, bf16[104,384]{1,0:T(8,128)(2,1)S(1)}, u32[]{:S(2)}, u32[]{:S(2)}) collective-permute-start(bf16[104,384]{1,0:T(8,128)(2,1)S(1)} %get-tuple-element.134), channel_id=1, source_target_pairs={{0,2},{1,3},{2,0},{3,1},{4,6},{5,7},{6,4},{7,5},{8,10},{9,11},{10,... | collective-permute-start | bytes 239624 | tf_op jit(solution)/shard_map/ppermute | solution.py:587
  77.9 17.9 %collective-permute-start.10 = (bf16[24,96,128]{2,1,0:T(8,128)(2,1)S(1)}, bf16[24,96,128]{2,1,0:T(8,128)(2,1)S(1)}, u32[]{:S(2)}, u32[]{:S(2)}) collective-permute-start(bf16[24,96,128]{2,1,0:T(8,128)(2,1)S(1)} %get-tuple-element.143), channel_id=1, source_target_pairs={{0,1},{1,0},{2,3},{3,2},{4,5},{5,4},{6,7},{7,6},{8,9},{9,8},{10,11... | collective-permute-start | bytes 1769480 | tf_op jit(solution)/shard_map/ppermute | solution.py:574
  81.0 35.2 %collective-permute-start.13 = (bf16[24,96,128]{2,1,0:T(8,128)(2,1)S(1)}, bf16[24,96,128]{2,1,0:T(8,128)(2,1)S(1)}, u32[]{:S(2)}, u32[]{:S(2)}) collective-permute-start(bf16[24,96,128]{2,1,0:T(8,128)(2,1)S(1)} %get-tuple-element.155), channel_id=1, source_target_pairs={{1,2},{2,1},{3,4},{4,3},{5,6},{6,5},{7,8},{8,7},{9,10},{10,9},{11,... | collective-permute-start | bytes 1769480 | tf_op jit(solution)/shard_map/ppermute | solution.py:582
  81.7 14.0 %collective-permute-start.8 = (f32[104,384]{1,0:T(8,128)S(1)}, f32[104,384]{1,0:T(8,128)S(1)}, u32[]{:S(2)}, u32[]{:S(2)}) collective-permute-start(f32[104,384]{1,0:T(8,128)S(1)} %get-tuple-element.141), channel_id=1, source_target_pairs={{0,1},{1,0},{2,3},{3,2},{4,5},{5,4},{6,7},{7,6},{8,9},{9,8},{10,11... | collective-permute-start | bytes 479240 | tf_op jit(solution)/shard_map/ppermute | solution.py:574
  85.3 10.5 %collective-permute-start.9 = (bf16[104,384]{1,0:T(8,128)(2,1)S(1)}, bf16[104,384]{1,0:T(8,128)(2,1)S(1)}, u32[]{:S(2)}, u32[]{:S(2)}) collective-permute-start(bf16[104,384]{1,0:T(8,128)(2,1)S(1)} %get-tuple-element.142), channel_id=1, source_target_pairs={{0,4},{1,5},{2,6},{3,7},{4,0},{5,1},{6,2},{7,3},{8,12},{9,13},{10,... | collective-permute-start | bytes 239624 | tf_op jit(solution)/shard_map/ppermute | solution.py:587
  95.8 7.7 %collective-permute-start.11 = (bf16[104,384]{1,0:T(8,128)(2,1)S(1)}, bf16[104,384]{1,0:T(8,128)(2,1)S(1)}, u32[]{:S(2)}, u32[]{:S(2)}) collective-permute-start(bf16[104,384]{1,0:T(8,128)(2,1)S(1)} %get-tuple-element.146), channel_id=1, source_target_pairs={{0,2},{1,3},{2,0},{3,1},{4,6},{5,7},{6,4},{7,5},{8,10},{9,11},{10,... | collective-permute-start | bytes 239624 | tf_op jit(solution)/shard_map/ppermute | solution.py:587
  95.9 7.7 %collective-permute-start.12 = (bf16[104,384]{1,0:T(8,128)(2,1)S(1)}, bf16[104,384]{1,0:T(8,128)(2,1)S(1)}, u32[]{:S(2)}, u32[]{:S(2)}) collective-permute-start(bf16[104,384]{1,0:T(8,128)(2,1)S(1)} %get-tuple-element.147), channel_id=1, source_target_pairs={{0,8},{1,9},{2,10},{3,11},{4,12},{5,13},{6,14},{7,15},{8,0},{9,1},... | collective-permute-start | bytes 239624 | tf_op jit(solution)/shard_map/ppermute | solution.py:587
  104.2 6.2 %collective-permute-start.14 = (bf16[104,384]{1,0:T(8,128)(2,1)S(1)}, bf16[104,384]{1,0:T(8,128)(2,1)S(1)}, u32[]{:S(2)}, u32[]{:S(2)}) collective-permute-start(bf16[104,384]{1,0:T(8,128)(2,1)S(1)} %get-tuple-element.156), channel_id=1, source_target_pairs={{0,4},{1,5},{2,6},{3,7},{4,0},{5,1},{6,2},{7,3},{8,12},{9,13},{10,... | collective-permute-start | bytes 239624 | tf_op jit(solution)/shard_map/ppermute | solution.py:587
  104.6 3.5 %collective-permute-start.17 = (f32[96,128]{1,0:T(8,128)S(1)}, f32[96,128]{1,0:T(8,128)S(1)}, u32[]{:S(2)}, u32[]{:S(2)}) collective-permute-start(f32[96,128]{1,0:T(8,128)S(1)} %taps_one.1.refs_4_.refs_2_), channel_id=1, source_target_pairs={{0,3},{1,2},{2,1},{3,0},{4,7},{5,6},{6,5},{7,4},{8,11},{9,10},{10,... | collective-permute-start | bytes 147464 | tf_op jit(solution)/shard_map/ppermute | solution.py:587
  105.7 4.7 %collective-permute-start.16 = (f32[96,128]{1,0:T(8,128)S(1)}, f32[96,128]{1,0:T(8,128)S(1)}, u32[]{:S(2)}, u32[]{:S(2)}) collective-permute-start(f32[96,128]{1,0:T(8,128)S(1)} %taps_one.1.refs_4_.refs_2_), channel_id=1, source_target_pairs={{0,2},{1,3},{2,0},{3,1},{4,6},{5,7},{6,4},{7,5},{8,10},{9,11},{10,... | collective-permute-start | bytes 147464 | tf_op jit(solution)/shard_map/ppermute | solution.py:587
  107.4 3.0 %collective-permute-start.15 = (f32[96,128]{1,0:T(8,128)S(1)}, f32[96,128]{1,0:T(8,128)S(1)}, u32[]{:S(2)}, u32[]{:S(2)}) collective-permute-start(f32[96,128]{1,0:T(8,128)S(1)} %taps_one.1.refs_4_.refs_2_), channel_id=1, source_target_pairs={{0,1},{1,0},{2,3},{3,2},{4,5},{5,4},{6,7},{7,6},{8,9},{9,8},{10,11... | collective-permute-start | bytes 147464 | tf_op jit(solution)/shard_map/ppermute | solution.py:587
  110.5 10.5 %collective-permute-start.18 = (bf16[104,384]{1,0:T(8,128)(2,1)S(1)}, bf16[104,384]{1,0:T(8,128)(2,1)S(1)}, u32[]{:S(2)}, u32[]{:S(2)}) collective-permute-start(bf16[104,384]{1,0:T(8,128)(2,1)S(1)} %get-tuple-element.158), channel_id=1, source_target_pairs={{0,8},{1,9},{2,10},{3,11},{4,12},{5,13},{6,14},{7,15},{8,0},{9,1},... | collective-permute-start | bytes 239624 | tf_op jit(solution)/shard_map/ppermute | solution.py:587
  111.8 5.9 %collective-permute-start.21 = (f32[96,128]{1,0:T(8,128)S(1)}, f32[96,128]{1,0:T(8,128)S(1)}, u32[]{:S(2)}, u32[]{:S(2)}) collective-permute-start(f32[96,128]{1,0:T(8,128)S(1)} %get-tuple-element.159.refs_2_), channel_id=1, source_target_pairs={{0,12},{1,13},{2,14},{3,15},{4,8},{5,9},{6,10},{7,11},{8,4},{9,5},... | collective-permute-start | bytes 147464 | tf_op jit(solution)/shard_map/ppermute | solution.py:587
  113.3 7.7 %collective-permute-start.20 = (f32[96,128]{1,0:T(8,128)S(1)}, f32[96,128]{1,0:T(8,128)S(1)}, u32[]{:S(2)}, u32[]{:S(2)}) collective-permute-start(f32[96,128]{1,0:T(8,128)S(1)} %get-tuple-element.159.refs_2_), channel_id=1, source_target_pairs={{0,8},{1,9},{2,10},{3,11},{4,12},{5,13},{6,14},{7,15},{8,0},{9,1},... | collective-permute-start | bytes 147464 | tf_op jit(solution)/shard_map/ppermute | solution.py:587
  113.8 7.2 %collective-permute-start.19 = (f32[96,128]{1,0:T(8,128)S(1)}, f32[96,128]{1,0:T(8,128)S(1)}, u32[]{:S(2)}, u32[]{:S(2)}) collective-permute-start(f32[96,128]{1,0:T(8,128)S(1)} %get-tuple-element.159.refs_2_), channel_id=1, source_target_pairs={{0,4},{1,5},{2,6},{3,7},{4,0},{5,1},{6,2},{7,3},{8,12},{9,13},{10,... | collective-permute-start | bytes 147464 | tf_op jit(solution)/shard_map/ppermute | solution.py:587
  116.2 8.5 %collective-permute-start.23 = (f32[104,384]{1,0:T(8,128)S(1)}, f32[104,384]{1,0:T(8,128)S(1)}, u32[]{:S(2)}, u32[]{:S(2)}) collective-permute-start(f32[104,384]{1,0:T(8,128)S(1)} %get-tuple-element.164.refs_3_), channel_id=1, source_target_pairs={{0,1},{1,0},{2,3},{3,2},{4,5},{5,4},{6,7},{7,6},{8,9},{9,8},{10,11... | collective-permute-start | bytes 479240 | tf_op jit(solution)/shard_map/ppermute | solution.py:574
  124.2 1.4 %collective-permute-start.22 = (f32[104,384]{1,0:T(8,128)S(1)}, f32[104,384]{1,0:T(8,128)S(1)}, u32[]{:S(2)}, u32[]{:S(2)}) collective-permute-start(f32[104,384]{1,0:T(8,128)S(1)} %get-tuple-element.163.refs_1_), channel_id=1, source_target_pairs={{0,1},{1,0},{2,3},{3,2},{4,5},{5,4},{6,7},{7,6},{8,9},{9,8},{10,11... | collective-permute-start | bytes 479240 | tf_op jit(solution)/shard_map/ppermute | solution.py:574
  (4 other events, 11.8 us)

commit v3 on v2

--- a/solution.py
+++ b/solution.py
@@ -21,11 +21,12 @@
 CHUNK = 12
 GELU_A = 0.7978845608028654
 GELU_B = 0.044715 * GELU_A
+STAT = 32
 MIB = 1024 * 1024
 
 
 T_X, T_Y, T_Z, T_Z_BACK = 0, 7, 14, 21
-GAIN, SCALE = 21, 22
+GAIN, SCALE, HEAD_BIAS, HEAD = 21, 22, 23, 24
 
 
 def group_rows(index, size=ROWS):
@@ -45,6 +46,7 @@
 def tables_kernel(
     cols, b_in, w_in, w_out, head, head_b, labels,
     tables, cols_out, b_out, w_in_out, w_in_t, w_out_out, w_out_t, head_out, head_t, head_b_out, labels_out,
+    select,
 ):
     def one(group, carry):
         rows = group_rows(group)
@@ -59,6 +61,9 @@
         return carry
 
     lax.fori_loop(0, tables.shape[2] // ROWS, one, 0)
+    lane = lax.broadcasted_iota(jnp.int32, (LANES, LANES), 1)
+    for k in range(3 * TAPS):
+        select[k * LANES : (k + 1) * LANES] = jnp.where(lane == k, 1.0, 0.0).astype(BF16)
     for s in range(2):
         w_in_t[s] = w_in[s].T
         w_out_t[s] = w_out[s].T
@@ -152,7 +157,7 @@
     return value if shift % LANES == 0 else pltpu.roll(value, shift % LANES, 1)
 
 
-def rest_of_conv(field, cols, mixed):
+def rest_of_conv(field, cols, crossed, mixed):
     def one(group, carry):
         rows = group_rows(group)
         ty = coeffs(cols, rows, T_Y)
@@ -161,6 +166,7 @@
             plane = [field[p * Y + y, rows, :] for y in range(Y)]
             for y in range(Y):
                 value = across(plane, ty, y)
+                crossed[p * Y + y, rows, :] = value
                 mixed[p * Y + y, rows, :] = weighted(
                     [(tz[k], turned(value, RADIUS - k)) for k in range(TAPS)]
                 )
@@ -169,18 +175,29 @@
     lax.fori_loop(0, mixed.shape[1] // ROWS, one, 0)
 
 
-def convolve_back(dmixed, cols, along):
+def convolve_back(dmixed, mxy, cols, cross_out, along, sums):
+    lane = lax.broadcasted_iota(jnp.int32, (ROWS, LANES), 1)
+
     def one(group, carry):
         rows = group_rows(group)
         ty = coeffs(cols, rows, T_Y)
         tz = coeffs(cols, rows, T_Z_BACK)
+        found = [None] * TAPS
         for p in range(PLANES):
             cross = []
             for y in range(Y):
                 value = dmixed[p * Y + y, rows, :]
-                cross.append(weighted([(tz[k], turned(value, k - RADIUS)) for k in range(TAPS)]))
+                spun = [turned(value, k - RADIUS) for k in range(TAPS)]
+                field = mxy[p * Y + y, rows, :]
+                for k in range(TAPS):
+                    found[k] = weighted([(spun[k], field)], found[k])
+                cross.append(weighted([(tz[k], spun[k]) for k in range(TAPS)]))
+                cross_out[p * Y + y, rows, :] = cross[y]
             for y in range(Y):
                 along[p * Y + y, rows, :] = across_back(cross, ty, y)
+        for k in range(TAPS):
+            shift = k - RADIUS
+            sums[k, rows, :] = jnp.where((lane - shift >= 0) & (lane - shift < LANES), found[k], 0.0)
         return carry
 
     lax.fori_loop(0, dmixed.shape[1] // ROWS, one, 0)
@@ -216,48 +233,55 @@
     lax.fori_loop(0, out.shape[1] // ROWS, one, 0)
 
 
-def tap_sums(ext, dmixed, along, cols, out):
-    lane = lax.broadcasted_iota(jnp.int32, (ROWS, LANES), 1)
-
-    def one(group, carry):
+def tap_sums(par, own, near, far, mx, cross, along, z_sums, select, sums):
+    reach = range(1 - PLANES, PLANES)
+
+    def along_track(group, carry):
+        rows = group_rows(group, PAIR)
+        found = []
+        for source in (own, near, far):
+            total = dict.fromkeys(reach)
+            for y in range(Y):
+                back = [along[p * Y + y, rows, :] for p in range(PLANES)]
+                field = [source[q * Y + y, rows, :].astype(F32) for q in range(PLANES)]
+                for d in reach:
+                    total[d] = weighted(
+                        [(back[p], field[p + d]) for p in range(PLANES) if 0 <= p + d < PLANES], total[d]
+                    )
+            found.append(total)
+        mine, close, away = found
+        even = par[0] == 0
+        low = [jnp.where(even, away[d], close[d]) for d in range(PLANES)]
+        high = [jnp.where(even, close[-d], away[-d]) for d in range(PLANES)]
+        resolved = [
+            low[0], mine[-2] + low[1], mine[-1] + low[2], mine[0], mine[1] + high[2], mine[2] + high[1], high[0]
+        ]
+        for k in range(TAPS):
+            sums[T_X + k, rows, :] = resolved[k]
+        return carry
+
+    lax.fori_loop(0, mx.shape[1] // PAIR, along_track, 0)
+
+    def cross_track(group, carry):
         rows = group_rows(group)
-        tx = coeffs(cols, rows, T_X)
-        ty = coeffs(cols, rows, T_Y)
-        tz = coeffs(cols, rows, T_Z_BACK)
-        sum_x, sum_y, sum_z = ([None] * TAPS for _ in range(3))
-
-        def add(sums, k, value):
-            sums[k] = value if sums[k] is None else sums[k] + value
-
+        total = [None] * TAPS
         for p in range(PLANES):
-            plane = []
+            plane = [mx[p * Y + y, rows, :] for y in range(Y)]
             for y in range(Y):
-                column = [ext[(p + k) * Y + y, rows, :] for k in range(TAPS)]
-                plane.append(weighted([(tx[k], column[k]) for k in range(TAPS)]))
-                back = along[p * Y + y, rows, :]
-                for k in range(TAPS):
-                    add(sum_x, k, back * column[k])
-            for y in range(Y):
-                value = dmixed[p * Y + y, rows, :]
-                spun = [turned(value, k - RADIUS) for k in range(TAPS)]
-                field = across(plane, ty, y)
-                for k in range(TAPS):
-                    add(sum_z, k, spun[k] * field)
-                cross = weighted([(tz[k], spun[k]) for k in range(TAPS)])
+                back = cross[p * Y + y, rows, :]
                 for k in range(TAPS):
                     if 0 <= y + k - RADIUS < Y:
-                        add(sum_y, k, cross * plane[y + k - RADIUS])
+                        total[k] = weighted([(back, plane[y + k - RADIUS])], total[k])
         for k in range(TAPS):
-            reach = k - RADIUS
-            kept = (lane - reach >= 0) & (lane - reach < LANES)
-            sum_z[k] = jnp.where(kept, sum_z[k], 0.0)
-        total = jnp.zeros((ROWS, LANES), F32)
-        for index, value in enumerate(sum_x + sum_y + sum_z):
-            total = jnp.where(lane == index, jnp.sum(value, axis=1, keepdims=True), total)
-        out[rows, :] = total
-        return carry
-
-    lax.fori_loop(0, dmixed.shape[1] // ROWS, one, 0)
+            sums[T_Y + k, rows, :] = total[k]
+        return carry
+
+    lax.fori_loop(0, mx.shape[1] // ROWS, cross_track, 0)
+    terms = [sums[k] for k in range(2 * TAPS)] + [z_sums[k] for k in range(TAPS)]
+    wide = jnp.concatenate(terms, axis=1)
+    high = wide.astype(BF16)
+    rest = (wide - high.astype(F32)).astype(BF16)
+    return dot(high, select[...]) + dot(rest, select[...])
 
 
 def tiles(ref, first):
@@ -313,12 +337,75 @@
     return [(step, step * CHUNK) for step in range(OWN // CHUNK)]
 
 
-def mixed_sums(pairs):
-    for have, got, out, low in pairs:
-        total = have[...] + got[...].astype(F32)
-        out[...] = total
-        if low is not None:
-            low[...] = total.astype(BF16)
+def fold_stats(value):
+    lane = lax.broadcasted_iota(jnp.int32, (ROWS, LANES), 1)
+    parts, blocks = LANES // STAT, []
+    for i in range(0, value.shape[0], ROWS):
+        block = jnp.where(lane < STAT, value[i : i + ROWS], 0.0)
+        shift = i // ROWS % parts * STAT
+        blocks.append(pltpu.roll(block, shift, 1) if shift else block)
+    sums = []
+    for i in range(0, len(blocks), parts):
+        total = blocks[i]
+        for block in blocks[i + 1 : i + parts]:
+            total = total + block
+        sums.append(total)
+    return jnp.concatenate(sums, axis=1)
+
+
+def unfold_stats(folded_stats, channels):
+    parts, blocks = LANES // STAT, []
+    for i in range(channels // ROWS):
+        block = folded_stats[:, i // parts * LANES : (i // parts + 1) * LANES]
+        shift = (LANES - i % parts * STAT) % LANES
+        blocks.append(pltpu.roll(block, shift, 1) if shift else block)
+    return jnp.concatenate(blocks, axis=0)
+
+
+def send_low(low, first, total):
+    weights = total.shape[0] - ROWS
+    low[first : first + weights] = total[:weights].astype(BF16)
+    stats = total[weights:]
+    high = stats.astype(BF16).astype(F32)
+    low[first + weights : first + weights + PAIR] = jnp.concatenate([high, stats - high], axis=0).astype(BF16)
+
+
+def take_low(low, first, height):
+    weights = height - ROWS
+    terms = low[first + weights : first + weights + PAIR].astype(F32)
+    return jnp.concatenate(
+        [low[first : first + weights].astype(F32), terms[:ROWS] + terms[ROWS:]], axis=0
+    )
+
+
+def pack_kernel(have, got, stats, total, low):
+    both = jnp.concatenate([have[...] + got[...], fold_stats(stats[...])], axis=0)
+    total[...] = both
+    send_low(low, 0, both)
+
+
+def gathered(have, first, second, third):
+    height = have.shape[0]
+    return (have[...] + take_low(first, 0, height)) + (take_low(second, 0, height) + take_low(third, 0, height))
+
+
+def spread_two_kernel(have, first, second, third, total):
+    total[...] = gathered(have, first, second, third)
+
+
+def spread_one_kernel(have, first, second, third, two, total, low):
+    out = gathered(have, first, second, third)
+    height = out.shape[0]
+    total[:height] = out
+    total[height:] = two[...]
+    send_low(low, 0, out)
+    send_low(low, height + ROWS, two[...])
+
+
+def joined_kernel(have, got, total):
+    height = have.shape[0] // 2
+    total[:height] = have[:height] + take_low(got, 0, height)
+    total[height:] = have[height:] + take_low(got, height + ROWS, height)
 
 
 def start_kernel(par, vol, near, tables, part, own, other, wide):
@@ -328,11 +415,11 @@
 
 
 def forward_kernel(
-    par, far, part, own_tiles, cols, tables, w_in, b_in, w_out, out, mixed, other, wide, field
+    par, far, part, own_tiles, cols, tables, w_in, b_in, w_out, out, mixed, other, field, crossed, wide
 ):
     unpack(far, wide, other)
     along_far(par, part, other, tables.at[0], field)
-    rest_of_conv(field, tables.at[0], mixed)
+    rest_of_conv(field, tables.at[0], crossed, mixed)
     gain, scale = cols[0, :, GAIN : GAIN + 1], cols[0, :, SCALE : SCALE + 1]
     for step, first in steps():
         normal, inverse = normalise(tiles(mixed, first))
@@ -358,13 +445,13 @@
 
 def turn_kernel(
     par, far, part, mid, labels, cols, tables, w_in, w_in_t, b_in, w_out, w_out_t, head, head_t,
-    head_b, rim_far, rim_near, along, dmixed, base, keep, send, acc_gain, acc_scale, head_cols, head_bias,
-    field, mixed, sums, acc_bias,
+    head_b, rim_far, rim_near, field, z_sums, cross, along, dmixed, base, keep, send, acc_gain, acc_scale, head_cols, head_bias,
+    mixed, crossed, sums, acc_bias,
 ):
     channels = mid.shape[1]
     taps = tables.at[1]
     along_far(par, part, far, taps, field)
-    rest_of_conv(field, taps, mixed)
+    rest_of_conv(field, taps, crossed, mixed)
     sums[...] = jnp.zeros_like(sums)
     acc_bias[...] = jnp.zeros_like(acc_bias)
     acc_gain[...] = jnp.zeros_like(acc_gain)
@@ -398,7 +485,7 @@
         g_norm = dot(w_in_t[1], g_hid)
         acc_gain[...] += folded(g_norm * normal)
         put(dmixed, first, normalise_back(g_norm, normal, inverse, gain))
-    convolve_back(dmixed, taps, along)
+    convolve_back(dmixed, crossed, taps, cross, along, z_sums)
     rim(par, along, taps, True, rim_far)
     rim(par, along, taps, False, rim_near)
     sums[1, channels : channels + 1] = jnp.sum(acc_bias[...].T, axis=0, keepdims=True)
@@ -406,44 +493,32 @@
     send[...] = sums[1 - par[0]]
 
 
-def fill(par, own, near, far, ext):
-    widen(own, ext, RADIUS * Y, OWN)
-    widen(near, ext, (1 - par[0]) * 2 * RADIUS * Y, OWN)
-    widen(far, ext, par[0] * 2 * RADIUS * Y, OWN)
-
-
 def total_of(ref):
     return jnp.sum(ref[...], axis=1, keepdims=True)
 
 
 def taps_two_kernel(
-    par, own, near, far, dmixed, along, base, tables, acc_gain, acc_scale, head_cols, head_bias,
-    have, got, out, inner, new, new_low, ext,
+    par, own, near, far, mx, cross, along, z_sums, select, base, tables, acc_gain, acc_scale, head_cols,
+    head_bias, out, inner, sums,
 ):
-    taps = tables.at[1]
-    mixed_sums([(have, got, new, new_low)])
-    fill(par, own, near, far, ext)
-    inside(along, taps, base, inner)
-    tap_sums(ext, dmixed, along, taps, out)
+    inside(along, tables.at[1], base, inner)
+    value = tap_sums(par, own, near, far, mx, cross, along, z_sums, select, sums)
     lane = lax.broadcasted_iota(jnp.int32, out.shape, 1)
-    value = jnp.where(lane == 3 * TAPS, total_of(acc_gain), out[...])
-    value = jnp.where(lane == 3 * TAPS + 1, total_of(acc_scale), value)
-    value = pltpu.roll(value, 32, 1)
+    value = jnp.where(lane == GAIN, total_of(acc_gain), value)
+    value = jnp.where(lane == SCALE, total_of(acc_scale), value)
     for k in range(ROWS):
-        value = jnp.where(lane == 64 + k, head_cols[:, k : k + 1], value)
+        value = jnp.where(lane == HEAD + k, head_cols[:, k : k + 1], value)
     out[...] = value
-    out[:ROWS] = jnp.where(lane[:ROWS] == 72, total_of(head_bias), out[:ROWS])
+    out[:ROWS] = jnp.where(lane[:ROWS] == HEAD_BIAS, total_of(head_bias), out[:ROWS])
 
 
 def taps_one_kernel(
-    par, own, near, far, dmixed, along, tables, acc_gain, gs_scale, stats_two, out, ext
+    par, own, near, far, mx, cross, along, z_sums, select, acc_gain, gs_scale, out, sums
 ):
-    fill(par, own, near, far, ext)
-    tap_sums(ext, dmixed, along, tables.at[0], out)
+    value = tap_sums(par, own, near, far, mx, cross, along, z_sums, select, sums)
     lane = lax.broadcasted_iota(jnp.int32, out.shape, 1)
-    value = jnp.where(lane == 3 * TAPS, total_of(acc_gain), out[...])
-    value = jnp.where(lane == 3 * TAPS + 1, gs_scale[...], value)
-    out[...] = jnp.where(lane < 32, value, stats_two[...])
+    value = jnp.where(lane == GAIN, total_of(acc_gain), value)
+    out[...] = jnp.where(lane == SCALE, gs_scale[...], value)
 
 
 def inside_kernel(along, base, tables, inner):
@@ -451,11 +526,10 @@
 
 
 def point_back_kernel(
-    par, inner, near, far, act, slope, normed, cols, w_in_t, w_out, w_out_t, have, got,
-    base, g_norm, keep, send, gs_scale, new, new_low, sums, acc_bias,
+    par, inner, near, far, act, slope, normed, cols, w_in_t, w_out, w_out_t,
+    base, g_norm, keep, send, gs_scale, sums, acc_bias,
 ):
     channels = inner.shape[1]
-    mixed_sums([(have, got, new, new_low)])
     sums[...] = jnp.zeros_like(sums)
     acc_bias[...] = jnp.zeros_like(acc_bias)
     scale = cols[0, :, SCALE : SCALE + 1]
@@ -477,7 +551,8 @@
 
 
 def conv_back_kernel(
-    par, g_norm, normal, inverse, cols, tables, rim_far, rim_near, along, dmixed, acc_gain
+    par, g_norm, normal, inverse, mxy, cols, tables, rim_far, rim_near, z_sums, cross, along, acc_gain,
+    dmixed,
 ):
     taps = tables.at[0]
     acc_gain[...] = jnp.zeros_like(acc_gain)
@@ -485,22 +560,14 @@
         value, unit = tiles(g_norm, first), tiles(normal, first)
         acc_gain[...] += folded(value * unit)
         put(dmixed, first, normalise_back(value, unit, inverse[step], cols[0, :, GAIN : GAIN + 1]))
-    convolve_back(dmixed, taps, along)
+    convolve_back(dmixed, mxy, taps, cross, along, z_sums)
     rim(par, along, taps, True, rim_far)
     rim(par, along, taps, False, rim_near)
 
 
-def sums_kernel(count, *refs):
-    have, got, out, low = (refs[i * count : (i + 1) * count] for i in range(4))
-    mixed_sums(zip(have, got, out, low))
-
-
-def gather_kernel(have, got, value, first, second, third, out, low, total):
-    mixed_sums([(have, got, out, low)])
-    total[...] = (value[...] + first[...]) + (second[...] + third[...])
-
-
-def last_kernel(inner, near, far, out, total):
+def last_kernel(inner, near, far, out, token, total):
+    token[...] = jnp.zeros_like(token)
+
     def add(tile, carry):
         total[tile] = inner[tile] + (near[tile].astype(F32) + far[tile].astype(F32))
         return carry
@@ -516,27 +583,27 @@
     lax.fori_loop(0, inner.shape[1] // ROWS, one, 0)
 
 
-def weights_kernel(share, par, one_a, one_b, two_a, two_b, g_in_t, g_bias, g_out):
+def final_kernel(share, par, mine, other, g_in_t, g_bias, g_out, g_taps, g_gain, g_scale, g_head, g_head_b):
     channels = g_out.shape[1]
-    for s, (mine, other) in enumerate(((one_a, one_b), (two_a, two_b))):
-        even = par[0] == 0
-        first = jnp.where(even, mine[...], other[...]) * share
-        second = jnp.where(even, other[...], mine[...]) * share
+    even = par[0] == 0
+    height = mine.shape[0] // 2
+    weights = height - ROWS
+    for s in range(2):
+        here, stop = s * height, s * height + weights
+        first = jnp.where(even, mine[here:stop], other[here:stop]) * share
+        second = jnp.where(even, other[here:stop], mine[here:stop]) * share
         g_out[s] = first[:channels]
         g_in_t[s] = second[:channels]
         g_bias[s : s + 1] = second[channels : channels + 1]
-
-
-def stats_kernel(share, stats, g_taps, g_gain, g_scale, g_head, g_head_b):
-    rows = stats[...].T * share
-    for s in range(2):
+        stats = mine[stop : stop + ROWS] + other[stop : stop + ROWS]
+        rows = unfold_stats(stats, channels).T * share
         for axis in range(3):
-            first = 32 * s + axis * TAPS
-            g_taps[s, axis] = rows[first : first + TAPS]
-        g_gain[s : s + 1] = rows[32 * s + 21 : 32 * s + 22]
-        g_scale[s : s + 1] = rows[32 * s + 22 : 32 * s + 23]
-    g_head[...] = rows[64 : 64 + g_head.shape[0]]
-    g_head_b[...] = rows[72:73]
+            for k in range(TAPS):
+                g_taps[axis, k, s : s + 1] = rows[axis * TAPS + k : axis * TAPS + k + 1]
+        g_gain[s : s + 1] = rows[GAIN : GAIN + 1]
+        g_scale[s : s + 1] = rows[SCALE : SCALE + 1]
+    g_head[...] = rows[HEAD : HEAD + g_head.shape[0]]
+    g_head_b[...] = rows[HEAD_BIAS : HEAD_BIAS + 1, : g_head_b.shape[1]]
 
 
 def call(kernel, name, operands, outs, scratch=(), room=8, after=()):
@@ -587,10 +654,6 @@
     return lax.ppermute(value, "track", [(i, i ^ step) for i in range(count)])
 
 
-def exchanged(value, step):
-    return value + bit_swap(value.astype(BF16), step).astype(F32)
-
-
 def on_device(
     volume, labels, conv_taps, norm_gain, weight_in, bias_in, weight_out, layer_scale, head_weight, head_bias
 ):
@@ -617,32 +680,30 @@
 
     low = shape((OWN, channels, depth), BF16)
     full = shape((OWN, channels, depth))
-    half = shape((channels + ROWS, hidden))
-    half_low = shape((channels + ROWS, hidden), BF16)
-    stat = shape((channels, LANES))
+    half = shape((channels + PAIR, hidden))
     s_full = pltpu.VMEM((OWN, channels, depth), F32)
     s_wide = pltpu.VMEM((channels * OWN, depth), F32)
-    s_ext = pltpu.VMEM((EXT, channels, depth), F32)
-    s_sums = pltpu.VMEM((2, channels + ROWS, hidden), F32)
+    s_sums = pltpu.VMEM((2, channels + PAIR, hidden), F32)
     s_bias = pltpu.VMEM((hidden, LANES), F32)
     k_full = pinned((OWN, channels, depth))
-    k_half = pinned((channels + ROWS, hidden))
+    k_half = pinned((channels + PAIR, hidden))
     k_stat = pinned((channels, LANES))
 
     small = (cols, b_in, weight_in, weight_out, head, head_b, flat_labels)
-    (tables, cols, b_in, w_in, w_in_t, w_out, w_out_t, head, head_t, head_b, flat_labels) = call(
+    (tables, cols, b_in, w_in, w_in_t, w_out, w_out_t, head, head_t, head_b, flat_labels, select) = call(
         tables_kernel, "tables", small,
         [pinned((2, 4 * TAPS, channels, LANES)), pinned(cols.shape), pinned(b_in.shape),
          pinned(weight_in.shape, BF16), pinned(weight_out.shape, BF16), pinned(weight_out.shape, BF16),
          pinned(weight_in.shape, BF16), pinned(head.shape, BF16), pinned((channels, ROWS), BF16),
-         pinned(head_b.shape), pinned(flat_labels.shape, jnp.int32)],
+         pinned(head_b.shape), pinned(flat_labels.shape, jnp.int32),
+         pinned((3 * TAPS * LANES, LANES), BF16)],
     )
     part, own_kept, near_kept = call(
         start_kernel, "start_one", (par, flat, near, tables), [k_full, k_full, k_full], [s_wide],
     )
-    mid, mixed_one, far_kept = call(
+    mid, mixed_one, far_kept, mx_one, mxy_one = call(
         forward_kernel, "forward_one", (par, far, part, own_kept, cols, tables, w_in, b_in, w_out),
-        [low, k_full, k_full], [s_wide, s_full], 16,
+        [low, k_full, k_full, k_full, k_full], [s_wide], 16,
     )
     near = near_swap(mid)
     far = far_swap(mid)
@@ -655,87 +716,79 @@
     (part,) = call(
         middle_kernel, "start_two", (par, mid, near, tables), [k_full], (), 4, after=(inverse,)
     )
-    (rim_far, rim_near, along, dmixed, base, keep, send,
+    k_taps = pinned((TAPS, channels, LANES))
+    s_taps = pltpu.VMEM((2 * TAPS, channels, LANES), F32)
+    (rim_far, rim_near, mx, z_sums, cross, along, dmixed, base, keep, send,
      acc_gain, acc_scale, head_cols, head_lanes) = call(
         turn_kernel, "turn_two",
         (par, far, part, mid, flat_labels, cols, tables, w_in, w_in_t, b_in, w_out, w_out_t,
          head, head_t, head_b),
-        [low, low, k_full, k_full, k_full, k_half, half, k_stat, k_stat, pinned((channels, ROWS)),
+        [low, low, k_full, k_taps, k_full, k_full, k_full, k_full, k_half, half, k_stat, k_stat, pinned((channels, ROWS)),
          pinned((ROWS, LANES))],
         [s_full, s_full, s_sums, s_bias], 24,
     )
     rim_near = near_swap(rim_near)
     rim_far = far_swap(rim_far)
     got = near_swap(send)
-    stats, inner, two, two_low = call(
+    stats, inner = call(
         taps_two_kernel, "taps_two",
-        (par, mid, near, far, dmixed, along, base, tables, acc_gain, acc_scale, head_cols, head_lanes,
-         keep, got),
-        [k_stat, k_full, k_half, half_low], [s_ext], 8, after=(rim_near,),
-    )
-    got = bit_swap(two_low, 2)
-    base, g_norm, keep, send, gs_scale, two, two_low = call(
+        (par, mid, near, far, mx, cross, along, z_sums, select, base, tables, acc_gain, acc_scale, head_cols,
+         head_lanes),
+        [k_stat, k_full], [s_taps], 8, after=(rim_near,),
+    )
+    tall = shape((channels + PAIR + ROWS, hidden))
+    k_tall = pinned(tall.shape)
+    tall_low = shape((channels + 2 * PAIR, hidden), BF16)
+    two, two_low = call(
+        pack_kernel, "pack_two", (keep, got, stats), [k_tall, tall_low], (), 4, after=(inner,)
+    )
+    got = [bit_swap(two_low, step) for step in (4, 8, 12)]
+    base, g_norm, keep, send, gs_scale = call(
         point_back_kernel, "point_back_one",
-        (par, inner, rim_near, rim_far, act, slope, normed, cols, w_in_t, w_out, w_out_t, two, got),
-        [k_full, k_full, k_half, half, pinned((channels, 1)), k_half, half_low], [s_sums, s_bias], 16,
-    )
-    got_two = bit_swap(two_low, 4)
-    got_one = near_swap(send)
-    rim_far, rim_near, along, dmixed, acc_gain = call(
-        conv_back_kernel, "conv_back_one", (par, g_norm, normal, inverse, cols, tables),
-        [low, low, k_full, k_full, k_stat], (), 12,
+        (par, inner, rim_near, rim_far, act, slope, normed, cols, w_in_t, w_out, w_out_t),
+        [k_full, k_full, k_half, half, pinned((channels, 1))], [s_sums, s_bias], 16,
+    )
+    (two,) = call(spread_two_kernel, "sums_two", (two, *got), [k_tall], (), 4, after=(base,))
+    got = near_swap(send)
+    rim_far, rim_near, z_sums, cross, along, acc_gain = call(
+        conv_back_kernel, "conv_back_one", (par, g_norm, normal, inverse, mxy_one, cols, tables),
+        [low, low, k_taps, k_full, k_full, k_stat], [s_full], 12, after=(two,),
     )
     rim_near = near_swap(rim_near)
     rim_far = far_swap(rim_far)
-    one, two, one_low, two_low = call(
-        functools.partial(sums_kernel, 2), "sums_a", (keep, two, got_one, got_two),
-        [k_half, k_half, half_low, half_low], (), 4, after=(rim_near,),
-    )
-    got_one = bit_swap(one_low, 2)
-    got_two = bit_swap(two_low, 8)
     (stats,) = call(
         taps_one_kernel, "taps_one",
-        (par, own_kept, near_kept, far_kept, dmixed, along, tables, acc_gain, gs_scale, stats),
-        [stat], [s_ext], 8, after=(one,),
-    )
-    one, two, one_low, two_low = call(
-        functools.partial(sums_kernel, 2), "sums_b", (one, two, got_one, got_two),
-        [k_half, half, half_low, half_low], (), 4, after=(stats,),
-    )
-    got_one = bit_swap(one_low, 4)
-    got_stats = [bit_swap(stats, step) for step in (1, 2, 3)]
+        (par, own_kept, near_kept, far_kept, mx_one, cross, along, z_sums, select, acc_gain, gs_scale),
+        [k_stat], [s_taps], 8, after=(rim_near,),
+    )
+    one, one_low = call(pack_kernel, "pack_one", (keep, got, stats), [k_tall, tall_low], (), 4)
+    got = [bit_swap(one_low, step) for step in (4, 8, 12)]
     (inner,) = call(inside_kernel, "inside_one", (along, base, tables), [k_full], (), 4, after=(one,))
-    one, one_low, stats = call(
-        gather_kernel, "sums_c", (one, got_one, stats, *got_stats), [k_half, half_low, stat], (), 4,
-        after=(inner,),
-    )
-    got_one = bit_swap(one_low, 8)
-    got_stats = [bit_swap(stats, step) for step in (4, 8, 12)]
-    (grad,) = call(
-        last_kernel, "last", (inner, rim_near, rim_far), [shape((channels * OWN, depth))], [s_full], 4,
-        after=(one,),
-    )
-    one, one_low, stats = call(
-        gather_kernel, "sums_d", (one, got_one, stats, *got_stats), [half, half_low, stat], (), 4,
-        after=(grad,),
-    )
+    both_shape = (2 * tall.shape[0], hidden)
+    both, both_low = call(
+        spread_one_kernel, "sums_one", (one, *got, two),
+        [pinned(both_shape), shape((2 * tall_low.shape[0], hidden), BF16)], (), 4, after=(inner,),
+    )
+    got = bit_swap(both_low, 2)
+    grad, token = call(
+        last_kernel, "last", (inner, rim_near, rim_far),
+        [shape((channels * OWN, depth)), pinned((ROWS, LANES))], [s_full], 4,
+        after=(both,),
+    )
+    (both,) = call(joined_kernel, "sums_last", (both, got), [shape(both_shape)], (), 4, after=(token,))
     step = 16
     while step < devices:
-        one, two, stats = exchanged(one, step), exchanged(two, step), stats + bit_swap(stats, step)
+        both = both + bit_swap(both, step)
         step *= 2
-    g_taps, g_gain, g_scale, g_head, g_head_b = call(
-        functools.partial(stats_kernel, share), "stats", (stats,),
-        [shape((2, 3, TAPS, channels)), shape((2, channels)), shape((2, channels)),
-         shape((classes, channels)), shape((1, channels))],
-    )
-    g_in_t, g_bias, g_out = call(
-        functools.partial(weights_kernel, share), "weights",
-        (par, one, near_swap(one), two, near_swap(two)),
-        [shape((2, channels, hidden)), shape((2, hidden)), shape((2, channels, hidden))],
+    g_in_t, g_bias, g_out, g_taps, g_gain, g_scale, g_head, g_head_b = call(
+        functools.partial(final_kernel, share), "final", (par, both, near_swap(both)),
+        [shape((2, channels, hidden)), shape((2, hidden)), shape((2, channels, hidden)),
+         shape((3, TAPS, 2, channels)), shape((2, channels)), shape((2, channels)),
+         shape((classes, channels)), shape((1, classes))],
     )
     return (
-        grad.reshape(volume.shape), g_taps, g_gain, jnp.swapaxes(g_in_t, 1, 2), g_bias, g_out, g_scale,
-        g_head, g_head_b[0, :classes],
+        grad.reshape(volume.shape), jnp.moveaxis(g_taps, 2, 0), g_gain, jnp.swapaxes(g_in_t, 1, 2), g_bias, g_out, g_scale,
+        g_head, g_head_b.reshape(classes),
     )
 
 

time: 127 us -> 112 us (0.88)
  starting transfers between devices: 50.8 us -> 39.6 us
  Pallas kernels: 47 us -> 40.7 us
  waiting for transfers between devices: 19.6 us -> 25 us
  local copies, waits for them, and re-layouts: 7.45 us -> 5.05 us
    pallas_call x18, Pallas kernels: 47 us -> 40.7 us  [call(): pl.pallas_call(run, name=name, out_shape=tuple(outs), in_specs=in_specs +...]
    ppermute x12 -> x7, starting transfers between devices: 15.2 us -> 8.92 us  [bit_swap(): return lax.ppermute(value, 'track', [(i, i ^ step) for i in range(count)])]
    ppermute x12 -> x7, waiting for transfers between devices: 17.7 us -> 23.3 us  [bit_swap(): return lax.ppermute(value, 'track', [(i, i ^ step) for i in range(count)])]
    ppermute x8 -> x7, starting transfers between devices: 32.5 us -> 27.6 us  [near_swap(): return lax.ppermute(value, 'track', [(i, i ^ 1) for i in range(count)])]
    unnamed x11 -> x8, local copies, waits for them, and re-layouts: 5.4 us -> 3.51 us
  transfers between devices with their start and end apart: 24 -> 18, of which waited for: 7 -> 6; matrix products, arithmetic and copies ran while one was open for 4% -> 4% of each run, Pallas kernels for 17% -> 15%
where the time goes in v3:
time: 112 us
  Pallas kernels  40.7 us (36%)
  starting transfers between devices  39.6 us (35%)
  waiting for transfers between devices  25 us (22%)
  local copies, waits for them, and re-layouts  5.05 us (5%)
    pallas_call x18, Pallas kernels, call(): pl.pallas_call(run, name=name, out_shape=tuple(outs), in_specs=in_specs +...  40.7 us
    ppermute x7, starting transfers between devices, near_swap(): return lax.ppermute(value, 'track', [(i, i ^ 1) for i in range(count)])  27.6 us
    ppermute x7, waiting for transfers between devices, bit_swap(): return lax.ppermute(value, 'track', [(i, i ^ step) for i in range(count)])  23.3 us
    ppermute x7, starting transfers between devices, bit_swap(): return lax.ppermute(value, 'track', [(i, i ^ step) for i in range(count)])  8.92 us
    unnamed x8, local copies, waits for them, and re-layouts  3.51 us
    ppermute x4, starting transfers between devices, far_swap(): return lax.ppermute(value, 'track', pairs)  3.16 us
  transfers between devices with their start and end apart: 18, of which 6 were waited for; matrix products, arithmetic and copies ran while one was open for 4% of the time, Pallas kernels for 15%

profile of v3, /device:TPU:0, one launch (start us, length us, event | category | flops | bytes accessed | tf_op | source)
XLA Modules:
  0.0 112.1 jit_solution(4822037485232198474)
XLA Ops:
  3.5 1.1 copy.32.refs_2_
  7.7 1.9 %tables.1 = (f32[2,28,96,128]{3,2,1,0:T(8,128)S(1)}, f32[2,96,23]{2,1,0:T(8,128)S(1)}, f32[384,2]{1,0:T(8,128)S(1)}, bf16[2,384,96]{2,1,0:T(8,128)(2,1)S(1)}, bf...) custom-call(f32[2,96,23]{2,1,0:T(8,128)S(1)} %bitcast.17, ...), custom_call_target="tpu_custom_call" | custom-call | tf_op jit(solution)/shard_map/tables/pallas_call | solution.py:619
  9.6 1.2 %start_one.1 = (f32[24,96,128]{2,1,0:T(8,128)S(1)}, f32[24,96,128]{2,1,0:T(8,128)S(1)}, f32[24,96,128]{2,1,0:T(8,128)S(1)}) custom-call(s32[1]{0:T(128)} %bitcast.refs_0_, bf16[2304,128]{1,0:T(8,128)(2,1)S(1)} %bitcast.16, bf16[2304,128]{1,0:T(8,128)(2,1)S(1)} %collective-permute-done.1.refs_2_, ...), custom_call_target="tpu_custom_call" | custom-call | tf_op jit(solution)/shard_map/start_one/pallas_call | solution.py:619
  10.8 5.6 %forward_one.1 = (bf16[24,96,128]{2,1,0:T(8,128)(2,1)S(1)}, f32[24,96,128]{2,1,0:T(8,128)S(1)}, f32[24,96,128]{2,1,0:T(8,128)S(1)}, f32[24,96,128]{2,1,0:T(8,128)S(1)}, f32[24,96,128]{2,1,0:T(8,128)S(1)}) custom-call(s32[1]{0:T(128)} %bitcast.refs_0_, bf16[2304,128]{1,0:T(8,128)(2,1)S(1)} %collective-permute-done.refs_1_, ...), custom_call_target="tpu_custom_call" | custom-call | tf_op jit(solution)/shard_map/forward_one/pallas_call | solution.py:619
  16.4 8.6 %collective-permute-start.2 = (bf16[24,96,128]{2,1,0:T(8,128)(2,1)S(1)}, bf16[24,96,128]{2,1,0:T(8,128)(2,1)S(1)}, u32[]{:S(2)}, u32[]{:S(2)}) collective-permute-start(bf16[24,96,128]{2,1,0:T(8,128)(2,1)S(1)} %get-tuple-element.107.refs_1_.refs_3_), channel_id=1, source_target_pairs={{0,1},{1,0},{2,3},{3,2},{4,5},{5,4},{6,7},{7,6},{8,9},{9,8},{10,11... | collective-permute-start | bytes 1769480 | tf_op jit(solution)/shard_map/ppermute | solution.py:641
  25.9 3.1 %save_one.1 = (bf16[24,96,128]{2,1,0:T(8,128)(2,1)S(1)}, f32[24,96,128]{2,1,0:T(8,128)S(1)}, f32[2,1,1536]{2,1,0:T(1,128)S(1)}, bf16[2,384,1536]{2,1,0:T(8,128)(2,1)S(1)}, f32[2,384,1536]{2,1,0:T(8,128)S(1)}) custom-call(f32[24,96,128]{2,1,0:T(8,128)S(1)} %get-tuple-element.108.refs_0_, f32[2,96,23]{2,1,0:T(8,128)S(1)} %get-tuple-element.103.refs_4_.refs_1_.refs_5_.refs_7_, ...), custom_call_target="tpu_custom_call" | custom-call | tf_op jit(solution)/shard_map/save_one/pallas_call | solution.py:619
  29.6 13.4 %turn_two.1 = (bf16[24,96,128]{2,1,0:T(8,128)(2,1)S(1)}, bf16[24,96,128]{2,1,0:T(8,128)(2,1)S(1)}, f32[24,96,128]{2,1,0:T(8,128)S(1)}, f32[7,96,128]{2,1,0:T(8,1...) custom-call(s32[1]{0:T(128)} %bitcast.refs_0_, ...), custom_call_target="tpu_custom_call" | custom-call | tf_op jit(solution)/shard_map/turn_two/pallas_call | solution.py:619
  43.0 12.8 %collective-permute-start.4 = (bf16[24,96,128]{2,1,0:T(8,128)(2,1)S(1)}, bf16[24,96,128]{2,1,0:T(8,128)(2,1)S(1)}, u32[]{:S(2)}, u32[]{:S(2)}) collective-permute-start(bf16[24,96,128]{2,1,0:T(8,128)(2,1)S(1)} %get-tuple-element.126), channel_id=1, source_target_pairs={{0,1},{1,0},{2,3},{3,2},{4,5},{5,4},{6,7},{7,6},{8,9},{9,8},{10,11... | collective-permute-start | bytes 1769480 | tf_op jit(solution)/shard_map/ppermute | solution.py:641
  56.7 3.8 %collective-permute-start.6 = (f32[112,384]{1,0:T(8,128)S(1)}, f32[112,384]{1,0:T(8,128)S(1)}, u32[]{:S(2)}, u32[]{:S(2)}) collective-permute-start(f32[112,384]{1,0:T(8,128)S(1)} %get-tuple-element.136), channel_id=1, source_target_pairs={{0,1},{1,0},{2,3},{3,2},{4,5},{5,4},{6,7},{7,6},{8,9},{9,8},{10,11... | collective-permute-start | bytes 516104 | tf_op jit(solution)/shard_map/ppermute | solution.py:641
  60.5 2.5 %taps_two.1 = (f32[96,128]{1,0:T(8,128)S(1)}, f32[24,96,128]{2,1,0:T(8,128)S(1)}) custom-call(s32[1]{0:T(128)} %bitcast.refs_0_, bf16[24,96,128]{2,1,0:T(8,128)(2,1)S(1)} %get-tuple-element.107.refs_1_.refs_3_, bf16[24,96,128]{2,1,0:T(8,128)(2,1)S(1)} %collective-permute-done.2.refs_2_, bf16[24,96,128]{2,1,0:T(8,128)(2,1)S(1)} %collective-permute-done.3.refs_1_.refs_3_, ...), custom_call_target="tpu_custom_call" | custom-call | tf_op jit(solution)/shard_map/taps_two/pallas_call | solution.py:619
  63.1 3.6 %collective-permute-start.9 = (bf16[128,384]{1,0:T(8,128)(2,1)S(1)}, bf16[128,384]{1,0:T(8,128)(2,1)S(1)}, u32[]{:S(2)}, u32[]{:S(2)}) collective-permute-start(bf16[128,384]{1,0:T(8,128)(2,1)S(1)} %get-tuple-element.139), channel_id=1, source_target_pairs={{0,12},{1,13},{2,14},{3,15},{4,8},{5,9},{6,10},{7,11},{8,4},{9,5},... | collective-permute-start | bytes 294920 | tf_op jit(solution)/shard_map/ppermute | solution.py:654
  67.5 2.6 %point_back_one.1 = (f32[24,96,128]{2,1,0:T(8,128)S(1)}, f32[24,96,128]{2,1,0:T(8,128)S(1)}, f32[112,384]{1,0:T(8,128)S(1)}, f32[112,384]{1,0:T(8,128)S(1)}, f32[96,1]{1,0:T(8,128)S(1)}) custom-call(s32[1]{0:T(128)} %bitcast.refs_0_, f32[24,96,128]{2,1,0:T(8,128)S(1)} %get-tuple-element.127.refs_1_.refs_3_, ...), custom_call_target="tpu_custom_call" | custom-call | tf_op jit(solution)/shard_map/point_back_one/pallas_call | solution.py:619
  70.2 5.7 %collective-permute-done.9.refs_3_ = bf16[128,384]{1,0:T(8,128)(2,1)S(1)} collective-permute-done((bf16[128,384]{1,0:T(8,128)(2,1)S(1)}, bf16[128,384]{1,0:T(8,128)(2,1)S(1)}, u32[]{:S(2)}, u32[]{:S(2)}) %collective-permute-start.9) | collective-permute-done | bytes 98336 | tf_op jit(solution)/shard_map/ppermute | solution.py:654
  75.9 3.1 %collective-permute-done.8.refs_2_ = bf16[128,384]{1,0:T(8,128)(2,1)S(1)} collective-permute-done((bf16[128,384]{1,0:T(8,128)(2,1)S(1)}, bf16[128,384]{1,0:T(8,128)(2,1)S(1)}, u32[]{:S(2)}, u32[]{:S(2)}) %collective-permute-start.8) | collective-permute-done | bytes 98336 | tf_op jit(solution)/shard_map/ppermute | solution.py:654
  79.0 4.2 %conv_back_one.1 = (bf16[24,96,128]{2,1,0:T(8,128)(2,1)S(1)}, bf16[24,96,128]{2,1,0:T(8,128)(2,1)S(1)}, f32[7,96,128]{2,1,0:T(8,128)S(1)}, f32[24,96,128]{2,1,0:...) custom-call(s32[1]{0:T(128)} %bitcast.refs_0_, f32[24,96,128]{2,1,0:T(8,128)S(1)} %get-tuple-element.132.refs_1_, ...), custom_call_target="tpu_custom_call" | custom-call | tf_op jit(solution)/shard_map/conv_back_one/pallas_call | solution.py:619
  84.0 1.8 %collective-permute-start.10 = (f32[112,384]{1,0:T(8,128)S(1)}, f32[112,384]{1,0:T(8,128)S(1)}, u32[]{:S(2)}, u32[]{:S(2)}) collective-permute-start(f32[112,384]{1,0:T(8,128)S(1)} %get-tuple-element.143), channel_id=1, source_target_pairs={{0,1},{1,0},{2,3},{3,2},{4,5},{5,4},{6,7},{7,6},{8,9},{9,8},{10,11... | collective-permute-start | bytes 516104 | tf_op jit(solution)/shard_map/ppermute | solution.py:641
  85.8 2.3 %taps_one.1.refs_2_ = f32[96,128]{1,0:T(8,128)S(1)} custom-call(s32[1]{0:T(128)} %bitcast.refs_0_, f32[24,96,128]{2,1,0:T(8,128)S(1)} %get-tuple-element.102.refs_3_.refs_1_, f32[24,96,128]{2,1,0:T(8,128)S(1)} %get-tuple-element.144.refs_2_, f32[24,96,128]{2,1,0:T(8,128)S(1)} %get-tuple-element.145.refs_3_, f32[24,96,128]{2,1,0:T(8,128)S(1)} %get-tuple-element.146.refs_4_, ...), custom_call_target="tpu_custom_call" | custom-call | tf_op jit(solution)/shard_map/taps_one/pallas_call | solution.py:619
  88.2 2.5 %collective-permute-start.15 = (bf16[128,384]{1,0:T(8,128)(2,1)S(1)}, bf16[128,384]{1,0:T(8,128)(2,1)S(1)}, u32[]{:S(2)}, u32[]{:S(2)}) collective-permute-start(bf16[128,384]{1,0:T(8,128)(2,1)S(1)} %get-tuple-element.154), channel_id=1, source_target_pairs={{0,12},{1,13},{2,14},{3,15},{4,8},{5,9},{6,10},{7,11},{8,4},{9,5},... | collective-permute-start | bytes 294920 | tf_op jit(solution)/shard_map/ppermute | solution.py:654
  90.8 1.9 %collective-permute-start.13 = (bf16[128,384]{1,0:T(8,128)(2,1)S(1)}, bf16[128,384]{1,0:T(8,128)(2,1)S(1)}, u32[]{:S(2)}, u32[]{:S(2)}) collective-permute-start(bf16[128,384]{1,0:T(8,128)(2,1)S(1)} %get-tuple-element.154), channel_id=1, source_target_pairs={{0,4},{1,5},{2,6},{3,7},{4,0},{5,1},{6,2},{7,3},{8,12},{9,13},{10,... | collective-permute-start | bytes 294920 | tf_op jit(solution)/shard_map/ppermute | solution.py:654
  93.1 7.4 %collective-permute-done.15.refs_3_ = bf16[128,384]{1,0:T(8,128)(2,1)S(1)} collective-permute-done((bf16[128,384]{1,0:T(8,128)(2,1)S(1)}, bf16[128,384]{1,0:T(8,128)(2,1)S(1)}, u32[]{:S(2)}, u32[]{:S(2)}) %collective-permute-start.15) | collective-permute-done | bytes 98336 | tf_op jit(solution)/shard_map/ppermute | solution.py:654
  100.4 3.1 %collective-permute-done.14.refs_2_ = bf16[128,384]{1,0:T(8,128)(2,1)S(1)} collective-permute-done((bf16[128,384]{1,0:T(8,128)(2,1)S(1)}, bf16[128,384]{1,0:T(8,128)(2,1)S(1)}, u32[]{:S(2)}, u32[]{:S(2)}) %collective-permute-start.14) | collective-permute-done | bytes 98336 | tf_op jit(solution)/shard_map/ppermute | solution.py:654
  103.7 1.5 %last.1 = (f32[2304,128]{1,0:T(8,128)}, f32[8,128]{1,0:T(8,128)S(1)}) custom-call(f32[24,96,128]{2,1,0:T(8,128)S(1)} %inside_one.1.refs_5_.refs_0_, bf16[24,96,128]{2,1,0:T(8,128)(2,1)S(1)} %collective-permute-done.11.refs_11_.refs_1_, bf16[24,96,128]{2,1,0:T(8,128)(2,1)S(1)} %collective-permute-done.12.refs_2_, ...), custom_call_target="tpu_custom_call" | custom-call | tf_op jit(solution)/shard_map/last/pallas_call | solution.py:619
  105.2 4.1 %collective-permute-done.16.refs_1_ = bf16[256,384]{1,0:T(8,128)(2,1)S(1)} collective-permute-done((bf16[256,384]{1,0:T(8,128)(2,1)S(1)}, bf16[256,384]{1,0:T(8,128)(2,1)S(1)}, u32[]{:S(2)}, u32[]{:S(2)}) %collective-permute-start.16) | collective-permute-done | bytes 196640 | tf_op jit(solution)/shard_map/ppermute | solution.py:654
  109.4 1.7 %collective-permute-done.17.refs_2_ = f32[240,384]{1,0:T(8,128)S(1)} collective-permute-done((f32[240,384]{1,0:T(8,128)S(1)}, f32[240,384]{1,0:T(8,128)S(1)}, u32[]{:S(2)}, u32[]{:S(2)}) %collective-permute-start.17) | collective-permute-done | bytes 368672 | tf_op jit(solution)/shard_map/ppermute | solution.py:641
  (43 shorter events, 11.8 us)
Async XLA Ops:
  0.6 9.0 %copy-start = (bf16[96,3,8,128]{3,2,1,0:T(8,128)(2,1)S(1)}, bf16[96,3,8,128]{3,2,1,0:T(8,128)(2,1)}, u32[]{:S(2)}) copy-start(bf16[96,3,8,128]{3,2,1,0:T(8,128)(2,1)} %param.14) | copy-start | bytes 1769476
  0.7 8.9 %collective-permute-start.1 = (bf16[2304,128]{1,0:T(8,128)(2,1)}, bf16[2304,128]{1,0:T(8,128)(2,1)S(1)}, u32[]{:S(2)}, u32[]{:S(2)}) collective-permute-start(bf16[2304,128]{1,0:T(8,128)(2,1)} %bitcast.14), channel_id=1, source_target_pairs={{0,1},{1,0},{2,3},{3,2},{4,5},{5,4},{6,7},{7,6},{8,9},{9,8},{10,11... | collective-permute-start | bytes 1769480 | tf_op jit(solution)/shard_map/ppermute | solution.py:641
  1.2 9.6 %collective-permute-start = (bf16[2304,128]{1,0:T(8,128)(2,1)}, bf16[2304,128]{1,0:T(8,128)(2,1)S(1)}, u32[]{:S(2)}, u32[]{:S(2)}) collective-permute-start(bf16[2304,128]{1,0:T(8,128)(2,1)} %bitcast.15), channel_id=1, source_target_pairs={{1,2},{2,1},{3,4},{4,3},{5,6},{6,5},{7,8},{8,7},{9,10},{10,9},{11,... | collective-permute-start | bytes 1769480 | tf_op jit(solution)/shard_map/ppermute | solution.py:649
  6.1 0.9 copy-start.1
  7.0 0.7 copy-start.2
  16.4 12.6 %collective-permute-start.2 = (bf16[24,96,128]{2,1,0:T(8,128)(2,1)S(1)}, bf16[24,96,128]{2,1,0:T(8,128)(2,1)S(1)}, u32[]{:S(2)}, u32[]{:S(2)}) collective-permute-start(bf16[24,96,128]{2,1,0:T(8,128)(2,1)S(1)} %get-tuple-element.107.refs_1_.refs_3_), channel_id=1, source_target_pairs={{0,1},{1,0},{2,3},{3,2},{4,5},{5,4},{6,7},{7,6},{8,9},{9,8},{10,11... | collective-permute-start | bytes 1769480 | tf_op jit(solution)/shard_map/ppermute | solution.py:641
  25.0 4.6 %collective-permute-start.3 = (bf16[24,96,128]{2,1,0:T(8,128)(2,1)S(1)}, bf16[24,96,128]{2,1,0:T(8,128)(2,1)S(1)}, u32[]{:S(2)}, u32[]{:S(2)}) collective-permute-start(bf16[24,96,128]{2,1,0:T(8,128)(2,1)S(1)} %get-tuple-element.107.refs_1_.refs_3_), channel_id=1, source_target_pairs={{1,2},{2,1},{3,4},{4,3},{5,6},{6,5},{7,8},{8,7},{9,10},{10,9},{11,... | collective-permute-start | bytes 1769480 | tf_op jit(solution)/shard_map/ppermute | solution.py:649
  43.0 17.5 %collective-permute-start.4 = (bf16[24,96,128]{2,1,0:T(8,128)(2,1)S(1)}, bf16[24,96,128]{2,1,0:T(8,128)(2,1)S(1)}, u32[]{:S(2)}, u32[]{:S(2)}) collective-permute-start(bf16[24,96,128]{2,1,0:T(8,128)(2,1)S(1)} %get-tuple-element.126), channel_id=1, source_target_pairs={{0,1},{1,0},{2,3},{3,2},{4,5},{5,4},{6,7},{7,6},{8,9},{9,8},{10,11... | collective-permute-start | bytes 1769480 | tf_op jit(solution)/shard_map/ppermute | solution.py:641
  55.8 11.7 %collective-permute-start.5 = (bf16[24,96,128]{2,1,0:T(8,128)(2,1)S(1)}, bf16[24,96,128]{2,1,0:T(8,128)(2,1)S(1)}, u32[]{:S(2)}, u32[]{:S(2)}) collective-permute-start(bf16[24,96,128]{2,1,0:T(8,128)(2,1)S(1)} %get-tuple-element.128), channel_id=1, source_target_pairs={{1,2},{2,1},{3,4},{4,3},{5,6},{6,5},{7,8},{8,7},{9,10},{10,9},{11,... | collective-permute-start | bytes 1769480 | tf_op jit(solution)/shard_map/ppermute | solution.py:649
  56.7 6.3 %collective-permute-start.6 = (f32[112,384]{1,0:T(8,128)S(1)}, f32[112,384]{1,0:T(8,128)S(1)}, u32[]{:S(2)}, u32[]{:S(2)}) collective-permute-start(f32[112,384]{1,0:T(8,128)S(1)} %get-tuple-element.136), channel_id=1, source_target_pairs={{0,1},{1,0},{2,3},{3,2},{4,5},{5,4},{6,7},{7,6},{8,9},{9,8},{10,11... | collective-permute-start | bytes 516104 | tf_op jit(solution)/shard_map/ppermute | solution.py:641
  63.1 12.8 %collective-permute-start.9 = (bf16[128,384]{1,0:T(8,128)(2,1)S(1)}, bf16[128,384]{1,0:T(8,128)(2,1)S(1)}, u32[]{:S(2)}, u32[]{:S(2)}) collective-permute-start(bf16[128,384]{1,0:T(8,128)(2,1)S(1)} %get-tuple-element.139), channel_id=1, source_target_pairs={{0,12},{1,13},{2,14},{3,15},{4,8},{5,9},{6,10},{7,11},{8,4},{9,5},... | collective-permute-start | bytes 294920 | tf_op jit(solution)/shard_map/ppermute | solution.py:654
  66.7 12.3 %collective-permute-start.8 = (bf16[128,384]{1,0:T(8,128)(2,1)S(1)}, bf16[128,384]{1,0:T(8,128)(2,1)S(1)}, u32[]{:S(2)}, u32[]{:S(2)}) collective-permute-start(bf16[128,384]{1,0:T(8,128)(2,1)S(1)} %get-tuple-element.139), channel_id=1, source_target_pairs={{0,8},{1,9},{2,10},{3,11},{4,12},{5,13},{6,14},{7,15},{8,0},{9,1},... | collective-permute-start | bytes 294920 | tf_op jit(solution)/shard_map/ppermute | solution.py:654
  66.7 12.3 %collective-permute-start.7 = (bf16[128,384]{1,0:T(8,128)(2,1)S(1)}, bf16[128,384]{1,0:T(8,128)(2,1)S(1)}, u32[]{:S(2)}, u32[]{:S(2)}) collective-permute-start(bf16[128,384]{1,0:T(8,128)(2,1)S(1)} %get-tuple-element.139), channel_id=1, source_target_pairs={{0,4},{1,5},{2,6},{3,7},{4,0},{5,1},{6,2},{7,3},{8,12},{9,13},{10,... | collective-permute-start | bytes 294920 | tf_op jit(solution)/shard_map/ppermute | solution.py:654
  83.2 2.6 %collective-permute-start.11 = (bf16[24,96,128]{2,1,0:T(8,128)(2,1)S(1)}, bf16[24,96,128]{2,1,0:T(8,128)(2,1)S(1)}, u32[]{:S(2)}, u32[]{:S(2)}) collective-permute-start(bf16[24,96,128]{2,1,0:T(8,128)(2,1)S(1)} %get-tuple-element.151), channel_id=1, source_target_pairs={{0,1},{1,0},{2,3},{3,2},{4,5},{5,4},{6,7},{7,6},{8,9},{9,8},{10,11... | collective-permute-start | bytes 1769480 | tf_op jit(solution)/shard_map/ppermute | solution.py:641
  83.3 20.3 %collective-permute-start.12 = (bf16[24,96,128]{2,1,0:T(8,128)(2,1)S(1)}, bf16[24,96,128]{2,1,0:T(8,128)(2,1)S(1)}, u32[]{:S(2)}, u32[]{:S(2)}) collective-permute-start(bf16[24,96,128]{2,1,0:T(8,128)(2,1)S(1)} %get-tuple-element.153), channel_id=1, source_target_pairs={{1,2},{2,1},{3,4},{4,3},{5,6},{6,5},{7,8},{8,7},{9,10},{10,9},{11,... | collective-permute-start | bytes 1769480 | tf_op jit(solution)/shard_map/ppermute | solution.py:649
  84.0 4.1 %collective-permute-start.10 = (f32[112,384]{1,0:T(8,128)S(1)}, f32[112,384]{1,0:T(8,128)S(1)}, u32[]{:S(2)}, u32[]{:S(2)}) collective-permute-start(f32[112,384]{1,0:T(8,128)S(1)} %get-tuple-element.143), channel_id=1, source_target_pairs={{0,1},{1,0},{2,3},{3,2},{4,5},{5,4},{6,7},{7,6},{8,9},{9,8},{10,11... | collective-permute-start | bytes 516104 | tf_op jit(solution)/shard_map/ppermute | solution.py:641
  88.2 12.2 %collective-permute-start.15 = (bf16[128,384]{1,0:T(8,128)(2,1)S(1)}, bf16[128,384]{1,0:T(8,128)(2,1)S(1)}, u32[]{:S(2)}, u32[]{:S(2)}) collective-permute-start(bf16[128,384]{1,0:T(8,128)(2,1)S(1)} %get-tuple-element.154), channel_id=1, source_target_pairs={{0,12},{1,13},{2,14},{3,15},{4,8},{5,9},{6,10},{7,11},{8,4},{9,5},... | collective-permute-start | bytes 294920 | tf_op jit(solution)/shard_map/ppermute | solution.py:654
  90.8 12.7 %collective-permute-start.14 = (bf16[128,384]{1,0:T(8,128)(2,1)S(1)}, bf16[128,384]{1,0:T(8,128)(2,1)S(1)}, u32[]{:S(2)}, u32[]{:S(2)}) collective-permute-start(bf16[128,384]{1,0:T(8,128)(2,1)S(1)} %get-tuple-element.154), channel_id=1, source_target_pairs={{0,8},{1,9},{2,10},{3,11},{4,12},{5,13},{6,14},{7,15},{8,0},{9,1},... | collective-permute-start | bytes 294920 | tf_op jit(solution)/shard_map/ppermute | solution.py:654
  90.8 12.7 %collective-permute-start.13 = (bf16[128,384]{1,0:T(8,128)(2,1)S(1)}, bf16[128,384]{1,0:T(8,128)(2,1)S(1)}, u32[]{:S(2)}, u32[]{:S(2)}) collective-permute-start(bf16[128,384]{1,0:T(8,128)(2,1)S(1)} %get-tuple-element.154), channel_id=1, source_target_pairs={{0,4},{1,5},{2,6},{3,7},{4,0},{5,1},{6,2},{7,3},{8,12},{9,13},{10,... | collective-permute-start | bytes 294920 | tf_op jit(solution)/shard_map/ppermute | solution.py:654
  103.6 5.7 %collective-permute-start.16 = (bf16[256,384]{1,0:T(8,128)(2,1)S(1)}, bf16[256,384]{1,0:T(8,128)(2,1)S(1)}, u32[]{:S(2)}, u32[]{:S(2)}) collective-permute-start(bf16[256,384]{1,0:T(8,128)(2,1)S(1)} %get-tuple-element.157), channel_id=1, source_target_pairs={{0,2},{1,3},{2,0},{3,1},{4,6},{5,7},{6,4},{7,5},{8,10},{9,11},{10,... | collective-permute-start | bytes 589832 | tf_op jit(solution)/shard_map/ppermute | solution.py:654
  109.4 1.8 %collective-permute-start.17 = (f32[240,384]{1,0:T(8,128)S(1)}, f32[240,384]{1,0:T(8,128)S(1)}, u32[]{:S(2)}, u32[]{:S(2)}) collective-permute-start(f32[240,384]{1,0:T(8,128)S(1)} %sums_last.1.refs_1_), channel_id=1, source_target_pairs={{0,1},{1,0},{2,3},{3,2},{4,5},{5,4},{6,7},{7,6},{8,9},{9,8},{10,11... | collective-permute-start | bytes 1105928 | tf_op jit(solution)/shard_map/ppermute | solution.py:641

commit v4 on v3

--- a/solution.py
+++ b/solution.py
@@ -153,13 +153,18 @@
     return weighted([(ty[k], field[y - k + RADIUS]) for k in range(TAPS) if 0 <= y - k + RADIUS < Y])
 
 
-def turned(value, shift):
-    return value if shift % LANES == 0 else pltpu.roll(value, shift % LANES, 1)
+def turns(value, sign):
+    low = value.astype(BF16)
+    moved = []
+    for k in range(TAPS):
+        shift = sign * (k - RADIUS) % LANES
+        moved.append(pltpu.roll(low, shift, 1).astype(F32) if shift else value)
+    return moved
 
 
 def rest_of_conv(field, cols, crossed, mixed):
     def one(group, carry):
-        rows = group_rows(group)
+        rows = group_rows(group, PAIR)
         ty = coeffs(cols, rows, T_Y)
         tz = coeffs(cols, rows, T_Z)
         for p in range(PLANES):
@@ -167,31 +172,28 @@
             for y in range(Y):
                 value = across(plane, ty, y)
                 crossed[p * Y + y, rows, :] = value
-                mixed[p * Y + y, rows, :] = weighted(
-                    [(tz[k], turned(value, RADIUS - k)) for k in range(TAPS)]
-                )
-        return carry
-
-    lax.fori_loop(0, mixed.shape[1] // ROWS, one, 0)
+                mixed[p * Y + y, rows, :] = weighted(zip(tz, turns(value, -1)))
+        return carry
+
+    lax.fori_loop(0, mixed.shape[1] // PAIR, one, 0)
 
 
 def convolve_back(dmixed, mxy, cols, cross_out, along, sums):
-    lane = lax.broadcasted_iota(jnp.int32, (ROWS, LANES), 1)
+    lane = lax.broadcasted_iota(jnp.int32, (PAIR, LANES), 1)
 
     def one(group, carry):
-        rows = group_rows(group)
+        rows = group_rows(group, PAIR)
         ty = coeffs(cols, rows, T_Y)
         tz = coeffs(cols, rows, T_Z_BACK)
         found = [None] * TAPS
         for p in range(PLANES):
             cross = []
             for y in range(Y):
-                value = dmixed[p * Y + y, rows, :]
-                spun = [turned(value, k - RADIUS) for k in range(TAPS)]
+                spun = turns(dmixed[p * Y + y, rows, :], 1)
                 field = mxy[p * Y + y, rows, :]
                 for k in range(TAPS):
                     found[k] = weighted([(spun[k], field)], found[k])
-                cross.append(weighted([(tz[k], spun[k]) for k in range(TAPS)]))
+                cross.append(weighted(zip(tz, spun)))
                 cross_out[p * Y + y, rows, :] = cross[y]
             for y in range(Y):
                 along[p * Y + y, rows, :] = across_back(cross, ty, y)
@@ -200,7 +202,7 @@
             sums[k, rows, :] = jnp.where((lane - shift >= 0) & (lane - shift < LANES), found[k], 0.0)
         return carry
 
-    lax.fori_loop(0, dmixed.shape[1] // ROWS, one, 0)
+    lax.fori_loop(0, dmixed.shape[1] // PAIR, one, 0)
 
 
 def rim(par, along, cols, far, out):
@@ -703,7 +705,7 @@
     )
     mid, mixed_one, far_kept, mx_one, mxy_one = call(
         forward_kernel, "forward_one", (par, far, part, own_kept, cols, tables, w_in, b_in, w_out),
-        [low, k_full, k_full, k_full, k_full], [s_wide], 16,
+        [low, k_full, k_full, k_full, k_full], [s_wide], 8,
     )
     near = near_swap(mid)
     far = far_swap(mid)
@@ -746,13 +748,13 @@
     base, g_norm, keep, send, gs_scale = call(
         point_back_kernel, "point_back_one",
         (par, inner, rim_near, rim_far, act, slope, normed, cols, w_in_t, w_out, w_out_t),
-        [k_full, k_full, k_half, half, pinned((channels, 1))], [s_sums, s_bias], 16,
+        [k_full, k_full, k_half, half, pinned((channels, 1))], [s_sums, s_bias], 8,
     )
     (two,) = call(spread_two_kernel, "sums_two", (two, *got), [k_tall], (), 4, after=(base,))
     got = near_swap(send)
     rim_far, rim_near, z_sums, cross, along, acc_gain = call(
         conv_back_kernel, "conv_back_one", (par, g_norm, normal, inverse, mxy_one, cols, tables),
-        [low, low, k_taps, k_full, k_full, k_stat], [s_full], 12, after=(two,),
+        [low, low, k_taps, k_full, k_full, k_stat], [s_full], 8, after=(two,),
     )
     rim_near = near_swap(rim_near)
     rim_far = far_swap(rim_far)

time: 112 us -> 108 us (0.964)
  Pallas kernels: 40.7 us -> 36.6 us
    pallas_call x18, Pallas kernels: 40.7 us -> 36.6 us  [call(): pl.pallas_call(run, name=name, out_shape=tuple(outs), in_specs=in_specs +...]
where the time goes in v4:
time: 108 us
  starting transfers between devices  39.7 us (37%)
  Pallas kernels  36.6 us (34%)
  waiting for transfers between devices  25.1 us (23%)
  local copies, waits for them, and re-layouts  5.05 us (5%)
    pallas_call x18, Pallas kernels, call(): pl.pallas_call(run, name=name, out_shape=tuple(outs), in_specs=in_specs +...  36.6 us
    ppermute x7, starting transfers between devices, near_swap(): return lax.ppermute(value, 'track', [(i, i ^ 1) for i in range(count)])  27.6 us
    ppermute x7, waiting for transfers between devices, bit_swap(): return lax.ppermute(value, 'track', [(i, i ^ step) for i in range(count)])  23.4 us
    ppermute x7, starting transfers between devices, bit_swap(): return lax.ppermute(value, 'track', [(i, i ^ step) for i in range(count)])  8.92 us
    unnamed x8, local copies, waits for them, and re-layouts  3.51 us
    ppermute x4, starting transfers between devices, far_swap(): return lax.ppermute(value, 'track', pairs)  3.16 us
  transfers between devices with their start and end apart: 18, of which 6 were waited for; matrix products, arithmetic and copies ran while one was open for 4% of the time, Pallas kernels for 15%

profile of v4, /device:TPU:0, one launch (start us, length us, event | category | flops | bytes accessed | tf_op | source)
XLA Modules:
  0.0 108.0 jit_solution(17277665131353341426)
XLA Ops:
  3.5 1.1 copy.32.refs_2_
  7.7 1.9 %tables.1 = (f32[2,28,96,128]{3,2,1,0:T(8,128)S(1)}, f32[2,96,23]{2,1,0:T(8,128)S(1)}, f32[384,2]{1,0:T(8,128)S(1)}, bf16[2,384,96]{2,1,0:T(8,128)(2,1)S(1)}, bf...) custom-call(f32[2,96,23]{2,1,0:T(8,128)S(1)} %bitcast.17, ...), custom_call_target="tpu_custom_call" | custom-call | tf_op jit(solution)/shard_map/tables/pallas_call | solution.py:621
  9.6 1.2 %start_one.1 = (f32[24,96,128]{2,1,0:T(8,128)S(1)}, f32[24,96,128]{2,1,0:T(8,128)S(1)}, f32[24,96,128]{2,1,0:T(8,128)S(1)}) custom-call(s32[1]{0:T(128)} %bitcast.refs_0_, bf16[2304,128]{1,0:T(8,128)(2,1)S(1)} %bitcast.16, bf16[2304,128]{1,0:T(8,128)(2,1)S(1)} %collective-permute-done.1.refs_2_, ...), custom_call_target="tpu_custom_call" | custom-call | tf_op jit(solution)/shard_map/start_one/pallas_call | solution.py:621
  10.8 4.3 %forward_one.1 = (bf16[24,96,128]{2,1,0:T(8,128)(2,1)S(1)}, f32[24,96,128]{2,1,0:T(8,128)S(1)}, f32[24,96,128]{2,1,0:T(8,128)S(1)}, f32[24,96,128]{2,1,0:T(8,128)S(1)}, f32[24,96,128]{2,1,0:T(8,128)S(1)}) custom-call(s32[1]{0:T(128)} %bitcast.refs_0_, bf16[2304,128]{1,0:T(8,128)(2,1)S(1)} %collective-permute-done.refs_1_, ...), custom_call_target="tpu_custom_call" | custom-call | tf_op jit(solution)/shard_map/forward_one/pallas_call | solution.py:621
  15.1 8.6 %collective-permute-start.2 = (bf16[24,96,128]{2,1,0:T(8,128)(2,1)S(1)}, bf16[24,96,128]{2,1,0:T(8,128)(2,1)S(1)}, u32[]{:S(2)}, u32[]{:S(2)}) collective-permute-start(bf16[24,96,128]{2,1,0:T(8,128)(2,1)S(1)} %get-tuple-element.107.refs_1_.refs_3_), channel_id=1, source_target_pairs={{0,1},{1,0},{2,3},{3,2},{4,5},{5,4},{6,7},{7,6},{8,9},{9,8},{10,11... | collective-permute-start | bytes 1769480 | tf_op jit(solution)/shard_map/ppermute | solution.py:643
  24.5 3.1 %save_one.1 = (bf16[24,96,128]{2,1,0:T(8,128)(2,1)S(1)}, f32[24,96,128]{2,1,0:T(8,128)S(1)}, f32[2,1,1536]{2,1,0:T(1,128)S(1)}, bf16[2,384,1536]{2,1,0:T(8,128)(2,1)S(1)}, f32[2,384,1536]{2,1,0:T(8,128)S(1)}) custom-call(f32[24,96,128]{2,1,0:T(8,128)S(1)} %get-tuple-element.108.refs_0_, f32[2,96,23]{2,1,0:T(8,128)S(1)} %get-tuple-element.103.refs_4_.refs_1_.refs_5_.refs_7_, ...), custom_call_target="tpu_custom_call" | custom-call | tf_op jit(solution)/shard_map/save_one/pallas_call | solution.py:621
  28.2 11.4 %turn_two.1 = (bf16[24,96,128]{2,1,0:T(8,128)(2,1)S(1)}, bf16[24,96,128]{2,1,0:T(8,128)(2,1)S(1)}, f32[24,96,128]{2,1,0:T(8,128)S(1)}, f32[7,96,128]{2,1,0:T(8,1...) custom-call(s32[1]{0:T(128)} %bitcast.refs_0_, ...), custom_call_target="tpu_custom_call" | custom-call | tf_op jit(solution)/shard_map/turn_two/pallas_call | solution.py:621
  39.6 12.8 %collective-permute-start.4 = (bf16[24,96,128]{2,1,0:T(8,128)(2,1)S(1)}, bf16[24,96,128]{2,1,0:T(8,128)(2,1)S(1)}, u32[]{:S(2)}, u32[]{:S(2)}) collective-permute-start(bf16[24,96,128]{2,1,0:T(8,128)(2,1)S(1)} %get-tuple-element.126), channel_id=1, source_target_pairs={{0,1},{1,0},{2,3},{3,2},{4,5},{5,4},{6,7},{7,6},{8,9},{9,8},{10,11... | collective-permute-start | bytes 1769480 | tf_op jit(solution)/shard_map/ppermute | solution.py:643
  53.3 3.8 %collective-permute-start.6 = (f32[112,384]{1,0:T(8,128)S(1)}, f32[112,384]{1,0:T(8,128)S(1)}, u32[]{:S(2)}, u32[]{:S(2)}) collective-permute-start(f32[112,384]{1,0:T(8,128)S(1)} %get-tuple-element.136), channel_id=1, source_target_pairs={{0,1},{1,0},{2,3},{3,2},{4,5},{5,4},{6,7},{7,6},{8,9},{9,8},{10,11... | collective-permute-start | bytes 516104 | tf_op jit(solution)/shard_map/ppermute | solution.py:643
  57.1 2.5 %taps_two.1 = (f32[96,128]{1,0:T(8,128)S(1)}, f32[24,96,128]{2,1,0:T(8,128)S(1)}) custom-call(s32[1]{0:T(128)} %bitcast.refs_0_, bf16[24,96,128]{2,1,0:T(8,128)(2,1)S(1)} %get-tuple-element.107.refs_1_.refs_3_, bf16[24,96,128]{2,1,0:T(8,128)(2,1)S(1)} %collective-permute-done.2.refs_2_, bf16[24,96,128]{2,1,0:T(8,128)(2,1)S(1)} %collective-permute-done.3.refs_1_.refs_3_, ...), custom_call_target="tpu_custom_call" | custom-call | tf_op jit(solution)/shard_map/taps_two/pallas_call | solution.py:621
  59.7 3.6 %collective-permute-start.9 = (bf16[128,384]{1,0:T(8,128)(2,1)S(1)}, bf16[128,384]{1,0:T(8,128)(2,1)S(1)}, u32[]{:S(2)}, u32[]{:S(2)}) collective-permute-start(bf16[128,384]{1,0:T(8,128)(2,1)S(1)} %get-tuple-element.139), channel_id=1, source_target_pairs={{0,12},{1,13},{2,14},{3,15},{4,8},{5,9},{6,10},{7,11},{8,4},{9,5},... | collective-permute-start | bytes 294920 | tf_op jit(solution)/shard_map/ppermute | solution.py:656
  64.2 2.6 %point_back_one.1 = (f32[24,96,128]{2,1,0:T(8,128)S(1)}, f32[24,96,128]{2,1,0:T(8,128)S(1)}, f32[112,384]{1,0:T(8,128)S(1)}, f32[112,384]{1,0:T(8,128)S(1)}, f32[96,1]{1,0:T(8,128)S(1)}) custom-call(s32[1]{0:T(128)} %bitcast.refs_0_, f32[24,96,128]{2,1,0:T(8,128)S(1)} %get-tuple-element.127.refs_1_.refs_3_, ...), custom_call_target="tpu_custom_call" | custom-call | tf_op jit(solution)/shard_map/point_back_one/pallas_call | solution.py:621
  66.8 5.7 %collective-permute-done.9.refs_3_ = bf16[128,384]{1,0:T(8,128)(2,1)S(1)} collective-permute-done((bf16[128,384]{1,0:T(8,128)(2,1)S(1)}, bf16[128,384]{1,0:T(8,128)(2,1)S(1)}, u32[]{:S(2)}, u32[]{:S(2)}) %collective-permute-start.9) | collective-permute-done | bytes 98336 | tf_op jit(solution)/shard_map/ppermute | solution.py:656
  72.5 3.1 %collective-permute-done.8.refs_2_ = bf16[128,384]{1,0:T(8,128)(2,1)S(1)} collective-permute-done((bf16[128,384]{1,0:T(8,128)(2,1)S(1)}, bf16[128,384]{1,0:T(8,128)(2,1)S(1)}, u32[]{:S(2)}, u32[]{:S(2)}) %collective-permute-start.8) | collective-permute-done | bytes 98336 | tf_op jit(solution)/shard_map/ppermute | solution.py:656
  75.7 3.6 %conv_back_one.1 = (bf16[24,96,128]{2,1,0:T(8,128)(2,1)S(1)}, bf16[24,96,128]{2,1,0:T(8,128)(2,1)S(1)}, f32[7,96,128]{2,1,0:T(8,128)S(1)}, f32[24,96,128]{2,1,0:...) custom-call(s32[1]{0:T(128)} %bitcast.refs_0_, f32[24,96,128]{2,1,0:T(8,128)S(1)} %get-tuple-element.132.refs_1_, ...), custom_call_target="tpu_custom_call" | custom-call | tf_op jit(solution)/shard_map/conv_back_one/pallas_call | solution.py:621
  80.0 1.8 %collective-permute-start.10 = (f32[112,384]{1,0:T(8,128)S(1)}, f32[112,384]{1,0:T(8,128)S(1)}, u32[]{:S(2)}, u32[]{:S(2)}) collective-permute-start(f32[112,384]{1,0:T(8,128)S(1)} %get-tuple-element.143), channel_id=1, source_target_pairs={{0,1},{1,0},{2,3},{3,2},{4,5},{5,4},{6,7},{7,6},{8,9},{9,8},{10,11... | collective-permute-start | bytes 516104 | tf_op jit(solution)/shard_map/ppermute | solution.py:643
  81.8 2.3 %taps_one.1.refs_2_ = f32[96,128]{1,0:T(8,128)S(1)} custom-call(s32[1]{0:T(128)} %bitcast.refs_0_, f32[24,96,128]{2,1,0:T(8,128)S(1)} %get-tuple-element.102.refs_3_.refs_1_, f32[24,96,128]{2,1,0:T(8,128)S(1)} %get-tuple-element.144.refs_2_, f32[24,96,128]{2,1,0:T(8,128)S(1)} %get-tuple-element.145.refs_3_, f32[24,96,128]{2,1,0:T(8,128)S(1)} %get-tuple-element.146.refs_4_, ...), custom_call_target="tpu_custom_call" | custom-call | tf_op jit(solution)/shard_map/taps_one/pallas_call | solution.py:621
  84.2 2.5 %collective-permute-start.15 = (bf16[128,384]{1,0:T(8,128)(2,1)S(1)}, bf16[128,384]{1,0:T(8,128)(2,1)S(1)}, u32[]{:S(2)}, u32[]{:S(2)}) collective-permute-start(bf16[128,384]{1,0:T(8,128)(2,1)S(1)} %get-tuple-element.154), channel_id=1, source_target_pairs={{0,12},{1,13},{2,14},{3,15},{4,8},{5,9},{6,10},{7,11},{8,4},{9,5},... | collective-permute-start | bytes 294920 | tf_op jit(solution)/shard_map/ppermute | solution.py:656
  86.7 1.9 %collective-permute-start.13 = (bf16[128,384]{1,0:T(8,128)(2,1)S(1)}, bf16[128,384]{1,0:T(8,128)(2,1)S(1)}, u32[]{:S(2)}, u32[]{:S(2)}) collective-permute-start(bf16[128,384]{1,0:T(8,128)(2,1)S(1)} %get-tuple-element.154), channel_id=1, source_target_pairs={{0,4},{1,5},{2,6},{3,7},{4,0},{5,1},{6,2},{7,3},{8,12},{9,13},{10,... | collective-permute-start | bytes 294920 | tf_op jit(solution)/shard_map/ppermute | solution.py:656
  89.0 7.3 %collective-permute-done.15.refs_3_ = bf16[128,384]{1,0:T(8,128)(2,1)S(1)} collective-permute-done((bf16[128,384]{1,0:T(8,128)(2,1)S(1)}, bf16[128,384]{1,0:T(8,128)(2,1)S(1)}, u32[]{:S(2)}, u32[]{:S(2)}) %collective-permute-start.15) | collective-permute-done | bytes 98336 | tf_op jit(solution)/shard_map/ppermute | solution.py:656
  96.4 3.1 %collective-permute-done.14.refs_2_ = bf16[128,384]{1,0:T(8,128)(2,1)S(1)} collective-permute-done((bf16[128,384]{1,0:T(8,128)(2,1)S(1)}, bf16[128,384]{1,0:T(8,128)(2,1)S(1)}, u32[]{:S(2)}, u32[]{:S(2)}) %collective-permute-start.14) | collective-permute-done | bytes 98336 | tf_op jit(solution)/shard_map/ppermute | solution.py:656
  99.6 1.5 %last.1 = (f32[2304,128]{1,0:T(8,128)}, f32[8,128]{1,0:T(8,128)S(1)}) custom-call(f32[24,96,128]{2,1,0:T(8,128)S(1)} %inside_one.1.refs_5_.refs_0_, bf16[24,96,128]{2,1,0:T(8,128)(2,1)S(1)} %collective-permute-done.11.refs_11_.refs_1_, bf16[24,96,128]{2,1,0:T(8,128)(2,1)S(1)} %collective-permute-done.12.refs_2_, ...), custom_call_target="tpu_custom_call" | custom-call | tf_op jit(solution)/shard_map/last/pallas_call | solution.py:621
  101.2 4.1 %collective-permute-done.16.refs_1_ = bf16[256,384]{1,0:T(8,128)(2,1)S(1)} collective-permute-done((bf16[256,384]{1,0:T(8,128)(2,1)S(1)}, bf16[256,384]{1,0:T(8,128)(2,1)S(1)}, u32[]{:S(2)}, u32[]{:S(2)}) %collective-permute-start.16) | collective-permute-done | bytes 196640 | tf_op jit(solution)/shard_map/ppermute | solution.py:656
  105.4 1.7 %collective-permute-done.17.refs_2_ = f32[240,384]{1,0:T(8,128)S(1)} collective-permute-done((f32[240,384]{1,0:T(8,128)S(1)}, f32[240,384]{1,0:T(8,128)S(1)}, u32[]{:S(2)}, u32[]{:S(2)}) %collective-permute-start.17) | collective-permute-done | bytes 368672 | tf_op jit(solution)/shard_map/ppermute | solution.py:643
  (43 shorter events, 11.8 us)
Async XLA Ops:
  0.6 9.0 %copy-start = (bf16[96,3,8,128]{3,2,1,0:T(8,128)(2,1)S(1)}, bf16[96,3,8,128]{3,2,1,0:T(8,128)(2,1)}, u32[]{:S(2)}) copy-start(bf16[96,3,8,128]{3,2,1,0:T(8,128)(2,1)} %param.14) | copy-start | bytes 1769476
  0.7 8.9 %collective-permute-start.1 = (bf16[2304,128]{1,0:T(8,128)(2,1)}, bf16[2304,128]{1,0:T(8,128)(2,1)S(1)}, u32[]{:S(2)}, u32[]{:S(2)}) collective-permute-start(bf16[2304,128]{1,0:T(8,128)(2,1)} %bitcast.14), channel_id=1, source_target_pairs={{0,1},{1,0},{2,3},{3,2},{4,5},{5,4},{6,7},{7,6},{8,9},{9,8},{10,11... | collective-permute-start | bytes 1769480 | tf_op jit(solution)/shard_map/ppermute | solution.py:643
  1.2 9.6 %collective-permute-start = (bf16[2304,128]{1,0:T(8,128)(2,1)}, bf16[2304,128]{1,0:T(8,128)(2,1)S(1)}, u32[]{:S(2)}, u32[]{:S(2)}) collective-permute-start(bf16[2304,128]{1,0:T(8,128)(2,1)} %bitcast.15), channel_id=1, source_target_pairs={{1,2},{2,1},{3,4},{4,3},{5,6},{6,5},{7,8},{8,7},{9,10},{10,9},{11,... | collective-permute-start | bytes 1769480 | tf_op jit(solution)/shard_map/ppermute | solution.py:651
  6.1 0.9 copy-start.1
  7.0 0.7 copy-start.2
  15.1 12.6 %collective-permute-start.2 = (bf16[24,96,128]{2,1,0:T(8,128)(2,1)S(1)}, bf16[24,96,128]{2,1,0:T(8,128)(2,1)S(1)}, u32[]{:S(2)}, u32[]{:S(2)}) collective-permute-start(bf16[24,96,128]{2,1,0:T(8,128)(2,1)S(1)} %get-tuple-element.107.refs_1_.refs_3_), channel_id=1, source_target_pairs={{0,1},{1,0},{2,3},{3,2},{4,5},{5,4},{6,7},{7,6},{8,9},{9,8},{10,11... | collective-permute-start | bytes 1769480 | tf_op jit(solution)/shard_map/ppermute | solution.py:643
  23.6 4.6 %collective-permute-start.3 = (bf16[24,96,128]{2,1,0:T(8,128)(2,1)S(1)}, bf16[24,96,128]{2,1,0:T(8,128)(2,1)S(1)}, u32[]{:S(2)}, u32[]{:S(2)}) collective-permute-start(bf16[24,96,128]{2,1,0:T(8,128)(2,1)S(1)} %get-tuple-element.107.refs_1_.refs_3_), channel_id=1, source_target_pairs={{1,2},{2,1},{3,4},{4,3},{5,6},{6,5},{7,8},{8,7},{9,10},{10,9},{11,... | collective-permute-start | bytes 1769480 | tf_op jit(solution)/shard_map/ppermute | solution.py:651
  39.6 17.5 %collective-permute-start.4 = (bf16[24,96,128]{2,1,0:T(8,128)(2,1)S(1)}, bf16[24,96,128]{2,1,0:T(8,128)(2,1)S(1)}, u32[]{:S(2)}, u32[]{:S(2)}) collective-permute-start(bf16[24,96,128]{2,1,0:T(8,128)(2,1)S(1)} %get-tuple-element.126), channel_id=1, source_target_pairs={{0,1},{1,0},{2,3},{3,2},{4,5},{5,4},{6,7},{7,6},{8,9},{9,8},{10,11... | collective-permute-start | bytes 1769480 | tf_op jit(solution)/shard_map/ppermute | solution.py:643
  52.4 11.7 %collective-permute-start.5 = (bf16[24,96,128]{2,1,0:T(8,128)(2,1)S(1)}, bf16[24,96,128]{2,1,0:T(8,128)(2,1)S(1)}, u32[]{:S(2)}, u32[]{:S(2)}) collective-permute-start(bf16[24,96,128]{2,1,0:T(8,128)(2,1)S(1)} %get-tuple-element.128), channel_id=1, source_target_pairs={{1,2},{2,1},{3,4},{4,3},{5,6},{6,5},{7,8},{8,7},{9,10},{10,9},{11,... | collective-permute-start | bytes 1769480 | tf_op jit(solution)/shard_map/ppermute | solution.py:651
  53.3 6.3 %collective-permute-start.6 = (f32[112,384]{1,0:T(8,128)S(1)}, f32[112,384]{1,0:T(8,128)S(1)}, u32[]{:S(2)}, u32[]{:S(2)}) collective-permute-start(f32[112,384]{1,0:T(8,128)S(1)} %get-tuple-element.136), channel_id=1, source_target_pairs={{0,1},{1,0},{2,3},{3,2},{4,5},{5,4},{6,7},{7,6},{8,9},{9,8},{10,11... | collective-permute-start | bytes 516104 | tf_op jit(solution)/shard_map/ppermute | solution.py:643
  59.7 12.8 %collective-permute-start.9 = (bf16[128,384]{1,0:T(8,128)(2,1)S(1)}, bf16[128,384]{1,0:T(8,128)(2,1)S(1)}, u32[]{:S(2)}, u32[]{:S(2)}) collective-permute-start(bf16[128,384]{1,0:T(8,128)(2,1)S(1)} %get-tuple-element.139), channel_id=1, source_target_pairs={{0,12},{1,13},{2,14},{3,15},{4,8},{5,9},{6,10},{7,11},{8,4},{9,5},... | collective-permute-start | bytes 294920 | tf_op jit(solution)/shard_map/ppermute | solution.py:656
  63.3 12.3 %collective-permute-start.8 = (bf16[128,384]{1,0:T(8,128)(2,1)S(1)}, bf16[128,384]{1,0:T(8,128)(2,1)S(1)}, u32[]{:S(2)}, u32[]{:S(2)}) collective-permute-start(bf16[128,384]{1,0:T(8,128)(2,1)S(1)} %get-tuple-element.139), channel_id=1, source_target_pairs={{0,8},{1,9},{2,10},{3,11},{4,12},{5,13},{6,14},{7,15},{8,0},{9,1},... | collective-permute-start | bytes 294920 | tf_op jit(solution)/shard_map/ppermute | solution.py:656
  63.3 12.3 %collective-permute-start.7 = (bf16[128,384]{1,0:T(8,128)(2,1)S(1)}, bf16[128,384]{1,0:T(8,128)(2,1)S(1)}, u32[]{:S(2)}, u32[]{:S(2)}) collective-permute-start(bf16[128,384]{1,0:T(8,128)(2,1)S(1)} %get-tuple-element.139), channel_id=1, source_target_pairs={{0,4},{1,5},{2,6},{3,7},{4,0},{5,1},{6,2},{7,3},{8,12},{9,13},{10,... | collective-permute-start | bytes 294920 | tf_op jit(solution)/shard_map/ppermute | solution.py:656
  79.2 2.6 %collective-permute-start.11 = (bf16[24,96,128]{2,1,0:T(8,128)(2,1)S(1)}, bf16[24,96,128]{2,1,0:T(8,128)(2,1)S(1)}, u32[]{:S(2)}, u32[]{:S(2)}) collective-permute-start(bf16[24,96,128]{2,1,0:T(8,128)(2,1)S(1)} %get-tuple-element.151), channel_id=1, source_target_pairs={{0,1},{1,0},{2,3},{3,2},{4,5},{5,4},{6,7},{7,6},{8,9},{9,8},{10,11... | collective-permute-start | bytes 1769480 | tf_op jit(solution)/shard_map/ppermute | solution.py:643
  79.3 20.3 %collective-permute-start.12 = (bf16[24,96,128]{2,1,0:T(8,128)(2,1)S(1)}, bf16[24,96,128]{2,1,0:T(8,128)(2,1)S(1)}, u32[]{:S(2)}, u32[]{:S(2)}) collective-permute-start(bf16[24,96,128]{2,1,0:T(8,128)(2,1)S(1)} %get-tuple-element.153), channel_id=1, source_target_pairs={{1,2},{2,1},{3,4},{4,3},{5,6},{6,5},{7,8},{8,7},{9,10},{10,9},{11,... | collective-permute-start | bytes 1769480 | tf_op jit(solution)/shard_map/ppermute | solution.py:651
  80.0 4.1 %collective-permute-start.10 = (f32[112,384]{1,0:T(8,128)S(1)}, f32[112,384]{1,0:T(8,128)S(1)}, u32[]{:S(2)}, u32[]{:S(2)}) collective-permute-start(f32[112,384]{1,0:T(8,128)S(1)} %get-tuple-element.143), channel_id=1, source_target_pairs={{0,1},{1,0},{2,3},{3,2},{4,5},{5,4},{6,7},{7,6},{8,9},{9,8},{10,11... | collective-permute-start | bytes 516104 | tf_op jit(solution)/shard_map/ppermute | solution.py:643
  84.2 12.1 %collective-permute-start.15 = (bf16[128,384]{1,0:T(8,128)(2,1)S(1)}, bf16[128,384]{1,0:T(8,128)(2,1)S(1)}, u32[]{:S(2)}, u32[]{:S(2)}) collective-permute-start(bf16[128,384]{1,0:T(8,128)(2,1)S(1)} %get-tuple-element.154), channel_id=1, source_target_pairs={{0,12},{1,13},{2,14},{3,15},{4,8},{5,9},{6,10},{7,11},{8,4},{9,5},... | collective-permute-start | bytes 294920 | tf_op jit(solution)/shard_map/ppermute | solution.py:656
  86.7 12.7 %collective-permute-start.14 = (bf16[128,384]{1,0:T(8,128)(2,1)S(1)}, bf16[128,384]{1,0:T(8,128)(2,1)S(1)}, u32[]{:S(2)}, u32[]{:S(2)}) collective-permute-start(bf16[128,384]{1,0:T(8,128)(2,1)S(1)} %get-tuple-element.154), channel_id=1, source_target_pairs={{0,8},{1,9},{2,10},{3,11},{4,12},{5,13},{6,14},{7,15},{8,0},{9,1},... | collective-permute-start | bytes 294920 | tf_op jit(solution)/shard_map/ppermute | solution.py:656
  86.7 12.7 %collective-permute-start.13 = (bf16[128,384]{1,0:T(8,128)(2,1)S(1)}, bf16[128,384]{1,0:T(8,128)(2,1)S(1)}, u32[]{:S(2)}, u32[]{:S(2)}) collective-permute-start(bf16[128,384]{1,0:T(8,128)(2,1)S(1)} %get-tuple-element.154), channel_id=1, source_target_pairs={{0,4},{1,5},{2,6},{3,7},{4,0},{5,1},{6,2},{7,3},{8,12},{9,13},{10,... | collective-permute-start | bytes 294920 | tf_op jit(solution)/shard_map/ppermute | solution.py:656
  99.5 5.7 %collective-permute-start.16 = (bf16[256,384]{1,0:T(8,128)(2,1)S(1)}, bf16[256,384]{1,0:T(8,128)(2,1)S(1)}, u32[]{:S(2)}, u32[]{:S(2)}) collective-permute-start(bf16[256,384]{1,0:T(8,128)(2,1)S(1)} %get-tuple-element.157), channel_id=1, source_target_pairs={{0,2},{1,3},{2,0},{3,1},{4,6},{5,7},{6,4},{7,5},{8,10},{9,11},{10,... | collective-permute-start | bytes 589832 | tf_op jit(solution)/shard_map/ppermute | solution.py:656
  105.3 1.8 %collective-permute-start.17 = (f32[240,384]{1,0:T(8,128)S(1)}, f32[240,384]{1,0:T(8,128)S(1)}, u32[]{:S(2)}, u32[]{:S(2)}) collective-permute-start(f32[240,384]{1,0:T(8,128)S(1)} %sums_last.1.refs_1_), channel_id=1, source_target_pairs={{0,1},{1,0},{2,3},{3,2},{4,5},{5,4},{6,7},{7,6},{8,9},{9,8},{10,11... | collective-permute-start | bytes 1105928 | tf_op jit(solution)/shard_map/ppermute | solution.py:643

commit v5 on v4

--- a/solution.py
+++ b/solution.py
@@ -326,6 +326,11 @@
     return lax.dot_general(a, b, (((1,), (1,)), ((), ())), preferred_element_type=F32)
 
 
+def with_ones(normed):
+    row = lax.broadcasted_iota(jnp.int32, (PAIR, normed.shape[1]), 0)
+    return jnp.concatenate([normed, jnp.where(row == 0, 1.0, 0.0).astype(BF16)], axis=0)
+
+
 def gelu_parts(hidden):
     square = hidden * hidden
     half = jnp.tanh(hidden * (GELU_A + GELU_B * square))
@@ -391,12 +396,31 @@
     return (have[...] + take_low(first, 0, height)) + (take_low(second, 0, height) + take_low(third, 0, height))
 
 
+def first_kernel(have, got, total, low):
+    out = have[...] + got[...]
+    total[...] = out
+    low[...] = out.astype(BF16)
+
+
 def spread_two_kernel(have, first, second, third, total):
     total[...] = gathered(have, first, second, third)
 
 
-def spread_one_kernel(have, first, second, third, two, total, low):
-    out = gathered(have, first, second, third)
+def spread_kernel(have, first, second, third, total):
+    total[...] = (have[...] + first[...].astype(F32)) + (second[...].astype(F32) + third[...].astype(F32))
+
+
+def stats_pack_kernel(stats, total, low):
+    out = fold_stats(stats[...])
+    high = out.astype(BF16).astype(F32)
+    total[...] = out
+    low[...] = jnp.concatenate([high, out - high], axis=0).astype(BF16)
+
+
+def spread_one_kernel(one, stats, first, second, third, two, total, low):
+    terms = [ref[...].astype(F32) for ref in (first, second, third)]
+    first, second, third = (term[:ROWS] + term[ROWS:] for term in terms)
+    out = jnp.concatenate([one[...], (stats[...] + first) + (second + third)], axis=0)
     height = out.shape[0]
     total[:height] = out
     total[height:] = two[...]
@@ -447,15 +471,14 @@
 
 def turn_kernel(
     par, far, part, mid, labels, cols, tables, w_in, w_in_t, b_in, w_out, w_out_t, head, head_t,
-    head_b, rim_far, rim_near, field, z_sums, cross, along, dmixed, base, keep, send, acc_gain, acc_scale, head_cols, head_bias,
-    mixed, crossed, sums, acc_bias,
+    head_b, rim_far, field, z_sums, cross, along, dmixed, base, keep, send, acc_gain, acc_scale, head_cols, head_bias,
+    mixed, crossed, sums,
 ):
     channels = mid.shape[1]
     taps = tables.at[1]
     along_far(par, part, far, taps, field)
     rest_of_conv(field, taps, crossed, mixed)
     sums[...] = jnp.zeros_like(sums)
-    acc_bias[...] = jnp.zeros_like(acc_bias)
     acc_gain[...] = jnp.zeros_like(acc_gain)
     acc_scale[...] = jnp.zeros_like(acc_scale)
     head_cols[...] = jnp.zeros_like(head_cols)
@@ -480,17 +503,13 @@
         put(base, first, grad)
         g_lift = (grad * scale).astype(BF16)
         sums[0, :channels] += dot_t(g_lift, act)
-        g_hidden = dot(w_out_t[1], g_lift) * slope
-        acc_bias[...] += folded(g_hidden)
-        g_hid = g_hidden.astype(BF16)
-        sums[1, :channels] += dot_t(normed, g_hid)
+        g_hid = (dot(w_out_t[1], g_lift) * slope).astype(BF16)
+        sums[1] += dot_t(with_ones(normed), g_hid)
         g_norm = dot(w_in_t[1], g_hid)
         acc_gain[...] += folded(g_norm * normal)
         put(dmixed, first, normalise_back(g_norm, normal, inverse, gain))
     convolve_back(dmixed, crossed, taps, cross, along, z_sums)
     rim(par, along, taps, True, rim_far)
-    rim(par, along, taps, False, rim_near)
-    sums[1, channels : channels + 1] = jnp.sum(acc_bias[...].T, axis=0, keepdims=True)
     keep[...] = sums[par[0]]
     send[...] = sums[1 - par[0]]
 
@@ -501,8 +520,9 @@
 
 def taps_two_kernel(
     par, own, near, far, mx, cross, along, z_sums, select, base, tables, acc_gain, acc_scale, head_cols,
-    head_bias, out, inner, sums,
+    head_bias, out, inner, rim_near, sums,
 ):
+    rim(par, along, tables.at[1], False, rim_near)
     inside(along, tables.at[1], base, inner)
     value = tap_sums(par, own, near, far, mx, cross, along, z_sums, select, sums)
     lane = lax.broadcasted_iota(jnp.int32, out.shape, 1)
@@ -523,29 +543,26 @@
     out[...] = jnp.where(lane == SCALE, gs_scale[...], value)
 
 
-def inside_kernel(along, base, tables, inner):
+def inside_kernel(par, along, base, tables, inner, rim_near):
+    rim(par, along, tables.at[0], False, rim_near)
     inside(along, tables.at[0], base, inner)
 
 
 def point_back_kernel(
     par, inner, near, far, act, slope, normed, cols, w_in_t, w_out, w_out_t,
-    base, g_norm, keep, send, gs_scale, sums, acc_bias,
+    base, g_norm, keep, send, gs_scale, sums,
 ):
     channels = inner.shape[1]
     sums[...] = jnp.zeros_like(sums)
-    acc_bias[...] = jnp.zeros_like(acc_bias)
     scale = cols[0, :, SCALE : SCALE + 1]
     for step, first in steps():
         grad = tiles(inner, first) + (tiles(near, first).astype(F32) + tiles(far, first).astype(F32))
         put(base, first, grad)
         g_lift = (grad * scale).astype(BF16)
         sums[0, :channels] += dot_t(g_lift, act[step])
-        g_hidden = dot(w_out_t[0], g_lift) * slope[step]
-        acc_bias[...] += folded(g_hidden)
-        g_hid = g_hidden.astype(BF16)
-        sums[1, :channels] += dot_t(tiles(normed, first), g_hid)
+        g_hid = (dot(w_out_t[0], g_lift) * slope[step]).astype(BF16)
+        sums[1] += dot_t(with_ones(tiles(normed, first)), g_hid)
         put(g_norm, first, dot(w_in_t[0], g_hid))
-    sums[1, channels : channels + 1] = jnp.sum(acc_bias[...].T, axis=0, keepdims=True)
     spread = jnp.sum(sums[0, :channels] * w_out[0].astype(F32), axis=1, keepdims=True)
     gs_scale[...] = spread / scale
     keep[...] = sums[par[0]]
@@ -553,7 +570,7 @@
 
 
 def conv_back_kernel(
-    par, g_norm, normal, inverse, mxy, cols, tables, rim_far, rim_near, z_sums, cross, along, acc_gain,
+    par, g_norm, normal, inverse, mxy, cols, tables, rim_far, z_sums, cross, along, acc_gain,
     dmixed,
 ):
     taps = tables.at[0]
@@ -564,7 +581,6 @@
         put(dmixed, first, normalise_back(value, unit, inverse[step], cols[0, :, GAIN : GAIN + 1]))
     convolve_back(dmixed, mxy, taps, cross, along, z_sums)
     rim(par, along, taps, True, rim_far)
-    rim(par, along, taps, False, rim_near)
 
 
 def last_kernel(inner, near, far, out, token, total):
@@ -608,7 +624,7 @@
     g_head_b[...] = rows[HEAD_BIAS : HEAD_BIAS + 1, : g_head_b.shape[1]]
 
 
-def call(kernel, name, operands, outs, scratch=(), room=8, after=()):
+def call(kernel, name, operands, outs, scratch=(), room=8, after=(), flops=0):
     smem = pl.BlockSpec(memory_space=pltpu.SMEM)
     vmem = pl.BlockSpec(memory_space=pltpu.VMEM)
     anywhere = pl.BlockSpec(memory_space=pl.ANY)
@@ -626,7 +642,7 @@
         out_specs=tuple([vmem] * len(outs)),
         scratch_shapes=list(scratch),
         compiler_params=pltpu.CompilerParams(vmem_limit_bytes=room * MIB),
-        cost_estimate=pl.CostEstimate(flops=0, bytes_accessed=0, transcendentals=0),
+        cost_estimate=pl.CostEstimate(flops=flops, bytes_accessed=0, transcendentals=0),
     )(*operands, *after)
 
 
@@ -686,7 +702,6 @@
     s_full = pltpu.VMEM((OWN, channels, depth), F32)
     s_wide = pltpu.VMEM((channels * OWN, depth), F32)
     s_sums = pltpu.VMEM((2, channels + PAIR, hidden), F32)
-    s_bias = pltpu.VMEM((hidden, LANES), F32)
     k_full = pinned((OWN, channels, depth))
     k_half = pinned((channels + PAIR, hidden))
     k_stat = pinned((channels, LANES))
@@ -720,24 +735,24 @@
     )
     k_taps = pinned((TAPS, channels, LANES))
     s_taps = pltpu.VMEM((2 * TAPS, channels, LANES), F32)
-    (rim_far, rim_near, mx, z_sums, cross, along, dmixed, base, keep, send,
+    (rim_far, mx, z_sums, cross, along, dmixed, base, keep, send,
      acc_gain, acc_scale, head_cols, head_lanes) = call(
         turn_kernel, "turn_two",
         (par, far, part, mid, flat_labels, cols, tables, w_in, w_in_t, b_in, w_out, w_out_t,
          head, head_t, head_b),
-        [low, low, k_full, k_taps, k_full, k_full, k_full, k_full, k_half, half, k_stat, k_stat, pinned((channels, ROWS)),
+        [low, k_full, k_taps, k_full, k_full, k_full, k_full, k_half, half, k_stat, k_stat, pinned((channels, ROWS)),
          pinned((ROWS, LANES))],
-        [s_full, s_full, s_sums, s_bias], 24,
-    )
-    rim_near = near_swap(rim_near)
+        [s_full, s_full, s_sums], 24,
+    )
     rim_far = far_swap(rim_far)
     got = near_swap(send)
-    stats, inner = call(
+    stats, inner, rim_near = call(
         taps_two_kernel, "taps_two",
         (par, mid, near, far, mx, cross, along, z_sums, select, base, tables, acc_gain, acc_scale, head_cols,
          head_lanes),
-        [k_stat, k_full], [s_taps], 8, after=(rim_near,),
-    )
+        [k_stat, k_full, low], [s_taps], 8, after=(got,),
+    )
+    rim_near = near_swap(rim_near)
     tall = shape((channels + PAIR + ROWS, hidden))
     k_tall = pinned(tall.shape)
     tall_low = shape((channels + 2 * PAIR, hidden), BF16)
@@ -748,27 +763,37 @@
     base, g_norm, keep, send, gs_scale = call(
         point_back_kernel, "point_back_one",
         (par, inner, rim_near, rim_far, act, slope, normed, cols, w_in_t, w_out, w_out_t),
-        [k_full, k_full, k_half, half, pinned((channels, 1))], [s_sums, s_bias], 8,
-    )
-    (two,) = call(spread_two_kernel, "sums_two", (two, *got), [k_tall], (), 4, after=(base,))
-    got = near_swap(send)
-    rim_far, rim_near, z_sums, cross, along, acc_gain = call(
+        [k_full, k_full, k_half, half, pinned((channels, 1))], [s_sums], 8,
+    )
+    got_two, got = got, near_swap(send)
+    rim_far, z_sums, cross, along, acc_gain = call(
         conv_back_kernel, "conv_back_one", (par, g_norm, normal, inverse, mxy_one, cols, tables),
-        [low, low, k_taps, k_full, k_full, k_stat], [s_full], 8, after=(two,),
-    )
-    rim_near = near_swap(rim_near)
+        [low, k_taps, k_full, k_full, k_stat], [s_full], 8,
+    )
     rim_far = far_swap(rim_far)
+    half_low = shape((channels + PAIR, hidden), BF16)
+    (two,) = call(
+        spread_two_kernel, "sums_two", (two, *got_two), [k_tall], (), 4, after=(along,), flops=4 * 10**10
+    )
+    one, one_low = call(first_kernel, "sums_one_a", (keep, got), [k_half, half_low], (), 4, after=(two,))
+    got = [bit_swap(one_low, step) for step in (4, 8, 12)]
     (stats,) = call(
         taps_one_kernel, "taps_one",
         (par, own_kept, near_kept, far_kept, mx_one, cross, along, z_sums, select, acc_gain, gs_scale),
-        [k_stat], [s_taps], 8, after=(rim_near,),
-    )
-    one, one_low = call(pack_kernel, "pack_one", (keep, got, stats), [k_tall, tall_low], (), 4)
-    got = [bit_swap(one_low, step) for step in (4, 8, 12)]
-    (inner,) = call(inside_kernel, "inside_one", (along, base, tables), [k_full], (), 4, after=(one,))
+        [k_stat], [s_taps], 8, after=(two,),
+    )
+    (one,) = call(spread_kernel, "sums_one_b", (one, *got), [k_half], (), 4, after=(stats,), flops=4 * 10**9)
+    stats, stats_low = call(
+        stats_pack_kernel, "pack_stats", (stats,), [pinned((ROWS, hidden)), shape((PAIR, hidden), BF16)], (), 4
+    )
+    got_stats = [bit_swap(stats_low, step) for step in (4, 8, 12)]
+    inner, rim_near = call(
+        inside_kernel, "inside_one", (par, along, base, tables), [k_full, low], (), 4
+    )
+    rim_near = near_swap(rim_near)
     both_shape = (2 * tall.shape[0], hidden)
     both, both_low = call(
-        spread_one_kernel, "sums_one", (one, *got, two),
+        spread_one_kernel, "sums_one", (one, stats, *got_stats, two),
         [pinned(both_shape), shape((2 * tall_low.shape[0], hidden), BF16)], (), 4, after=(inner,),
     )
     got = bit_swap(both_low, 2)

time: 108 us -> 105 us (0.972)
  waiting for transfers between devices: 25.1 us -> 9.56 us
  starting transfers between devices: 39.7 us -> 52.1 us
    ppermute x7 -> x10, waiting for transfers between devices: 23.4 us -> 8.09 us  [bit_swap(): return lax.ppermute(value, 'track', [(i, i ^ step) for i in range(count)])]
    ppermute x7, starting transfers between devices: 27.6 us -> 34.1 us  [near_swap(): return lax.ppermute(value, 'track', [(i, i ^ 1) for i in range(count)])]
    ppermute x7 -> x10, starting transfers between devices: 8.92 us -> 14.8 us  [bit_swap(): return lax.ppermute(value, 'track', [(i, i ^ step) for i in range(count)])]
    pallas_call x18 -> x20, Pallas kernels: 36.6 us -> 36.4 us  [call(): pl.pallas_call(run, name=name, out_shape=tuple(outs), in_specs=in_specs +...]
  transfers between devices with their start and end apart: 18 -> 21, of which waited for: 6 -> 4; matrix products, arithmetic and copies ran while one was open for 4% -> 4% of each run, Pallas kernels for 15% -> 19%
where the time goes in v5:
time: 105 us
  starting transfers between devices  52.1 us (50%)
  Pallas kernels  36.4 us (35%)
  waiting for transfers between devices  9.56 us (9%)
  local copies, waits for them, and re-layouts  5.05 us (5%)
    pallas_call x20, Pallas kernels, call(): pl.pallas_call(run, name=name, out_shape=tuple(outs), in_specs=in_specs +...  36.4 us
    ppermute x7, starting transfers between devices, near_swap(): return lax.ppermute(value, 'track', [(i, i ^ 1) for i in range(count)])  34.1 us
    ppermute x10, starting transfers between devices, bit_swap(): return lax.ppermute(value, 'track', [(i, i ^ step) for i in range(count)])  14.8 us
    ppermute x10, waiting for transfers between devices, bit_swap(): return lax.ppermute(value, 'track', [(i, i ^ step) for i in range(count)])  8.09 us
    unnamed x8, local copies, waits for them, and re-layouts  3.51 us
    ppermute x4, starting transfers between devices, far_swap(): return lax.ppermute(value, 'track', pairs)  3.16 us
  transfers between devices with their start and end apart: 21, of which 4 were waited for; matrix products, arithmetic and copies ran while one was open for 4% of the time, Pallas kernels for 19%

profile of v5, /device:TPU:0, one launch (start us, length us, event | category | flops | bytes accessed | tf_op | source)
XLA Modules:
  0.0 104.8 jit_solution(6892107242066214629)
XLA Ops:
  3.5 1.1 %copy.32.refs_2_ = bf16[2,384,96]{2,1,0:T(8,128)(2,1)S(1)} copy(bf16[2,384,96]{1,2,0:T(8,128)(2,1)} %param.18) | data formatting | bytes 294912 | tf_op args[4]
  7.7 1.9 %tables.1 = (f32[2,28,96,128]{3,2,1,0:T(8,128)S(1)}, f32[2,96,23]{2,1,0:T(8,128)S(1)}, f32[384,2]{1,0:T(8,128)S(1)}, bf16[2,384,96]{2,1,0:T(8,128)(2,1)S(1)}, bf...) custom-call(f32[2,96,23]{2,1,0:T(8,128)S(1)} %bitcast.17, ...), custom_call_target="tpu_custom_call" | custom-call | tf_op jit(solution)/shard_map/tables/pallas_call | solution.py:637
  9.6 1.2 %start_one.1 = (f32[24,96,128]{2,1,0:T(8,128)S(1)}, f32[24,96,128]{2,1,0:T(8,128)S(1)}, f32[24,96,128]{2,1,0:T(8,128)S(1)}) custom-call(s32[1]{0:T(128)} %bitcast.refs_0_, bf16[2304,128]{1,0:T(8,128)(2,1)S(1)} %bitcast.16, bf16[2304,128]{1,0:T(8,128)(2,1)S(1)} %collective-permute-done.1.refs_2_, ...), custom_call_target="tpu_custom_call" | custom-call | tf_op jit(solution)/shard_map/start_one/pallas_call | solution.py:637
  10.8 4.3 %forward_one.1 = (bf16[24,96,128]{2,1,0:T(8,128)(2,1)S(1)}, f32[24,96,128]{2,1,0:T(8,128)S(1)}, f32[24,96,128]{2,1,0:T(8,128)S(1)}, f32[24,96,128]{2,1,0:T(8,128)S(1)}, f32[24,96,128]{2,1,0:T(8,128)S(1)}) custom-call(s32[1]{0:T(128)} %bitcast.refs_0_, bf16[2304,128]{1,0:T(8,128)(2,1)S(1)} %collective-permute-done.refs_1_, ...), custom_call_target="tpu_custom_call" | custom-call | tf_op jit(solution)/shard_map/forward_one/pallas_call | solution.py:637
  15.1 8.5 %collective-permute-start.2 = (bf16[24,96,128]{2,1,0:T(8,128)(2,1)S(1)}, bf16[24,96,128]{2,1,0:T(8,128)(2,1)S(1)}, u32[]{:S(2)}, u32[]{:S(2)}) collective-permute-start(bf16[24,96,128]{2,1,0:T(8,128)(2,1)S(1)} %get-tuple-element.110.refs_1_.refs_3_), channel_id=1, source_target_pairs={{0,1},{1,0},{2,3},{3,2},{4,5},{5,4},{6,7},{7,6},{8,9},{9,8},{10,11... | collective-permute-start | bytes 1769480 | tf_op jit(solution)/shard_map/ppermute | solution.py:659
  24.5 3.1 %save_one.1 = (bf16[24,96,128]{2,1,0:T(8,128)(2,1)S(1)}, f32[24,96,128]{2,1,0:T(8,128)S(1)}, f32[2,1,1536]{2,1,0:T(1,128)S(1)}, bf16[2,384,1536]{2,1,0:T(8,128)(2,1)S(1)}, f32[2,384,1536]{2,1,0:T(8,128)S(1)}) custom-call(f32[24,96,128]{2,1,0:T(8,128)S(1)} %get-tuple-element.111.refs_0_, f32[2,96,23]{2,1,0:T(8,128)S(1)} %get-tuple-element.106.refs_4_.refs_1_.refs_5_.refs_7_, ...), custom_call_target="tpu_custom_call" | custom-call | tf_op jit(solution)/shard_map/save_one/pallas_call | solution.py:637
  28.2 11.0 %turn_two.1 = (bf16[24,96,128]{2,1,0:T(8,128)(2,1)S(1)}, f32[24,96,128]{2,1,0:T(8,128)S(1)}, f32[7,96,128]{2,1,0:T(8,128)S(1)}, f32[24,96,128]{2,1,0:T(8,128)S(1...) custom-call(s32[1]{0:T(128)} %bitcast.refs_0_, ...), custom_call_target="tpu_custom_call" | custom-call | tf_op jit(solution)/shard_map/turn_two/pallas_call | solution.py:637
  39.2 12.8 %collective-permute-start.4 = (f32[112,384]{1,0:T(8,128)S(1)}, f32[112,384]{1,0:T(8,128)S(1)}, u32[]{:S(2)}, u32[]{:S(2)}) collective-permute-start(f32[112,384]{1,0:T(8,128)S(1)} %get-tuple-element.129), channel_id=1, source_target_pairs={{0,1},{1,0},{2,3},{3,2},{4,5},{5,4},{6,7},{7,6},{8,9},{9,8},{10,11... | collective-permute-start | bytes 516104 | tf_op jit(solution)/shard_map/ppermute | solution.py:659
  53.1 2.8 %taps_two.1 = (f32[96,128]{1,0:T(8,128)S(1)}, f32[24,96,128]{2,1,0:T(8,128)S(1)}, bf16[24,96,128]{2,1,0:T(8,128)(2,1)S(1)}) custom-call(s32[1]{0:T(128)} %bitcast.refs_0_, bf16[24,96,128]{2,1,0:T(8,128)(2,1)S(1)} %get-tuple-element.110.refs_1_.refs_3_, bf16[24,96,128]{2,1,0:T(8,128)(2,1)S(1)} %collective-permute-done.2.refs_2_, ...), custom_call_target="tpu_custom_call" | custom-call | tf_op jit(solution)/shard_map/taps_two/pallas_call | solution.py:637
  55.9 3.7 %collective-permute-start.5 = (bf16[24,96,128]{2,1,0:T(8,128)(2,1)S(1)}, bf16[24,96,128]{2,1,0:T(8,128)(2,1)S(1)}, u32[]{:S(2)}, u32[]{:S(2)}) collective-permute-start(bf16[24,96,128]{2,1,0:T(8,128)(2,1)S(1)} %get-tuple-element.131), channel_id=1, source_target_pairs={{0,1},{1,0},{2,3},{3,2},{4,5},{5,4},{6,7},{7,6},{8,9},{9,8},{10,11... | collective-permute-start | bytes 1769480 | tf_op jit(solution)/shard_map/ppermute | solution.py:659
  59.6 3.5 %collective-permute-start.12 = (bf16[128,384]{1,0:T(8,128)(2,1)S(1)}, bf16[128,384]{1,0:T(8,128)(2,1)S(1)}, u32[]{:S(2)}, u32[]{:S(2)}) collective-permute-start(bf16[128,384]{1,0:T(8,128)(2,1)S(1)} %get-tuple-element.149), channel_id=1, source_target_pairs={{0,12},{1,13},{2,14},{3,15},{4,8},{5,9},{6,10},{7,11},{8,4},{9,5},... | collective-permute-start | bytes 294920 | tf_op jit(solution)/shard_map/ppermute | solution.py:672
  64.0 2.5 %point_back_one.1 = (f32[24,96,128]{2,1,0:T(8,128)S(1)}, f32[24,96,128]{2,1,0:T(8,128)S(1)}, f32[112,384]{1,0:T(8,128)S(1)}, f32[112,384]{1,0:T(8,128)S(1)}, f32[96,1]{1,0:T(8,128)S(1)}) custom-call(s32[1]{0:T(128)} %bitcast.refs_0_, f32[24,96,128]{2,1,0:T(8,128)S(1)} %get-tuple-element.130.refs_1_.refs_3_, ...), custom_call_target="tpu_custom_call" | custom-call | tf_op jit(solution)/shard_map/point_back_one/pallas_call | solution.py:637
  66.5 5.6 %collective-permute-start.9 = (f32[112,384]{1,0:T(8,128)S(1)}, f32[112,384]{1,0:T(8,128)S(1)}, u32[]{:S(2)}, u32[]{:S(2)}) collective-permute-start(f32[112,384]{1,0:T(8,128)S(1)} %get-tuple-element.145), channel_id=1, source_target_pairs={{0,1},{1,0},{2,3},{3,2},{4,5},{5,4},{6,7},{7,6},{8,9},{9,8},{10,11... | collective-permute-start | bytes 516104 | tf_op jit(solution)/shard_map/ppermute | solution.py:659
  72.1 3.3 %conv_back_one.1 = (bf16[24,96,128]{2,1,0:T(8,128)(2,1)S(1)}, f32[7,96,128]{2,1,0:T(8,128)S(1)}, f32[24,96,128]{2,1,0:T(8,128)S(1)}, f32[24,96,128]{2,1,0:T(8,128)S(1)}, f32[96,128]{1,0:T(8,128)S(1)}) custom-call(s32[1]{0:T(128)} %bitcast.refs_0_, f32[24,96,128]{2,1,0:T(8,128)S(1)} %get-tuple-element.136.refs_1_, ...), custom_call_target="tpu_custom_call" | custom-call | tf_op jit(solution)/shard_map/conv_back_one/pallas_call | solution.py:637
  75.6 5.2 %collective-permute-start.15 = (bf16[112,384]{1,0:T(8,128)(2,1)S(1)}, bf16[112,384]{1,0:T(8,128)(2,1)S(1)}, u32[]{:S(2)}, u32[]{:S(2)}) collective-permute-start(bf16[112,384]{1,0:T(8,128)(2,1)S(1)} %get-tuple-element.151), channel_id=1, source_target_pairs={{0,12},{1,13},{2,14},{3,15},{4,8},{5,9},{6,10},{7,11},{8,4},{9,5},... | collective-permute-start | bytes 258056 | tf_op jit(solution)/shard_map/ppermute | solution.py:672
  82.8 2.4 %collective-permute-start.7 = (bf16[24,96,128]{2,1,0:T(8,128)(2,1)S(1)}, bf16[24,96,128]{2,1,0:T(8,128)(2,1)S(1)}, u32[]{:S(2)}, u32[]{:S(2)}) collective-permute-start(bf16[24,96,128]{2,1,0:T(8,128)(2,1)S(1)} %get-tuple-element.142), channel_id=1, source_target_pairs={{0,1},{1,0},{2,3},{3,2},{4,5},{5,4},{6,7},{7,6},{8,9},{9,8},{10,11... | collective-permute-start | bytes 1769480 | tf_op jit(solution)/shard_map/ppermute | solution.py:659
  85.2 2.3 %taps_one.1.refs_4_.refs_0_ = f32[96,128]{1,0:T(8,128)S(1)} custom-call(s32[1]{0:T(128)} %bitcast.refs_0_, f32[24,96,128]{2,1,0:T(8,128)S(1)} %get-tuple-element.105.refs_3_.refs_1_, f32[24,96,128]{2,1,0:T(8,128)S(1)} %get-tuple-element.152.refs_2_, f32[24,96,128]{2,1,0:T(8,128)S(1)} %get-tuple-element.153.refs_3_, ...), custom_call_target="tpu_custom_call" | custom-call | tf_op jit(solution)/shard_map/taps_one/pallas_call | solution.py:637
  87.6 2.7 %collective-permute-start.18 = (bf16[16,384]{1,0:T(8,128)(2,1)S(1)}, bf16[16,384]{1,0:T(8,128)(2,1)S(1)}, u32[]{:S(2)}, u32[]{:S(2)}) collective-permute-start(bf16[16,384]{1,0:T(8,128)(2,1)S(1)} %get-tuple-element.160), channel_id=1, source_target_pairs={{0,12},{1,13},{2,14},{3,15},{4,8},{5,9},{6,10},{7,11},{8,4},{9,5},... | collective-permute-start | bytes 36872 | tf_op jit(solution)/shard_map/ppermute | solution.py:672
  90.3 1.8 %collective-permute-start.16 = (bf16[16,384]{1,0:T(8,128)(2,1)S(1)}, bf16[16,384]{1,0:T(8,128)(2,1)S(1)}, u32[]{:S(2)}, u32[]{:S(2)}) collective-permute-start(bf16[16,384]{1,0:T(8,128)(2,1)S(1)} %get-tuple-element.160), channel_id=1, source_target_pairs={{0,4},{1,5},{2,6},{3,7},{4,0},{5,1},{6,2},{7,3},{8,12},{9,13},{10,... | collective-permute-start | bytes 36872 | tf_op jit(solution)/shard_map/ppermute | solution.py:672
  92.1 4.0 %collective-permute-done.18.refs_4_ = bf16[16,384]{1,0:T(8,128)(2,1)S(1)} collective-permute-done((bf16[16,384]{1,0:T(8,128)(2,1)S(1)}, bf16[16,384]{1,0:T(8,128)(2,1)S(1)}, u32[]{:S(2)}, u32[]{:S(2)}) %collective-permute-start.18) | collective-permute-done | bytes 12320 | tf_op jit(solution)/shard_map/ppermute | solution.py:672
  96.3 1.5 %last.1 = (f32[2304,128]{1,0:T(8,128)}, f32[8,128]{1,0:T(8,128)S(1)}) custom-call(f32[24,96,128]{2,1,0:T(8,128)S(1)} %get-tuple-element.141.refs_6_.refs_0_, bf16[24,96,128]{2,1,0:T(8,128)(2,1)S(1)} %collective-permute-done.7.refs_1_, bf16[24,96,128]{2,1,0:T(8,128)(2,1)S(1)} %collective-permute-done.8.refs_2_, f32[240,384]{1,0:T(8,128)S(1)} %get-tuple-element.161.refs_3_.refs_0_), custom_call_target="tpu_custom_call" | custom-call | tf_op jit(solution)/shard_map/last/pallas_call | solution.py:637
  97.9 4.1 %collective-permute-done.19.refs_1_ = bf16[256,384]{1,0:T(8,128)(2,1)S(1)} collective-permute-done((bf16[256,384]{1,0:T(8,128)(2,1)S(1)}, bf16[256,384]{1,0:T(8,128)(2,1)S(1)}, u32[]{:S(2)}, u32[]{:S(2)}) %collective-permute-start.19) | collective-permute-done | bytes 196640 | tf_op jit(solution)/shard_map/ppermute | solution.py:672
  102.6 1.3 %collective-permute-done.20.refs_2_ = f32[240,384]{1,0:T(8,128)S(1)} collective-permute-done((f32[240,384]{1,0:T(8,128)S(1)}, f32[240,384]{1,0:T(8,128)S(1)}, u32[]{:S(2)}, u32[]{:S(2)}) %collective-permute-start.20) | collective-permute-done | bytes 368672 | tf_op jit(solution)/shard_map/ppermute | solution.py:659
  103.9 0.9 final.1
  (51 shorter events, 12.5 us)
Async XLA Ops:
  0.6 9.0 %copy-start = (bf16[96,3,8,128]{3,2,1,0:T(8,128)(2,1)S(1)}, bf16[96,3,8,128]{3,2,1,0:T(8,128)(2,1)}, u32[]{:S(2)}) copy-start(bf16[96,3,8,128]{3,2,1,0:T(8,128)(2,1)} %param.14) | copy-start | bytes 1769476
  0.7 8.9 %collective-permute-start.1 = (bf16[2304,128]{1,0:T(8,128)(2,1)}, bf16[2304,128]{1,0:T(8,128)(2,1)S(1)}, u32[]{:S(2)}, u32[]{:S(2)}) collective-permute-start(bf16[2304,128]{1,0:T(8,128)(2,1)} %bitcast.14), channel_id=1, source_target_pairs={{0,1},{1,0},{2,3},{3,2},{4,5},{5,4},{6,7},{7,6},{8,9},{9,8},{10,11... | collective-permute-start | bytes 1769480 | tf_op jit(solution)/shard_map/ppermute | solution.py:659
  1.2 9.6 %collective-permute-start = (bf16[2304,128]{1,0:T(8,128)(2,1)}, bf16[2304,128]{1,0:T(8,128)(2,1)S(1)}, u32[]{:S(2)}, u32[]{:S(2)}) collective-permute-start(bf16[2304,128]{1,0:T(8,128)(2,1)} %bitcast.15), channel_id=1, source_target_pairs={{1,2},{2,1},{3,4},{4,3},{5,6},{6,5},{7,8},{8,7},{9,10},{10,9},{11,... | collective-permute-start | bytes 1769480 | tf_op jit(solution)/shard_map/ppermute | solution.py:667
  6.1 0.9 copy-start.1
  7.0 0.7 copy-start.2
  15.1 12.6 %collective-permute-start.2 = (bf16[24,96,128]{2,1,0:T(8,128)(2,1)S(1)}, bf16[24,96,128]{2,1,0:T(8,128)(2,1)S(1)}, u32[]{:S(2)}, u32[]{:S(2)}) collective-permute-start(bf16[24,96,128]{2,1,0:T(8,128)(2,1)S(1)} %get-tuple-element.110.refs_1_.refs_3_), channel_id=1, source_target_pairs={{0,1},{1,0},{2,3},{3,2},{4,5},{5,4},{6,7},{7,6},{8,9},{9,8},{10,11... | collective-permute-start | bytes 1769480 | tf_op jit(solution)/shard_map/ppermute | solution.py:659
  23.6 4.6 %collective-permute-start.3 = (bf16[24,96,128]{2,1,0:T(8,128)(2,1)S(1)}, bf16[24,96,128]{2,1,0:T(8,128)(2,1)S(1)}, u32[]{:S(2)}, u32[]{:S(2)}) collective-permute-start(bf16[24,96,128]{2,1,0:T(8,128)(2,1)S(1)} %get-tuple-element.110.refs_1_.refs_3_), channel_id=1, source_target_pairs={{1,2},{2,1},{3,4},{4,3},{5,6},{6,5},{7,8},{8,7},{9,10},{10,9},{11,... | collective-permute-start | bytes 1769480 | tf_op jit(solution)/shard_map/ppermute | solution.py:667
  39.2 13.9 %collective-permute-start.4 = (f32[112,384]{1,0:T(8,128)S(1)}, f32[112,384]{1,0:T(8,128)S(1)}, u32[]{:S(2)}, u32[]{:S(2)}) collective-permute-start(f32[112,384]{1,0:T(8,128)S(1)} %get-tuple-element.129), channel_id=1, source_target_pairs={{0,1},{1,0},{2,3},{3,2},{4,5},{5,4},{6,7},{7,6},{8,9},{9,8},{10,11... | collective-permute-start | bytes 516104 | tf_op jit(solution)/shard_map/ppermute | solution.py:659
  52.0 12.0 %collective-permute-start.6 = (bf16[24,96,128]{2,1,0:T(8,128)(2,1)S(1)}, bf16[24,96,128]{2,1,0:T(8,128)(2,1)S(1)}, u32[]{:S(2)}, u32[]{:S(2)}) collective-permute-start(bf16[24,96,128]{2,1,0:T(8,128)(2,1)S(1)} %get-tuple-element.132), channel_id=1, source_target_pairs={{1,2},{2,1},{3,4},{4,3},{5,6},{6,5},{7,8},{8,7},{9,10},{10,9},{11,... | collective-permute-start | bytes 1769480 | tf_op jit(solution)/shard_map/ppermute | solution.py:667
  55.9 8.2 %collective-permute-start.5 = (bf16[24,96,128]{2,1,0:T(8,128)(2,1)S(1)}, bf16[24,96,128]{2,1,0:T(8,128)(2,1)S(1)}, u32[]{:S(2)}, u32[]{:S(2)}) collective-permute-start(bf16[24,96,128]{2,1,0:T(8,128)(2,1)S(1)} %get-tuple-element.131), channel_id=1, source_target_pairs={{0,1},{1,0},{2,3},{3,2},{4,5},{5,4},{6,7},{7,6},{8,9},{9,8},{10,11... | collective-permute-start | bytes 1769480 | tf_op jit(solution)/shard_map/ppermute | solution.py:659
  59.6 15.8 %collective-permute-start.12 = (bf16[128,384]{1,0:T(8,128)(2,1)S(1)}, bf16[128,384]{1,0:T(8,128)(2,1)S(1)}, u32[]{:S(2)}, u32[]{:S(2)}) collective-permute-start(bf16[128,384]{1,0:T(8,128)(2,1)S(1)} %get-tuple-element.149), channel_id=1, source_target_pairs={{0,12},{1,13},{2,14},{3,15},{4,8},{5,9},{6,10},{7,11},{8,4},{9,5},... | collective-permute-start | bytes 294920 | tf_op jit(solution)/shard_map/ppermute | solution.py:672
  63.1 12.3 %collective-permute-start.11 = (bf16[128,384]{1,0:T(8,128)(2,1)S(1)}, bf16[128,384]{1,0:T(8,128)(2,1)S(1)}, u32[]{:S(2)}, u32[]{:S(2)}) collective-permute-start(bf16[128,384]{1,0:T(8,128)(2,1)S(1)} %get-tuple-element.149), channel_id=1, source_target_pairs={{0,8},{1,9},{2,10},{3,11},{4,12},{5,13},{6,14},{7,15},{8,0},{9,1},... | collective-permute-start | bytes 294920 | tf_op jit(solution)/shard_map/ppermute | solution.py:672
  63.1 12.3 %collective-permute-start.10 = (bf16[128,384]{1,0:T(8,128)(2,1)S(1)}, bf16[128,384]{1,0:T(8,128)(2,1)S(1)}, u32[]{:S(2)}, u32[]{:S(2)}) collective-permute-start(bf16[128,384]{1,0:T(8,128)(2,1)S(1)} %get-tuple-element.149), channel_id=1, source_target_pairs={{0,4},{1,5},{2,6},{3,7},{4,0},{5,1},{6,2},{7,3},{8,12},{9,13},{10,... | collective-permute-start | bytes 294920 | tf_op jit(solution)/shard_map/ppermute | solution.py:672
  66.5 9.0 %collective-permute-start.9 = (f32[112,384]{1,0:T(8,128)S(1)}, f32[112,384]{1,0:T(8,128)S(1)}, u32[]{:S(2)}, u32[]{:S(2)}) collective-permute-start(f32[112,384]{1,0:T(8,128)S(1)} %get-tuple-element.145), channel_id=1, source_target_pairs={{0,1},{1,0},{2,3},{3,2},{4,5},{5,4},{6,7},{7,6},{8,9},{9,8},{10,11... | collective-permute-start | bytes 516104 | tf_op jit(solution)/shard_map/ppermute | solution.py:659
  75.6 12.0 %collective-permute-start.15 = (bf16[112,384]{1,0:T(8,128)(2,1)S(1)}, bf16[112,384]{1,0:T(8,128)(2,1)S(1)}, u32[]{:S(2)}, u32[]{:S(2)}) collective-permute-start(bf16[112,384]{1,0:T(8,128)(2,1)S(1)} %get-tuple-element.151), channel_id=1, source_target_pairs={{0,12},{1,13},{2,14},{3,15},{4,8},{5,9},{6,10},{7,11},{8,4},{9,5},... | collective-permute-start | bytes 258056 | tf_op jit(solution)/shard_map/ppermute | solution.py:672
  80.7 9.6 %collective-permute-start.14 = (bf16[112,384]{1,0:T(8,128)(2,1)S(1)}, bf16[112,384]{1,0:T(8,128)(2,1)S(1)}, u32[]{:S(2)}, u32[]{:S(2)}) collective-permute-start(bf16[112,384]{1,0:T(8,128)(2,1)S(1)} %get-tuple-element.151), channel_id=1, source_target_pairs={{0,8},{1,9},{2,10},{3,11},{4,12},{5,13},{6,14},{7,15},{8,0},{9,1},... | collective-permute-start | bytes 258056 | tf_op jit(solution)/shard_map/ppermute | solution.py:672
  80.7 9.6 %collective-permute-start.13 = (bf16[112,384]{1,0:T(8,128)(2,1)S(1)}, bf16[112,384]{1,0:T(8,128)(2,1)S(1)}, u32[]{:S(2)}, u32[]{:S(2)}) collective-permute-start(bf16[112,384]{1,0:T(8,128)(2,1)S(1)} %get-tuple-element.151), channel_id=1, source_target_pairs={{0,4},{1,5},{2,6},{3,7},{4,0},{5,1},{6,2},{7,3},{8,12},{9,13},{10,... | collective-permute-start | bytes 258056 | tf_op jit(solution)/shard_map/ppermute | solution.py:672
  82.0 14.3 %collective-permute-start.8 = (bf16[24,96,128]{2,1,0:T(8,128)(2,1)S(1)}, bf16[24,96,128]{2,1,0:T(8,128)(2,1)S(1)}, u32[]{:S(2)}, u32[]{:S(2)}) collective-permute-start(bf16[24,96,128]{2,1,0:T(8,128)(2,1)S(1)} %get-tuple-element.143), channel_id=1, source_target_pairs={{1,2},{2,1},{3,4},{4,3},{5,6},{6,5},{7,8},{8,7},{9,10},{10,9},{11,... | collective-permute-start | bytes 1769480 | tf_op jit(solution)/shard_map/ppermute | solution.py:667
  82.8 13.6 %collective-permute-start.7 = (bf16[24,96,128]{2,1,0:T(8,128)(2,1)S(1)}, bf16[24,96,128]{2,1,0:T(8,128)(2,1)S(1)}, u32[]{:S(2)}, u32[]{:S(2)}) collective-permute-start(bf16[24,96,128]{2,1,0:T(8,128)(2,1)S(1)} %get-tuple-element.142), channel_id=1, source_target_pairs={{0,1},{1,0},{2,3},{3,2},{4,5},{5,4},{6,7},{7,6},{8,9},{9,8},{10,11... | collective-permute-start | bytes 1769480 | tf_op jit(solution)/shard_map/ppermute | solution.py:659
  87.6 8.5 %collective-permute-start.18 = (bf16[16,384]{1,0:T(8,128)(2,1)S(1)}, bf16[16,384]{1,0:T(8,128)(2,1)S(1)}, u32[]{:S(2)}, u32[]{:S(2)}) collective-permute-start(bf16[16,384]{1,0:T(8,128)(2,1)S(1)} %get-tuple-element.160), channel_id=1, source_target_pairs={{0,12},{1,13},{2,14},{3,15},{4,8},{5,9},{6,10},{7,11},{8,4},{9,5},... | collective-permute-start | bytes 36872 | tf_op jit(solution)/shard_map/ppermute | solution.py:672
  90.3 5.8 %collective-permute-start.17 = (bf16[16,384]{1,0:T(8,128)(2,1)S(1)}, bf16[16,384]{1,0:T(8,128)(2,1)S(1)}, u32[]{:S(2)}, u32[]{:S(2)}) collective-permute-start(bf16[16,384]{1,0:T(8,128)(2,1)S(1)} %get-tuple-element.160), channel_id=1, source_target_pairs={{0,8},{1,9},{2,10},{3,11},{4,12},{5,13},{6,14},{7,15},{8,0},{9,1},... | collective-permute-start | bytes 36872 | tf_op jit(solution)/shard_map/ppermute | solution.py:672
  90.3 5.8 %collective-permute-start.16 = (bf16[16,384]{1,0:T(8,128)(2,1)S(1)}, bf16[16,384]{1,0:T(8,128)(2,1)S(1)}, u32[]{:S(2)}, u32[]{:S(2)}) collective-permute-start(bf16[16,384]{1,0:T(8,128)(2,1)S(1)} %get-tuple-element.160), channel_id=1, source_target_pairs={{0,4},{1,5},{2,6},{3,7},{4,0},{5,1},{6,2},{7,3},{8,12},{9,13},{10,... | collective-permute-start | bytes 36872 | tf_op jit(solution)/shard_map/ppermute | solution.py:672
  96.2 5.7 %collective-permute-start.19 = (bf16[256,384]{1,0:T(8,128)(2,1)S(1)}, bf16[256,384]{1,0:T(8,128)(2,1)S(1)}, u32[]{:S(2)}, u32[]{:S(2)}) collective-permute-start(bf16[256,384]{1,0:T(8,128)(2,1)S(1)} %get-tuple-element.163), channel_id=1, source_target_pairs={{0,2},{1,3},{2,0},{3,1},{4,6},{5,7},{6,4},{7,5},{8,10},{9,11},{10,... | collective-permute-start | bytes 589832 | tf_op jit(solution)/shard_map/ppermute | solution.py:672
  102.0 1.9 %collective-permute-start.20 = (f32[240,384]{1,0:T(8,128)S(1)}, f32[240,384]{1,0:T(8,128)S(1)}, u32[]{:S(2)}, u32[]{:S(2)}) collective-permute-start(f32[240,384]{1,0:T(8,128)S(1)} %sums_last.1.refs_1_), channel_id=1, source_target_pairs={{0,1},{1,0},{2,3},{3,2},{4,5},{5,4},{6,7},{7,6},{8,9},{9,8},{10,11... | collective-permute-start | bytes 1105928 | tf_op jit(solution)/shard_map/ppermute | solution.py:659

commit v6 on v5

--- a/solution.py
+++ b/solution.py
@@ -175,7 +175,7 @@
                 mixed[p * Y + y, rows, :] = weighted(zip(tz, turns(value, -1)))
         return carry
 
-    lax.fori_loop(0, mixed.shape[1] // PAIR, one, 0)
+    lax.fori_loop(0, mixed.shape[1] // PAIR, one, 0, unroll=3)
 
 
 def convolve_back(dmixed, mxy, cols, cross_out, along, sums):
@@ -202,7 +202,7 @@
             sums[k, rows, :] = jnp.where((lane - shift >= 0) & (lane - shift < LANES), found[k], 0.0)
         return carry
 
-    lax.fori_loop(0, dmixed.shape[1] // PAIR, one, 0)
+    lax.fori_loop(0, dmixed.shape[1] // PAIR, one, 0, unroll=6)
 
 
 def rim(par, along, cols, far, out):
@@ -262,7 +262,7 @@
             sums[T_X + k, rows, :] = resolved[k]
         return carry
 
-    lax.fori_loop(0, mx.shape[1] // PAIR, along_track, 0)
+    lax.fori_loop(0, mx.shape[1] // PAIR, along_track, 0, unroll=3)
 
     def cross_track(group, carry):
         rows = group_rows(group)
@@ -278,7 +278,7 @@
             sums[T_Y + k, rows, :] = total[k]
         return carry
 
-    lax.fori_loop(0, mx.shape[1] // ROWS, cross_track, 0)
+    lax.fori_loop(0, mx.shape[1] // ROWS, cross_track, 0, unroll=3)
     terms = [sums[k] for k in range(2 * TAPS)] + [z_sums[k] for k in range(TAPS)]
     wide = jnp.concatenate(terms, axis=1)
     high = wide.astype(BF16)

time: 105 us -> 104 us (level)
  Pallas kernels: 36.4 us -> 35.2 us
    pallas_call x20, Pallas kernels: 36.4 us -> 35.2 us  [call(): pl.pallas_call(run, name=name, out_shape=tuple(outs), in_specs=in_specs +...]
  transfers between devices with their start and end apart: 21 -> 21, of which waited for: 4 -> 5; matrix products, arithmetic and copies ran while one was open for 4% -> 4% of each run, Pallas kernels for 19% -> 19%
where the time goes in v6:
time: 104 us
  starting transfers between devices  51.9 us (50%)
  Pallas kernels  35.2 us (34%)
  waiting for transfers between devices  9.96 us (10%)
  local copies, waits for them, and re-layouts  5.05 us (5%)
    pallas_call x20, Pallas kernels, call(): pl.pallas_call(run, name=name, out_shape=tuple(outs), in_specs=in_specs +...  35.2 us
    ppermute x7, starting transfers between devices, near_swap(): return lax.ppermute(value, 'track', [(i, i ^ 1) for i in range(count)])  34.4 us
    ppermute x10, starting transfers between devices, bit_swap(): return lax.ppermute(value, 'track', [(i, i ^ step) for i in range(count)])  14.3 us
    ppermute x10, waiting for transfers between devices, bit_swap(): return lax.ppermute(value, 'track', [(i, i ^ step) for i in range(count)])  8.5 us
    unnamed x8, local copies, waits for them, and re-layouts  3.51 us
    ppermute x4, starting transfers between devices, far_swap(): return lax.ppermute(value, 'track', pairs)  3.16 us
  transfers between devices with their start and end apart: 21, of which 5 were waited for; matrix products, arithmetic and copies ran while one was open for 4% of the time, Pallas kernels for 19%

profile of v6, /device:TPU:0, one launch (start us, length us, event | category | flops | bytes accessed | tf_op | source)
XLA Modules:
  0.0 103.7 jit_solution(11240276307076279070)
XLA Ops:
  3.5 1.1 %copy.32.refs_2_ = bf16[2,384,96]{2,1,0:T(8,128)(2,1)S(1)} copy(bf16[2,384,96]{1,2,0:T(8,128)(2,1)} %param.18) | data formatting | bytes 294912 | tf_op args[4]
  7.7 1.9 %tables.1 = (f32[2,28,96,128]{3,2,1,0:T(8,128)S(1)}, f32[2,96,23]{2,1,0:T(8,128)S(1)}, f32[384,2]{1,0:T(8,128)S(1)}, bf16[2,384,96]{2,1,0:T(8,128)(2,1)S(1)}, bf...) custom-call(f32[2,96,23]{2,1,0:T(8,128)S(1)} %bitcast.17, ...), custom_call_target="tpu_custom_call" | custom-call | tf_op jit(solution)/shard_map/tables/pallas_call | solution.py:637
  9.6 1.2 %start_one.1 = (f32[24,96,128]{2,1,0:T(8,128)S(1)}, f32[24,96,128]{2,1,0:T(8,128)S(1)}, f32[24,96,128]{2,1,0:T(8,128)S(1)}) custom-call(s32[1]{0:T(128)} %bitcast.refs_0_, bf16[2304,128]{1,0:T(8,128)(2,1)S(1)} %bitcast.16, bf16[2304,128]{1,0:T(8,128)(2,1)S(1)} %collective-permute-done.1.refs_2_, ...), custom_call_target="tpu_custom_call" | custom-call | tf_op jit(solution)/shard_map/start_one/pallas_call | solution.py:637
  10.8 4.1 %forward_one.1 = (bf16[24,96,128]{2,1,0:T(8,128)(2,1)S(1)}, f32[24,96,128]{2,1,0:T(8,128)S(1)}, f32[24,96,128]{2,1,0:T(8,128)S(1)}, f32[24,96,128]{2,1,0:T(8,128)S(1)}, f32[24,96,128]{2,1,0:T(8,128)S(1)}) custom-call(s32[1]{0:T(128)} %bitcast.refs_0_, bf16[2304,128]{1,0:T(8,128)(2,1)S(1)} %collective-permute-done.refs_1_, ...), custom_call_target="tpu_custom_call" | custom-call | tf_op jit(solution)/shard_map/forward_one/pallas_call | solution.py:637
  14.9 8.5 %collective-permute-start.2 = (bf16[24,96,128]{2,1,0:T(8,128)(2,1)S(1)}, bf16[24,96,128]{2,1,0:T(8,128)(2,1)S(1)}, u32[]{:S(2)}, u32[]{:S(2)}) collective-permute-start(bf16[24,96,128]{2,1,0:T(8,128)(2,1)S(1)} %get-tuple-element.110.refs_1_.refs_3_), channel_id=1, source_target_pairs={{0,1},{1,0},{2,3},{3,2},{4,5},{5,4},{6,7},{7,6},{8,9},{9,8},{10,11... | collective-permute-start | bytes 1769480 | tf_op jit(solution)/shard_map/ppermute | solution.py:659
  24.4 3.1 %save_one.1 = (bf16[24,96,128]{2,1,0:T(8,128)(2,1)S(1)}, f32[24,96,128]{2,1,0:T(8,128)S(1)}, f32[2,1,1536]{2,1,0:T(1,128)S(1)}, bf16[2,384,1536]{2,1,0:T(8,128)(2,1)S(1)}, f32[2,384,1536]{2,1,0:T(8,128)S(1)}) custom-call(f32[24,96,128]{2,1,0:T(8,128)S(1)} %get-tuple-element.111.refs_0_, f32[2,96,23]{2,1,0:T(8,128)S(1)} %get-tuple-element.106.refs_4_.refs_1_.refs_5_.refs_7_, ...), custom_call_target="tpu_custom_call" | custom-call | tf_op jit(solution)/shard_map/save_one/pallas_call | solution.py:637
  28.1 10.7 %turn_two.1 = (bf16[24,96,128]{2,1,0:T(8,128)(2,1)S(1)}, f32[24,96,128]{2,1,0:T(8,128)S(1)}, f32[7,96,128]{2,1,0:T(8,128)S(1)}, f32[24,96,128]{2,1,0:T(8,128)S(1...) custom-call(s32[1]{0:T(128)} %bitcast.refs_0_, ...), custom_call_target="tpu_custom_call" | custom-call | tf_op jit(solution)/shard_map/turn_two/pallas_call | solution.py:637
  38.7 12.8 %collective-permute-start.4 = (f32[112,384]{1,0:T(8,128)S(1)}, f32[112,384]{1,0:T(8,128)S(1)}, u32[]{:S(2)}, u32[]{:S(2)}) collective-permute-start(f32[112,384]{1,0:T(8,128)S(1)} %get-tuple-element.129), channel_id=1, source_target_pairs={{0,1},{1,0},{2,3},{3,2},{4,5},{5,4},{6,7},{7,6},{8,9},{9,8},{10,11... | collective-permute-start | bytes 516104 | tf_op jit(solution)/shard_map/ppermute | solution.py:659
  52.6 2.7 %taps_two.1 = (f32[96,128]{1,0:T(8,128)S(1)}, f32[24,96,128]{2,1,0:T(8,128)S(1)}, bf16[24,96,128]{2,1,0:T(8,128)(2,1)S(1)}) custom-call(s32[1]{0:T(128)} %bitcast.refs_0_, bf16[24,96,128]{2,1,0:T(8,128)(2,1)S(1)} %get-tuple-element.110.refs_1_.refs_3_, bf16[24,96,128]{2,1,0:T(8,128)(2,1)S(1)} %collective-permute-done.2.refs_2_, ...), custom_call_target="tpu_custom_call" | custom-call | tf_op jit(solution)/shard_map/taps_two/pallas_call | solution.py:637
  55.3 3.7 %collective-permute-start.5 = (bf16[24,96,128]{2,1,0:T(8,128)(2,1)S(1)}, bf16[24,96,128]{2,1,0:T(8,128)(2,1)S(1)}, u32[]{:S(2)}, u32[]{:S(2)}) collective-permute-start(bf16[24,96,128]{2,1,0:T(8,128)(2,1)S(1)} %get-tuple-element.131), channel_id=1, source_target_pairs={{0,1},{1,0},{2,3},{3,2},{4,5},{5,4},{6,7},{7,6},{8,9},{9,8},{10,11... | collective-permute-start | bytes 1769480 | tf_op jit(solution)/shard_map/ppermute | solution.py:659
  59.1 3.5 %collective-permute-start.12 = (bf16[128,384]{1,0:T(8,128)(2,1)S(1)}, bf16[128,384]{1,0:T(8,128)(2,1)S(1)}, u32[]{:S(2)}, u32[]{:S(2)}) collective-permute-start(bf16[128,384]{1,0:T(8,128)(2,1)S(1)} %get-tuple-element.149), channel_id=1, source_target_pairs={{0,12},{1,13},{2,14},{3,15},{4,8},{5,9},{6,10},{7,11},{8,4},{9,5},... | collective-permute-start | bytes 294920 | tf_op jit(solution)/shard_map/ppermute | solution.py:672
  63.5 2.5 %point_back_one.1 = (f32[24,96,128]{2,1,0:T(8,128)S(1)}, f32[24,96,128]{2,1,0:T(8,128)S(1)}, f32[112,384]{1,0:T(8,128)S(1)}, f32[112,384]{1,0:T(8,128)S(1)}, f32[96,1]{1,0:T(8,128)S(1)}) custom-call(s32[1]{0:T(128)} %bitcast.refs_0_, f32[24,96,128]{2,1,0:T(8,128)S(1)} %get-tuple-element.130.refs_1_.refs_3_, ...), custom_call_target="tpu_custom_call" | custom-call | tf_op jit(solution)/shard_map/point_back_one/pallas_call | solution.py:637
  66.0 5.7 %collective-permute-start.9 = (f32[112,384]{1,0:T(8,128)S(1)}, f32[112,384]{1,0:T(8,128)S(1)}, u32[]{:S(2)}, u32[]{:S(2)}) collective-permute-start(f32[112,384]{1,0:T(8,128)S(1)} %get-tuple-element.145), channel_id=1, source_target_pairs={{0,1},{1,0},{2,3},{3,2},{4,5},{5,4},{6,7},{7,6},{8,9},{9,8},{10,11... | collective-permute-start | bytes 516104 | tf_op jit(solution)/shard_map/ppermute | solution.py:659
  71.6 2.7 %conv_back_one.1 = (bf16[24,96,128]{2,1,0:T(8,128)(2,1)S(1)}, f32[7,96,128]{2,1,0:T(8,128)S(1)}, f32[24,96,128]{2,1,0:T(8,128)S(1)}, f32[24,96,128]{2,1,0:T(8,128)S(1)}, f32[96,128]{1,0:T(8,128)S(1)}) custom-call(s32[1]{0:T(128)} %bitcast.refs_0_, f32[24,96,128]{2,1,0:T(8,128)S(1)} %get-tuple-element.136.refs_1_, ...), custom_call_target="tpu_custom_call" | custom-call | tf_op jit(solution)/shard_map/conv_back_one/pallas_call | solution.py:637
  74.8 4.7 %collective-permute-start.15 = (bf16[112,384]{1,0:T(8,128)(2,1)S(1)}, bf16[112,384]{1,0:T(8,128)(2,1)S(1)}, u32[]{:S(2)}, u32[]{:S(2)}) collective-permute-start(bf16[112,384]{1,0:T(8,128)(2,1)S(1)} %get-tuple-element.151), channel_id=1, source_target_pairs={{0,12},{1,13},{2,14},{3,15},{4,8},{5,9},{6,10},{7,11},{8,4},{9,5},... | collective-permute-start | bytes 258056 | tf_op jit(solution)/shard_map/ppermute | solution.py:672
  81.6 2.5 %collective-permute-start.7 = (bf16[24,96,128]{2,1,0:T(8,128)(2,1)S(1)}, bf16[24,96,128]{2,1,0:T(8,128)(2,1)S(1)}, u32[]{:S(2)}, u32[]{:S(2)}) collective-permute-start(bf16[24,96,128]{2,1,0:T(8,128)(2,1)S(1)} %get-tuple-element.142), channel_id=1, source_target_pairs={{0,1},{1,0},{2,3},{3,2},{4,5},{5,4},{6,7},{7,6},{8,9},{9,8},{10,11... | collective-permute-start | bytes 1769480 | tf_op jit(solution)/shard_map/ppermute | solution.py:659
  84.1 2.3 %taps_one.1.refs_4_.refs_0_ = f32[96,128]{1,0:T(8,128)S(1)} custom-call(s32[1]{0:T(128)} %bitcast.refs_0_, f32[24,96,128]{2,1,0:T(8,128)S(1)} %get-tuple-element.105.refs_3_.refs_1_, f32[24,96,128]{2,1,0:T(8,128)S(1)} %get-tuple-element.152.refs_2_, f32[24,96,128]{2,1,0:T(8,128)S(1)} %get-tuple-element.153.refs_3_, ...), custom_call_target="tpu_custom_call" | custom-call | tf_op jit(solution)/shard_map/taps_one/pallas_call | solution.py:637
  86.4 2.6 %collective-permute-start.18 = (bf16[16,384]{1,0:T(8,128)(2,1)S(1)}, bf16[16,384]{1,0:T(8,128)(2,1)S(1)}, u32[]{:S(2)}, u32[]{:S(2)}) collective-permute-start(bf16[16,384]{1,0:T(8,128)(2,1)S(1)} %get-tuple-element.160), channel_id=1, source_target_pairs={{0,12},{1,13},{2,14},{3,15},{4,8},{5,9},{6,10},{7,11},{8,4},{9,5},... | collective-permute-start | bytes 36872 | tf_op jit(solution)/shard_map/ppermute | solution.py:672
  89.0 1.8 %collective-permute-start.16 = (bf16[16,384]{1,0:T(8,128)(2,1)S(1)}, bf16[16,384]{1,0:T(8,128)(2,1)S(1)}, u32[]{:S(2)}, u32[]{:S(2)}) collective-permute-start(bf16[16,384]{1,0:T(8,128)(2,1)S(1)} %get-tuple-element.160), channel_id=1, source_target_pairs={{0,4},{1,5},{2,6},{3,7},{4,0},{5,1},{6,2},{7,3},{8,12},{9,13},{10,... | collective-permute-start | bytes 36872 | tf_op jit(solution)/shard_map/ppermute | solution.py:672
  90.9 4.0 %collective-permute-done.18.refs_4_ = bf16[16,384]{1,0:T(8,128)(2,1)S(1)} collective-permute-done((bf16[16,384]{1,0:T(8,128)(2,1)S(1)}, bf16[16,384]{1,0:T(8,128)(2,1)S(1)}, u32[]{:S(2)}, u32[]{:S(2)}) %collective-permute-start.18) | collective-permute-done | bytes 12320 | tf_op jit(solution)/shard_map/ppermute | solution.py:672
  95.1 1.5 %last.1 = (f32[2304,128]{1,0:T(8,128)}, f32[8,128]{1,0:T(8,128)S(1)}) custom-call(f32[24,96,128]{2,1,0:T(8,128)S(1)} %get-tuple-element.141.refs_6_.refs_0_, bf16[24,96,128]{2,1,0:T(8,128)(2,1)S(1)} %collective-permute-done.7.refs_1_, bf16[24,96,128]{2,1,0:T(8,128)(2,1)S(1)} %collective-permute-done.8.refs_2_, f32[240,384]{1,0:T(8,128)S(1)} %get-tuple-element.161.refs_3_.refs_0_), custom_call_target="tpu_custom_call" | custom-call | tf_op jit(solution)/shard_map/last/pallas_call | solution.py:637
  96.6 4.1 %collective-permute-done.19.refs_1_ = bf16[256,384]{1,0:T(8,128)(2,1)S(1)} collective-permute-done((bf16[256,384]{1,0:T(8,128)(2,1)S(1)}, bf16[256,384]{1,0:T(8,128)(2,1)S(1)}, u32[]{:S(2)}, u32[]{:S(2)}) %collective-permute-start.19) | collective-permute-done | bytes 196640 | tf_op jit(solution)/shard_map/ppermute | solution.py:672
  101.4 1.3 %collective-permute-done.20.refs_2_ = f32[240,384]{1,0:T(8,128)S(1)} collective-permute-done((f32[240,384]{1,0:T(8,128)S(1)}, f32[240,384]{1,0:T(8,128)S(1)}, u32[]{:S(2)}, u32[]{:S(2)}) %collective-permute-start.20) | collective-permute-done | bytes 368672 | tf_op jit(solution)/shard_map/ppermute | solution.py:659
  102.8 0.9 final.1
  (51 shorter events, 12.8 us)
Async XLA Ops:
  0.6 9.0 %copy-start = (bf16[96,3,8,128]{3,2,1,0:T(8,128)(2,1)S(1)}, bf16[96,3,8,128]{3,2,1,0:T(8,128)(2,1)}, u32[]{:S(2)}) copy-start(bf16[96,3,8,128]{3,2,1,0:T(8,128)(2,1)} %param.14) | copy-start | bytes 1769476
  0.7 8.9 %collective-permute-start.1 = (bf16[2304,128]{1,0:T(8,128)(2,1)}, bf16[2304,128]{1,0:T(8,128)(2,1)S(1)}, u32[]{:S(2)}, u32[]{:S(2)}) collective-permute-start(bf16[2304,128]{1,0:T(8,128)(2,1)} %bitcast.14), channel_id=1, source_target_pairs={{0,1},{1,0},{2,3},{3,2},{4,5},{5,4},{6,7},{7,6},{8,9},{9,8},{10,11... | collective-permute-start | bytes 1769480 | tf_op jit(solution)/shard_map/ppermute | solution.py:659
  1.2 9.6 %collective-permute-start = (bf16[2304,128]{1,0:T(8,128)(2,1)}, bf16[2304,128]{1,0:T(8,128)(2,1)S(1)}, u32[]{:S(2)}, u32[]{:S(2)}) collective-permute-start(bf16[2304,128]{1,0:T(8,128)(2,1)} %bitcast.15), channel_id=1, source_target_pairs={{1,2},{2,1},{3,4},{4,3},{5,6},{6,5},{7,8},{8,7},{9,10},{10,9},{11,... | collective-permute-start | bytes 1769480 | tf_op jit(solution)/shard_map/ppermute | solution.py:667
  6.1 0.9 copy-start.1
  7.0 0.7 copy-start.2
  14.9 12.6 %collective-permute-start.2 = (bf16[24,96,128]{2,1,0:T(8,128)(2,1)S(1)}, bf16[24,96,128]{2,1,0:T(8,128)(2,1)S(1)}, u32[]{:S(2)}, u32[]{:S(2)}) collective-permute-start(bf16[24,96,128]{2,1,0:T(8,128)(2,1)S(1)} %get-tuple-element.110.refs_1_.refs_3_), channel_id=1, source_target_pairs={{0,1},{1,0},{2,3},{3,2},{4,5},{5,4},{6,7},{7,6},{8,9},{9,8},{10,11... | collective-permute-start | bytes 1769480 | tf_op jit(solution)/shard_map/ppermute | solution.py:659
  23.5 4.6 %collective-permute-start.3 = (bf16[24,96,128]{2,1,0:T(8,128)(2,1)S(1)}, bf16[24,96,128]{2,1,0:T(8,128)(2,1)S(1)}, u32[]{:S(2)}, u32[]{:S(2)}) collective-permute-start(bf16[24,96,128]{2,1,0:T(8,128)(2,1)S(1)} %get-tuple-element.110.refs_1_.refs_3_), channel_id=1, source_target_pairs={{1,2},{2,1},{3,4},{4,3},{5,6},{6,5},{7,8},{8,7},{9,10},{10,9},{11,... | collective-permute-start | bytes 1769480 | tf_op jit(solution)/shard_map/ppermute | solution.py:667
  38.7 13.9 %collective-permute-start.4 = (f32[112,384]{1,0:T(8,128)S(1)}, f32[112,384]{1,0:T(8,128)S(1)}, u32[]{:S(2)}, u32[]{:S(2)}) collective-permute-start(f32[112,384]{1,0:T(8,128)S(1)} %get-tuple-element.129), channel_id=1, source_target_pairs={{0,1},{1,0},{2,3},{3,2},{4,5},{5,4},{6,7},{7,6},{8,9},{9,8},{10,11... | collective-permute-start | bytes 516104 | tf_op jit(solution)/shard_map/ppermute | solution.py:659
  51.6 11.9 %collective-permute-start.6 = (bf16[24,96,128]{2,1,0:T(8,128)(2,1)S(1)}, bf16[24,96,128]{2,1,0:T(8,128)(2,1)S(1)}, u32[]{:S(2)}, u32[]{:S(2)}) collective-permute-start(bf16[24,96,128]{2,1,0:T(8,128)(2,1)S(1)} %get-tuple-element.132), channel_id=1, source_target_pairs={{1,2},{2,1},{3,4},{4,3},{5,6},{6,5},{7,8},{8,7},{9,10},{10,9},{11,... | collective-permute-start | bytes 1769480 | tf_op jit(solution)/shard_map/ppermute | solution.py:667
  55.3 8.2 %collective-permute-start.5 = (bf16[24,96,128]{2,1,0:T(8,128)(2,1)S(1)}, bf16[24,96,128]{2,1,0:T(8,128)(2,1)S(1)}, u32[]{:S(2)}, u32[]{:S(2)}) collective-permute-start(bf16[24,96,128]{2,1,0:T(8,128)(2,1)S(1)} %get-tuple-element.131), channel_id=1, source_target_pairs={{0,1},{1,0},{2,3},{3,2},{4,5},{5,4},{6,7},{7,6},{8,9},{9,8},{10,11... | collective-permute-start | bytes 1769480 | tf_op jit(solution)/shard_map/ppermute | solution.py:659
  59.1 15.3 %collective-permute-start.12 = (bf16[128,384]{1,0:T(8,128)(2,1)S(1)}, bf16[128,384]{1,0:T(8,128)(2,1)S(1)}, u32[]{:S(2)}, u32[]{:S(2)}) collective-permute-start(bf16[128,384]{1,0:T(8,128)(2,1)S(1)} %get-tuple-element.149), channel_id=1, source_target_pairs={{0,12},{1,13},{2,14},{3,15},{4,8},{5,9},{6,10},{7,11},{8,4},{9,5},... | collective-permute-start | bytes 294920 | tf_op jit(solution)/shard_map/ppermute | solution.py:672
  62.6 12.1 %collective-permute-start.11 = (bf16[128,384]{1,0:T(8,128)(2,1)S(1)}, bf16[128,384]{1,0:T(8,128)(2,1)S(1)}, u32[]{:S(2)}, u32[]{:S(2)}) collective-permute-start(bf16[128,384]{1,0:T(8,128)(2,1)S(1)} %get-tuple-element.149), channel_id=1, source_target_pairs={{0,8},{1,9},{2,10},{3,11},{4,12},{5,13},{6,14},{7,15},{8,0},{9,1},... | collective-permute-start | bytes 294920 | tf_op jit(solution)/shard_map/ppermute | solution.py:672
  62.6 12.1 %collective-permute-start.10 = (bf16[128,384]{1,0:T(8,128)(2,1)S(1)}, bf16[128,384]{1,0:T(8,128)(2,1)S(1)}, u32[]{:S(2)}, u32[]{:S(2)}) collective-permute-start(bf16[128,384]{1,0:T(8,128)(2,1)S(1)} %get-tuple-element.149), channel_id=1, source_target_pairs={{0,4},{1,5},{2,6},{3,7},{4,0},{5,1},{6,2},{7,3},{8,12},{9,13},{10,... | collective-permute-start | bytes 294920 | tf_op jit(solution)/shard_map/ppermute | solution.py:672
  66.0 8.8 %collective-permute-start.9 = (f32[112,384]{1,0:T(8,128)S(1)}, f32[112,384]{1,0:T(8,128)S(1)}, u32[]{:S(2)}, u32[]{:S(2)}) collective-permute-start(f32[112,384]{1,0:T(8,128)S(1)} %get-tuple-element.145), channel_id=1, source_target_pairs={{0,1},{1,0},{2,3},{3,2},{4,5},{5,4},{6,7},{7,6},{8,9},{9,8},{10,11... | collective-permute-start | bytes 516104 | tf_op jit(solution)/shard_map/ppermute | solution.py:659
  74.8 11.6 %collective-permute-start.15 = (bf16[112,384]{1,0:T(8,128)(2,1)S(1)}, bf16[112,384]{1,0:T(8,128)(2,1)S(1)}, u32[]{:S(2)}, u32[]{:S(2)}) collective-permute-start(bf16[112,384]{1,0:T(8,128)(2,1)S(1)} %get-tuple-element.151), channel_id=1, source_target_pairs={{0,12},{1,13},{2,14},{3,15},{4,8},{5,9},{6,10},{7,11},{8,4},{9,5},... | collective-permute-start | bytes 258056 | tf_op jit(solution)/shard_map/ppermute | solution.py:672
  79.6 9.5 %collective-permute-start.14 = (bf16[112,384]{1,0:T(8,128)(2,1)S(1)}, bf16[112,384]{1,0:T(8,128)(2,1)S(1)}, u32[]{:S(2)}, u32[]{:S(2)}) collective-permute-start(bf16[112,384]{1,0:T(8,128)(2,1)S(1)} %get-tuple-element.151), channel_id=1, source_target_pairs={{0,8},{1,9},{2,10},{3,11},{4,12},{5,13},{6,14},{7,15},{8,0},{9,1},... | collective-permute-start | bytes 258056 | tf_op jit(solution)/shard_map/ppermute | solution.py:672
  79.6 9.5 %collective-permute-start.13 = (bf16[112,384]{1,0:T(8,128)(2,1)S(1)}, bf16[112,384]{1,0:T(8,128)(2,1)S(1)}, u32[]{:S(2)}, u32[]{:S(2)}) collective-permute-start(bf16[112,384]{1,0:T(8,128)(2,1)S(1)} %get-tuple-element.151), channel_id=1, source_target_pairs={{0,4},{1,5},{2,6},{3,7},{4,0},{5,1},{6,2},{7,3},{8,12},{9,13},{10,... | collective-permute-start | bytes 258056 | tf_op jit(solution)/shard_map/ppermute | solution.py:672
  80.9 14.2 %collective-permute-start.8 = (bf16[24,96,128]{2,1,0:T(8,128)(2,1)S(1)}, bf16[24,96,128]{2,1,0:T(8,128)(2,1)S(1)}, u32[]{:S(2)}, u32[]{:S(2)}) collective-permute-start(bf16[24,96,128]{2,1,0:T(8,128)(2,1)S(1)} %get-tuple-element.143), channel_id=1, source_target_pairs={{1,2},{2,1},{3,4},{4,3},{5,6},{6,5},{7,8},{8,7},{9,10},{10,9},{11,... | collective-permute-start | bytes 1769480 | tf_op jit(solution)/shard_map/ppermute | solution.py:667
  81.6 13.5 %collective-permute-start.7 = (bf16[24,96,128]{2,1,0:T(8,128)(2,1)S(1)}, bf16[24,96,128]{2,1,0:T(8,128)(2,1)S(1)}, u32[]{:S(2)}, u32[]{:S(2)}) collective-permute-start(bf16[24,96,128]{2,1,0:T(8,128)(2,1)S(1)} %get-tuple-element.142), channel_id=1, source_target_pairs={{0,1},{1,0},{2,3},{3,2},{4,5},{5,4},{6,7},{7,6},{8,9},{9,8},{10,11... | collective-permute-start | bytes 1769480 | tf_op jit(solution)/shard_map/ppermute | solution.py:659
  86.4 8.5 %collective-permute-start.18 = (bf16[16,384]{1,0:T(8,128)(2,1)S(1)}, bf16[16,384]{1,0:T(8,128)(2,1)S(1)}, u32[]{:S(2)}, u32[]{:S(2)}) collective-permute-start(bf16[16,384]{1,0:T(8,128)(2,1)S(1)} %get-tuple-element.160), channel_id=1, source_target_pairs={{0,12},{1,13},{2,14},{3,15},{4,8},{5,9},{6,10},{7,11},{8,4},{9,5},... | collective-permute-start | bytes 36872 | tf_op jit(solution)/shard_map/ppermute | solution.py:672
  89.0 5.9 %collective-permute-start.17 = (bf16[16,384]{1,0:T(8,128)(2,1)S(1)}, bf16[16,384]{1,0:T(8,128)(2,1)S(1)}, u32[]{:S(2)}, u32[]{:S(2)}) collective-permute-start(bf16[16,384]{1,0:T(8,128)(2,1)S(1)} %get-tuple-element.160), channel_id=1, source_target_pairs={{0,8},{1,9},{2,10},{3,11},{4,12},{5,13},{6,14},{7,15},{8,0},{9,1},... | collective-permute-start | bytes 36872 | tf_op jit(solution)/shard_map/ppermute | solution.py:672
  89.0 5.9 %collective-permute-start.16 = (bf16[16,384]{1,0:T(8,128)(2,1)S(1)}, bf16[16,384]{1,0:T(8,128)(2,1)S(1)}, u32[]{:S(2)}, u32[]{:S(2)}) collective-permute-start(bf16[16,384]{1,0:T(8,128)(2,1)S(1)} %get-tuple-element.160), channel_id=1, source_target_pairs={{0,4},{1,5},{2,6},{3,7},{4,0},{5,1},{6,2},{7,3},{8,12},{9,13},{10,... | collective-permute-start | bytes 36872 | tf_op jit(solution)/shard_map/ppermute | solution.py:672
  95.0 5.7 %collective-permute-start.19 = (bf16[256,384]{1,0:T(8,128)(2,1)S(1)}, bf16[256,384]{1,0:T(8,128)(2,1)S(1)}, u32[]{:S(2)}, u32[]{:S(2)}) collective-permute-start(bf16[256,384]{1,0:T(8,128)(2,1)S(1)} %get-tuple-element.163), channel_id=1, source_target_pairs={{0,2},{1,3},{2,0},{3,1},{4,6},{5,7},{6,4},{7,5},{8,10},{9,11},{10,... | collective-permute-start | bytes 589832 | tf_op jit(solution)/shard_map/ppermute | solution.py:672
  100.8 2.0 %collective-permute-start.20 = (f32[240,384]{1,0:T(8,128)S(1)}, f32[240,384]{1,0:T(8,128)S(1)}, u32[]{:S(2)}, u32[]{:S(2)}) collective-permute-start(f32[240,384]{1,0:T(8,128)S(1)} %sums_last.1.refs_1_), channel_id=1, source_target_pairs={{0,1},{1,0},{2,3},{3,2},{4,5},{5,4},{6,7},{7,6},{8,9},{9,8},{10,11... | collective-permute-start | bytes 1105928 | tf_op jit(solution)/shard_map/ppermute | solution.py:659

commit v7 on v6

--- a/solution.py
+++ b/solution.py
@@ -85,16 +85,11 @@
     return found
 
 
-def unpack(source, wide, out, first=0):
+def unpack(source, wide, out):
     wide[...] = source[...].astype(F32)
-
-    def one(group, carry):
-        rows = group_rows(group)
+    for first in range(0, out.shape[1], ROWS):
         for tile in range(OWN):
-            out[first + tile, rows, :] = wide[pl.ds(group * ROWS * OWN + tile, ROWS, stride=OWN), :]
-        return carry
-
-    lax.fori_loop(0, out.shape[1] // ROWS, one, 0)
+            out[tile, first : first + ROWS, :] = wide[pl.ds(first * OWN + tile, ROWS, stride=OWN), :]
 
 
 def widen(source, ext, first, count):
@@ -592,13 +587,9 @@
 
     lax.fori_loop(0, OWN, add, 0, unroll=2)
 
-    def one(group, carry):
-        rows = group_rows(group)
+    for first in range(0, inner.shape[1], ROWS):
         for tile in range(OWN):
-            out[pl.ds(group * ROWS * OWN + tile, ROWS, stride=OWN), :] = total[tile, rows, :]
-        return carry
-
-    lax.fori_loop(0, inner.shape[1] // ROWS, one, 0)
+            out[pl.ds(first * OWN + tile, ROWS, stride=OWN), :] = total[tile, first : first + ROWS, :]
 
 
 def final_kernel(share, par, mine, other, g_in_t, g_bias, g_out, g_taps, g_gain, g_scale, g_head, g_head_b):

time: 104 us -> 104 us (level)
  transfers between devices with their start and end apart: 21 -> 21, of which waited for: 5 -> 5; matrix products, arithmetic and copies ran while one was open for 4% -> 4% of each run, Pallas kernels for 19% -> 18%
where the time goes in v7:
time: 104 us
  starting transfers between devices  51.9 us (50%)
  Pallas kernels  34.9 us (34%)
  waiting for transfers between devices  10.1 us (10%)
  local copies, waits for them, and re-layouts  5.05 us (5%)
    pallas_call x20, Pallas kernels, call(): pl.pallas_call(run, name=name, out_shape=tuple(outs), in_specs=in_specs +...  34.9 us
    ppermute x7, starting transfers between devices, near_swap(): return lax.ppermute(value, 'track', [(i, i ^ 1) for i in range(count)])  34.4 us
    ppermute x10, starting transfers between devices, bit_swap(): return lax.ppermute(value, 'track', [(i, i ^ step) for i in range(count)])  14.3 us
    ppermute x10, waiting for transfers between devices, bit_swap(): return lax.ppermute(value, 'track', [(i, i ^ step) for i in range(count)])  8.64 us
    unnamed x8, local copies, waits for them, and re-layouts  3.51 us
    ppermute x4, starting transfers between devices, far_swap(): return lax.ppermute(value, 'track', pairs)  3.16 us
  transfers between devices with their start and end apart: 21, of which 5 were waited for; matrix products, arithmetic and copies ran while one was open for 4% of the time, Pallas kernels for 18%

profile of v7, /device:TPU:0, one launch (start us, length us, event | category | flops | bytes accessed | tf_op | source)
XLA Modules:
  0.0 103.7 jit_solution(15946918293651588419)
XLA Ops:
  3.5 1.1 %copy.32.refs_2_ = bf16[2,384,96]{2,1,0:T(8,128)(2,1)S(1)} copy(bf16[2,384,96]{1,2,0:T(8,128)(2,1)} %param.18) | data formatting | bytes 294912 | tf_op args[4]
  7.7 1.9 %tables.1 = (f32[2,28,96,128]{3,2,1,0:T(8,128)S(1)}, f32[2,96,23]{2,1,0:T(8,128)S(1)}, f32[384,2]{1,0:T(8,128)S(1)}, bf16[2,384,96]{2,1,0:T(8,128)(2,1)S(1)}, bf...) custom-call(f32[2,96,23]{2,1,0:T(8,128)S(1)} %bitcast.17, ...), custom_call_target="tpu_custom_call" | custom-call | tf_op jit(solution)/shard_map/tables/pallas_call | solution.py:628
  9.6 1.1 %start_one.1 = (f32[24,96,128]{2,1,0:T(8,128)S(1)}, f32[24,96,128]{2,1,0:T(8,128)S(1)}, f32[24,96,128]{2,1,0:T(8,128)S(1)}) custom-call(s32[1]{0:T(128)} %bitcast.refs_0_, bf16[2304,128]{1,0:T(8,128)(2,1)S(1)} %bitcast.16, bf16[2304,128]{1,0:T(8,128)(2,1)S(1)} %collective-permute-done.1.refs_2_, ...), custom_call_target="tpu_custom_call" | custom-call | tf_op jit(solution)/shard_map/start_one/pallas_call | solution.py:628
  10.7 4.1 %forward_one.1 = (bf16[24,96,128]{2,1,0:T(8,128)(2,1)S(1)}, f32[24,96,128]{2,1,0:T(8,128)S(1)}, f32[24,96,128]{2,1,0:T(8,128)S(1)}, f32[24,96,128]{2,1,0:T(8,128)S(1)}, f32[24,96,128]{2,1,0:T(8,128)S(1)}) custom-call(s32[1]{0:T(128)} %bitcast.refs_0_, bf16[2304,128]{1,0:T(8,128)(2,1)S(1)} %collective-permute-done.refs_1_, ...), custom_call_target="tpu_custom_call" | custom-call | tf_op jit(solution)/shard_map/forward_one/pallas_call | solution.py:628
  14.8 8.6 %collective-permute-start.2 = (bf16[24,96,128]{2,1,0:T(8,128)(2,1)S(1)}, bf16[24,96,128]{2,1,0:T(8,128)(2,1)S(1)}, u32[]{:S(2)}, u32[]{:S(2)}) collective-permute-start(bf16[24,96,128]{2,1,0:T(8,128)(2,1)S(1)} %get-tuple-element.110.refs_1_.refs_3_), channel_id=1, source_target_pairs={{0,1},{1,0},{2,3},{3,2},{4,5},{5,4},{6,7},{7,6},{8,9},{9,8},{10,11... | collective-permute-start | bytes 1769480 | tf_op jit(solution)/shard_map/ppermute | solution.py:650
  24.3 3.1 %save_one.1 = (bf16[24,96,128]{2,1,0:T(8,128)(2,1)S(1)}, f32[24,96,128]{2,1,0:T(8,128)S(1)}, f32[2,1,1536]{2,1,0:T(1,128)S(1)}, bf16[2,384,1536]{2,1,0:T(8,128)(2,1)S(1)}, f32[2,384,1536]{2,1,0:T(8,128)S(1)}) custom-call(f32[24,96,128]{2,1,0:T(8,128)S(1)} %get-tuple-element.111.refs_0_, f32[2,96,23]{2,1,0:T(8,128)S(1)} %get-tuple-element.106.refs_4_.refs_1_.refs_5_.refs_7_, ...), custom_call_target="tpu_custom_call" | custom-call | tf_op jit(solution)/shard_map/save_one/pallas_call | solution.py:628
  28.0 10.7 %turn_two.1 = (bf16[24,96,128]{2,1,0:T(8,128)(2,1)S(1)}, f32[24,96,128]{2,1,0:T(8,128)S(1)}, f32[7,96,128]{2,1,0:T(8,128)S(1)}, f32[24,96,128]{2,1,0:T(8,128)S(1...) custom-call(s32[1]{0:T(128)} %bitcast.refs_0_, ...), custom_call_target="tpu_custom_call" | custom-call | tf_op jit(solution)/shard_map/turn_two/pallas_call | solution.py:628
  38.7 12.8 %collective-permute-start.4 = (f32[112,384]{1,0:T(8,128)S(1)}, f32[112,384]{1,0:T(8,128)S(1)}, u32[]{:S(2)}, u32[]{:S(2)}) collective-permute-start(f32[112,384]{1,0:T(8,128)S(1)} %get-tuple-element.129), channel_id=1, source_target_pairs={{0,1},{1,0},{2,3},{3,2},{4,5},{5,4},{6,7},{7,6},{8,9},{9,8},{10,11... | collective-permute-start | bytes 516104 | tf_op jit(solution)/shard_map/ppermute | solution.py:650
  52.6 2.7 %taps_two.1 = (f32[96,128]{1,0:T(8,128)S(1)}, f32[24,96,128]{2,1,0:T(8,128)S(1)}, bf16[24,96,128]{2,1,0:T(8,128)(2,1)S(1)}) custom-call(s32[1]{0:T(128)} %bitcast.refs_0_, bf16[24,96,128]{2,1,0:T(8,128)(2,1)S(1)} %get-tuple-element.110.refs_1_.refs_3_, bf16[24,96,128]{2,1,0:T(8,128)(2,1)S(1)} %collective-permute-done.2.refs_2_, ...), custom_call_target="tpu_custom_call" | custom-call | tf_op jit(solution)/shard_map/taps_two/pallas_call | solution.py:628
  55.3 3.7 %collective-permute-start.5 = (bf16[24,96,128]{2,1,0:T(8,128)(2,1)S(1)}, bf16[24,96,128]{2,1,0:T(8,128)(2,1)S(1)}, u32[]{:S(2)}, u32[]{:S(2)}) collective-permute-start(bf16[24,96,128]{2,1,0:T(8,128)(2,1)S(1)} %get-tuple-element.131), channel_id=1, source_target_pairs={{0,1},{1,0},{2,3},{3,2},{4,5},{5,4},{6,7},{7,6},{8,9},{9,8},{10,11... | collective-permute-start | bytes 1769480 | tf_op jit(solution)/shard_map/ppermute | solution.py:650
  59.0 3.5 %collective-permute-start.12 = (bf16[128,384]{1,0:T(8,128)(2,1)S(1)}, bf16[128,384]{1,0:T(8,128)(2,1)S(1)}, u32[]{:S(2)}, u32[]{:S(2)}) collective-permute-start(bf16[128,384]{1,0:T(8,128)(2,1)S(1)} %get-tuple-element.149), channel_id=1, source_target_pairs={{0,12},{1,13},{2,14},{3,15},{4,8},{5,9},{6,10},{7,11},{8,4},{9,5},... | collective-permute-start | bytes 294920 | tf_op jit(solution)/shard_map/ppermute | solution.py:663
  63.4 2.5 %point_back_one.1 = (f32[24,96,128]{2,1,0:T(8,128)S(1)}, f32[24,96,128]{2,1,0:T(8,128)S(1)}, f32[112,384]{1,0:T(8,128)S(1)}, f32[112,384]{1,0:T(8,128)S(1)}, f32[96,1]{1,0:T(8,128)S(1)}) custom-call(s32[1]{0:T(128)} %bitcast.refs_0_, f32[24,96,128]{2,1,0:T(8,128)S(1)} %get-tuple-element.130.refs_1_.refs_3_, ...), custom_call_target="tpu_custom_call" | custom-call | tf_op jit(solution)/shard_map/point_back_one/pallas_call | solution.py:628
  65.9 5.7 %collective-permute-start.9 = (f32[112,384]{1,0:T(8,128)S(1)}, f32[112,384]{1,0:T(8,128)S(1)}, u32[]{:S(2)}, u32[]{:S(2)}) collective-permute-start(f32[112,384]{1,0:T(8,128)S(1)} %get-tuple-element.145), channel_id=1, source_target_pairs={{0,1},{1,0},{2,3},{3,2},{4,5},{5,4},{6,7},{7,6},{8,9},{9,8},{10,11... | collective-permute-start | bytes 516104 | tf_op jit(solution)/shard_map/ppermute | solution.py:650
  71.6 2.7 %conv_back_one.1 = (bf16[24,96,128]{2,1,0:T(8,128)(2,1)S(1)}, f32[7,96,128]{2,1,0:T(8,128)S(1)}, f32[24,96,128]{2,1,0:T(8,128)S(1)}, f32[24,96,128]{2,1,0:T(8,128)S(1)}, f32[96,128]{1,0:T(8,128)S(1)}) custom-call(s32[1]{0:T(128)} %bitcast.refs_0_, f32[24,96,128]{2,1,0:T(8,128)S(1)} %get-tuple-element.136.refs_1_, ...), custom_call_target="tpu_custom_call" | custom-call | tf_op jit(solution)/shard_map/conv_back_one/pallas_call | solution.py:628
  74.8 4.7 %collective-permute-start.15 = (bf16[112,384]{1,0:T(8,128)(2,1)S(1)}, bf16[112,384]{1,0:T(8,128)(2,1)S(1)}, u32[]{:S(2)}, u32[]{:S(2)}) collective-permute-start(bf16[112,384]{1,0:T(8,128)(2,1)S(1)} %get-tuple-element.151), channel_id=1, source_target_pairs={{0,12},{1,13},{2,14},{3,15},{4,8},{5,9},{6,10},{7,11},{8,4},{9,5},... | collective-permute-start | bytes 258056 | tf_op jit(solution)/shard_map/ppermute | solution.py:663
  81.5 2.5 %collective-permute-start.7 = (bf16[24,96,128]{2,1,0:T(8,128)(2,1)S(1)}, bf16[24,96,128]{2,1,0:T(8,128)(2,1)S(1)}, u32[]{:S(2)}, u32[]{:S(2)}) collective-permute-start(bf16[24,96,128]{2,1,0:T(8,128)(2,1)S(1)} %get-tuple-element.142), channel_id=1, source_target_pairs={{0,1},{1,0},{2,3},{3,2},{4,5},{5,4},{6,7},{7,6},{8,9},{9,8},{10,11... | collective-permute-start | bytes 1769480 | tf_op jit(solution)/shard_map/ppermute | solution.py:650
  84.0 2.3 %taps_one.1.refs_4_.refs_0_ = f32[96,128]{1,0:T(8,128)S(1)} custom-call(s32[1]{0:T(128)} %bitcast.refs_0_, f32[24,96,128]{2,1,0:T(8,128)S(1)} %get-tuple-element.105.refs_3_.refs_1_, f32[24,96,128]{2,1,0:T(8,128)S(1)} %get-tuple-element.152.refs_2_, f32[24,96,128]{2,1,0:T(8,128)S(1)} %get-tuple-element.153.refs_3_, ...), custom_call_target="tpu_custom_call" | custom-call | tf_op jit(solution)/shard_map/taps_one/pallas_call | solution.py:628
  86.4 2.6 %collective-permute-start.18 = (bf16[16,384]{1,0:T(8,128)(2,1)S(1)}, bf16[16,384]{1,0:T(8,128)(2,1)S(1)}, u32[]{:S(2)}, u32[]{:S(2)}) collective-permute-start(bf16[16,384]{1,0:T(8,128)(2,1)S(1)} %get-tuple-element.160), channel_id=1, source_target_pairs={{0,12},{1,13},{2,14},{3,15},{4,8},{5,9},{6,10},{7,11},{8,4},{9,5},... | collective-permute-start | bytes 36872 | tf_op jit(solution)/shard_map/ppermute | solution.py:663
  89.0 1.8 %collective-permute-start.16 = (bf16[16,384]{1,0:T(8,128)(2,1)S(1)}, bf16[16,384]{1,0:T(8,128)(2,1)S(1)}, u32[]{:S(2)}, u32[]{:S(2)}) collective-permute-start(bf16[16,384]{1,0:T(8,128)(2,1)S(1)} %get-tuple-element.160), channel_id=1, source_target_pairs={{0,4},{1,5},{2,6},{3,7},{4,0},{5,1},{6,2},{7,3},{8,12},{9,13},{10,... | collective-permute-start | bytes 36872 | tf_op jit(solution)/shard_map/ppermute | solution.py:663
  90.9 4.0 %collective-permute-done.18.refs_4_ = bf16[16,384]{1,0:T(8,128)(2,1)S(1)} collective-permute-done((bf16[16,384]{1,0:T(8,128)(2,1)S(1)}, bf16[16,384]{1,0:T(8,128)(2,1)S(1)}, u32[]{:S(2)}, u32[]{:S(2)}) %collective-permute-start.18) | collective-permute-done | bytes 12320 | tf_op jit(solution)/shard_map/ppermute | solution.py:663
  95.1 1.4 %last.1 = (f32[2304,128]{1,0:T(8,128)}, f32[8,128]{1,0:T(8,128)S(1)}) custom-call(f32[24,96,128]{2,1,0:T(8,128)S(1)} %get-tuple-element.141.refs_6_.refs_0_, bf16[24,96,128]{2,1,0:T(8,128)(2,1)S(1)} %collective-permute-done.7.refs_1_, bf16[24,96,128]{2,1,0:T(8,128)(2,1)S(1)} %collective-permute-done.8.refs_2_, f32[240,384]{1,0:T(8,128)S(1)} %get-tuple-element.161.refs_3_.refs_0_), custom_call_target="tpu_custom_call" | custom-call | tf_op jit(solution)/shard_map/last/pallas_call | solution.py:628
  96.5 4.2 %collective-permute-done.19.refs_1_ = bf16[256,384]{1,0:T(8,128)(2,1)S(1)} collective-permute-done((bf16[256,384]{1,0:T(8,128)(2,1)S(1)}, bf16[256,384]{1,0:T(8,128)(2,1)S(1)}, u32[]{:S(2)}, u32[]{:S(2)}) %collective-permute-start.19) | collective-permute-done | bytes 196640 | tf_op jit(solution)/shard_map/ppermute | solution.py:663
  101.4 1.3 %collective-permute-done.20.refs_2_ = f32[240,384]{1,0:T(8,128)S(1)} collective-permute-done((f32[240,384]{1,0:T(8,128)S(1)}, f32[240,384]{1,0:T(8,128)S(1)}, u32[]{:S(2)}, u32[]{:S(2)}) %collective-permute-start.20) | collective-permute-done | bytes 368672 | tf_op jit(solution)/shard_map/ppermute | solution.py:650
  102.7 0.9 final.1
  (51 shorter events, 12.8 us)
Async XLA Ops:
  0.6 9.0 %copy-start = (bf16[96,3,8,128]{3,2,1,0:T(8,128)(2,1)S(1)}, bf16[96,3,8,128]{3,2,1,0:T(8,128)(2,1)}, u32[]{:S(2)}) copy-start(bf16[96,3,8,128]{3,2,1,0:T(8,128)(2,1)} %param.14) | copy-start | bytes 1769476
  0.7 8.9 %collective-permute-start.1 = (bf16[2304,128]{1,0:T(8,128)(2,1)}, bf16[2304,128]{1,0:T(8,128)(2,1)S(1)}, u32[]{:S(2)}, u32[]{:S(2)}) collective-permute-start(bf16[2304,128]{1,0:T(8,128)(2,1)} %bitcast.14), channel_id=1, source_target_pairs={{0,1},{1,0},{2,3},{3,2},{4,5},{5,4},{6,7},{7,6},{8,9},{9,8},{10,11... | collective-permute-start | bytes 1769480 | tf_op jit(solution)/shard_map/ppermute | solution.py:650
  1.2 9.6 %collective-permute-start = (bf16[2304,128]{1,0:T(8,128)(2,1)}, bf16[2304,128]{1,0:T(8,128)(2,1)S(1)}, u32[]{:S(2)}, u32[]{:S(2)}) collective-permute-start(bf16[2304,128]{1,0:T(8,128)(2,1)} %bitcast.15), channel_id=1, source_target_pairs={{1,2},{2,1},{3,4},{4,3},{5,6},{6,5},{7,8},{8,7},{9,10},{10,9},{11,... | collective-permute-start | bytes 1769480 | tf_op jit(solution)/shard_map/ppermute | solution.py:658
  6.1 0.9 copy-start.1
  7.0 0.7 copy-start.2
  14.8 12.6 %collective-permute-start.2 = (bf16[24,96,128]{2,1,0:T(8,128)(2,1)S(1)}, bf16[24,96,128]{2,1,0:T(8,128)(2,1)S(1)}, u32[]{:S(2)}, u32[]{:S(2)}) collective-permute-start(bf16[24,96,128]{2,1,0:T(8,128)(2,1)S(1)} %get-tuple-element.110.refs_1_.refs_3_), channel_id=1, source_target_pairs={{0,1},{1,0},{2,3},{3,2},{4,5},{5,4},{6,7},{7,6},{8,9},{9,8},{10,11... | collective-permute-start | bytes 1769480 | tf_op jit(solution)/shard_map/ppermute | solution.py:650
  23.4 4.6 %collective-permute-start.3 = (bf16[24,96,128]{2,1,0:T(8,128)(2,1)S(1)}, bf16[24,96,128]{2,1,0:T(8,128)(2,1)S(1)}, u32[]{:S(2)}, u32[]{:S(2)}) collective-permute-start(bf16[24,96,128]{2,1,0:T(8,128)(2,1)S(1)} %get-tuple-element.110.refs_1_.refs_3_), channel_id=1, source_target_pairs={{1,2},{2,1},{3,4},{4,3},{5,6},{6,5},{7,8},{8,7},{9,10},{10,9},{11,... | collective-permute-start | bytes 1769480 | tf_op jit(solution)/shard_map/ppermute | solution.py:658
  38.7 13.9 %collective-permute-start.4 = (f32[112,384]{1,0:T(8,128)S(1)}, f32[112,384]{1,0:T(8,128)S(1)}, u32[]{:S(2)}, u32[]{:S(2)}) collective-permute-start(f32[112,384]{1,0:T(8,128)S(1)} %get-tuple-element.129), channel_id=1, source_target_pairs={{0,1},{1,0},{2,3},{3,2},{4,5},{5,4},{6,7},{7,6},{8,9},{9,8},{10,11... | collective-permute-start | bytes 516104 | tf_op jit(solution)/shard_map/ppermute | solution.py:650
  51.5 11.9 %collective-permute-start.6 = (bf16[24,96,128]{2,1,0:T(8,128)(2,1)S(1)}, bf16[24,96,128]{2,1,0:T(8,128)(2,1)S(1)}, u32[]{:S(2)}, u32[]{:S(2)}) collective-permute-start(bf16[24,96,128]{2,1,0:T(8,128)(2,1)S(1)} %get-tuple-element.132), channel_id=1, source_target_pairs={{1,2},{2,1},{3,4},{4,3},{5,6},{6,5},{7,8},{8,7},{9,10},{10,9},{11,... | collective-permute-start | bytes 1769480 | tf_op jit(solution)/shard_map/ppermute | solution.py:658
  55.3 8.2 %collective-permute-start.5 = (bf16[24,96,128]{2,1,0:T(8,128)(2,1)S(1)}, bf16[24,96,128]{2,1,0:T(8,128)(2,1)S(1)}, u32[]{:S(2)}, u32[]{:S(2)}) collective-permute-start(bf16[24,96,128]{2,1,0:T(8,128)(2,1)S(1)} %get-tuple-element.131), channel_id=1, source_target_pairs={{0,1},{1,0},{2,3},{3,2},{4,5},{5,4},{6,7},{7,6},{8,9},{9,8},{10,11... | collective-permute-start | bytes 1769480 | tf_op jit(solution)/shard_map/ppermute | solution.py:650
  59.0 15.3 %collective-permute-start.12 = (bf16[128,384]{1,0:T(8,128)(2,1)S(1)}, bf16[128,384]{1,0:T(8,128)(2,1)S(1)}, u32[]{:S(2)}, u32[]{:S(2)}) collective-permute-start(bf16[128,384]{1,0:T(8,128)(2,1)S(1)} %get-tuple-element.149), channel_id=1, source_target_pairs={{0,12},{1,13},{2,14},{3,15},{4,8},{5,9},{6,10},{7,11},{8,4},{9,5},... | collective-permute-start | bytes 294920 | tf_op jit(solution)/shard_map/ppermute | solution.py:663
  62.5 12.1 %collective-permute-start.11 = (bf16[128,384]{1,0:T(8,128)(2,1)S(1)}, bf16[128,384]{1,0:T(8,128)(2,1)S(1)}, u32[]{:S(2)}, u32[]{:S(2)}) collective-permute-start(bf16[128,384]{1,0:T(8,128)(2,1)S(1)} %get-tuple-element.149), channel_id=1, source_target_pairs={{0,8},{1,9},{2,10},{3,11},{4,12},{5,13},{6,14},{7,15},{8,0},{9,1},... | collective-permute-start | bytes 294920 | tf_op jit(solution)/shard_map/ppermute | solution.py:663
  62.5 12.1 %collective-permute-start.10 = (bf16[128,384]{1,0:T(8,128)(2,1)S(1)}, bf16[128,384]{1,0:T(8,128)(2,1)S(1)}, u32[]{:S(2)}, u32[]{:S(2)}) collective-permute-start(bf16[128,384]{1,0:T(8,128)(2,1)S(1)} %get-tuple-element.149), channel_id=1, source_target_pairs={{0,4},{1,5},{2,6},{3,7},{4,0},{5,1},{6,2},{7,3},{8,12},{9,13},{10,... | collective-permute-start | bytes 294920 | tf_op jit(solution)/shard_map/ppermute | solution.py:663
  65.9 8.8 %collective-permute-start.9 = (f32[112,384]{1,0:T(8,128)S(1)}, f32[112,384]{1,0:T(8,128)S(1)}, u32[]{:S(2)}, u32[]{:S(2)}) collective-permute-start(f32[112,384]{1,0:T(8,128)S(1)} %get-tuple-element.145), channel_id=1, source_target_pairs={{0,1},{1,0},{2,3},{3,2},{4,5},{5,4},{6,7},{7,6},{8,9},{9,8},{10,11... | collective-permute-start | bytes 516104 | tf_op jit(solution)/shard_map/ppermute | solution.py:650
  74.8 11.6 %collective-permute-start.15 = (bf16[112,384]{1,0:T(8,128)(2,1)S(1)}, bf16[112,384]{1,0:T(8,128)(2,1)S(1)}, u32[]{:S(2)}, u32[]{:S(2)}) collective-permute-start(bf16[112,384]{1,0:T(8,128)(2,1)S(1)} %get-tuple-element.151), channel_id=1, source_target_pairs={{0,12},{1,13},{2,14},{3,15},{4,8},{5,9},{6,10},{7,11},{8,4},{9,5},... | collective-permute-start | bytes 258056 | tf_op jit(solution)/shard_map/ppermute | solution.py:663
  79.5 9.5 %collective-permute-start.14 = (bf16[112,384]{1,0:T(8,128)(2,1)S(1)}, bf16[112,384]{1,0:T(8,128)(2,1)S(1)}, u32[]{:S(2)}, u32[]{:S(2)}) collective-permute-start(bf16[112,384]{1,0:T(8,128)(2,1)S(1)} %get-tuple-element.151), channel_id=1, source_target_pairs={{0,8},{1,9},{2,10},{3,11},{4,12},{5,13},{6,14},{7,15},{8,0},{9,1},... | collective-permute-start | bytes 258056 | tf_op jit(solution)/shard_map/ppermute | solution.py:663
  79.5 9.5 %collective-permute-start.13 = (bf16[112,384]{1,0:T(8,128)(2,1)S(1)}, bf16[112,384]{1,0:T(8,128)(2,1)S(1)}, u32[]{:S(2)}, u32[]{:S(2)}) collective-permute-start(bf16[112,384]{1,0:T(8,128)(2,1)S(1)} %get-tuple-element.151), channel_id=1, source_target_pairs={{0,4},{1,5},{2,6},{3,7},{4,0},{5,1},{6,2},{7,3},{8,12},{9,13},{10,... | collective-permute-start | bytes 258056 | tf_op jit(solution)/shard_map/ppermute | solution.py:663
  80.8 14.2 %collective-permute-start.8 = (bf16[24,96,128]{2,1,0:T(8,128)(2,1)S(1)}, bf16[24,96,128]{2,1,0:T(8,128)(2,1)S(1)}, u32[]{:S(2)}, u32[]{:S(2)}) collective-permute-start(bf16[24,96,128]{2,1,0:T(8,128)(2,1)S(1)} %get-tuple-element.143), channel_id=1, source_target_pairs={{1,2},{2,1},{3,4},{4,3},{5,6},{6,5},{7,8},{8,7},{9,10},{10,9},{11,... | collective-permute-start | bytes 1769480 | tf_op jit(solution)/shard_map/ppermute | solution.py:658
  81.5 13.5 %collective-permute-start.7 = (bf16[24,96,128]{2,1,0:T(8,128)(2,1)S(1)}, bf16[24,96,128]{2,1,0:T(8,128)(2,1)S(1)}, u32[]{:S(2)}, u32[]{:S(2)}) collective-permute-start(bf16[24,96,128]{2,1,0:T(8,128)(2,1)S(1)} %get-tuple-element.142), channel_id=1, source_target_pairs={{0,1},{1,0},{2,3},{3,2},{4,5},{5,4},{6,7},{7,6},{8,9},{9,8},{10,11... | collective-permute-start | bytes 1769480 | tf_op jit(solution)/shard_map/ppermute | solution.py:650
  86.4 8.5 %collective-permute-start.18 = (bf16[16,384]{1,0:T(8,128)(2,1)S(1)}, bf16[16,384]{1,0:T(8,128)(2,1)S(1)}, u32[]{:S(2)}, u32[]{:S(2)}) collective-permute-start(bf16[16,384]{1,0:T(8,128)(2,1)S(1)} %get-tuple-element.160), channel_id=1, source_target_pairs={{0,12},{1,13},{2,14},{3,15},{4,8},{5,9},{6,10},{7,11},{8,4},{9,5},... | collective-permute-start | bytes 36872 | tf_op jit(solution)/shard_map/ppermute | solution.py:663
  89.0 5.9 %collective-permute-start.17 = (bf16[16,384]{1,0:T(8,128)(2,1)S(1)}, bf16[16,384]{1,0:T(8,128)(2,1)S(1)}, u32[]{:S(2)}, u32[]{:S(2)}) collective-permute-start(bf16[16,384]{1,0:T(8,128)(2,1)S(1)} %get-tuple-element.160), channel_id=1, source_target_pairs={{0,8},{1,9},{2,10},{3,11},{4,12},{5,13},{6,14},{7,15},{8,0},{9,1},... | collective-permute-start | bytes 36872 | tf_op jit(solution)/shard_map/ppermute | solution.py:663
  89.0 5.9 %collective-permute-start.16 = (bf16[16,384]{1,0:T(8,128)(2,1)S(1)}, bf16[16,384]{1,0:T(8,128)(2,1)S(1)}, u32[]{:S(2)}, u32[]{:S(2)}) collective-permute-start(bf16[16,384]{1,0:T(8,128)(2,1)S(1)} %get-tuple-element.160), channel_id=1, source_target_pairs={{0,4},{1,5},{2,6},{3,7},{4,0},{5,1},{6,2},{7,3},{8,12},{9,13},{10,... | collective-permute-start | bytes 36872 | tf_op jit(solution)/shard_map/ppermute | solution.py:663
  95.0 5.7 %collective-permute-start.19 = (bf16[256,384]{1,0:T(8,128)(2,1)S(1)}, bf16[256,384]{1,0:T(8,128)(2,1)S(1)}, u32[]{:S(2)}, u32[]{:S(2)}) collective-permute-start(bf16[256,384]{1,0:T(8,128)(2,1)S(1)} %get-tuple-element.163), channel_id=1, source_target_pairs={{0,2},{1,3},{2,0},{3,1},{4,6},{5,7},{6,4},{7,5},{8,10},{9,11},{10,... | collective-permute-start | bytes 589832 | tf_op jit(solution)/shard_map/ppermute | solution.py:663
  100.7 2.0 %collective-permute-start.20 = (f32[240,384]{1,0:T(8,128)S(1)}, f32[240,384]{1,0:T(8,128)S(1)}, u32[]{:S(2)}, u32[]{:S(2)}) collective-permute-start(f32[240,384]{1,0:T(8,128)S(1)} %sums_last.1.refs_1_), channel_id=1, source_target_pairs={{0,1},{1,0},{2,3},{3,2},{4,5},{5,4},{6,7},{7,6},{8,9},{9,8},{10,11... | collective-permute-start | bytes 1105928 | tf_op jit(solution)/shard_map/ppermute | solution.py:650
